TPU v7x, 128 devices: a whole 4x4x4 slice. The times are simulated.
128 devices in a mesh: fsdp: 16 (over y, x), tensor: 8 (over z, core).
Axes of the slice: x: 4, y: 4, z: 4, core: 2. Of those that a mesh axis runs over, the one named last changes fastest.
Arguments:
- activations: bfloat16 [4096, 14336], P('fsdp'), may hold values from -6 to 6
- output_grad: bfloat16 [4096, 14336], P('fsdp'), may hold values from -6 to 6
- up_blocks: bfloat16 [8, 192, 128, 128], P('tensor', 'fsdp'), may hold values from -0.5 to 0.5
- up_scale: bfloat16 [8, 192], P('tensor', 'fsdp'), may hold values from 0.25 to 4
- down_blocks: bfloat16 [8, 192, 128, 128], P('tensor', 'fsdp'), may hold values from -0.5 to 0.5
- down_scale: bfloat16 [8, 192], P('tensor', 'fsdp'), may hold values from 0.25 to 4
- up_row_block: int32 [8, 192], P('tensor'), may hold values from 0 to 111, as said below
- up_col_block: int32 [8, 192], P('tensor'), may hold values from 0 to 55
- down_row_block: int32 [8, 192], P('tensor'), may hold values from 0 to 55, as said below
- down_col_block: int32 [8, 192], P('tensor'), may hold values from 0 to 111
- up_count: int32 [8, 16], P('tensor'), may hold values from 2 to 12, as said below
- down_count: int32 [8, 16], P('tensor'), may hold values from 2 to 12, as said below
Outputs:
- input_grad: bfloat16 [4096, 14336], P('fsdp', 'tensor')
- up_grad: bfloat16 [8, 192, 128, 128], P('tensor', 'fsdp')
- down_grad: bfloat16 [8, 192, 128, 128], P('tensor', 'fsdp')
Inputs may be any that keep to these rules, and one draw needn't show every extreme that they name: `up_row_block`: within one tensor shard the up slots name distinct block positions, over all 192 slots. `down_row_block`: within one tensor shard the down slots name distinct block positions, over all 192 slots. `up_count`: A slot holds a kept block when its place within its owner is below the owner's count; in every tensor shard some owner holds exactly 12. `down_count`: as for up_count.
All inputs are finite; a program needn't handle non-finite values.
Results may differ from a plain program's by a relative error of at most 0.019.
Values may be sent and summed in bfloat16 or wider, within the bound.
No kernel may reach another device: no remote copies, remote signals or barrier semaphores. Data moves between devices by JAX's collectives and lax.ppermute only.
A program may use at most 256 MiB of HBM per device.

v0:
```python
import jax
import jax.numpy as jnp
from jax import lax
from jax.sharding import PartitionSpec as P

FF = 57344


ROOT_TWO_PI = 0.7978845608028654
CUBIC = 0.044715


def gelu_parts(hidden):
    tangent = jnp.tanh(ROOT_TWO_PI * (hidden + CUBIC * hidden * hidden * hidden))
    gelu_value = 0.5 * hidden * (1.0 + tangent)
    gelu_slope = 0.5 * (1.0 + tangent) + 0.5 * hidden * (1.0 - tangent * tangent) * ROOT_TWO_PI * (
        1.0 + 3.0 * CUBIC * hidden * hidden
    )
    return (gelu_value, gelu_slope)


def pick_matrix(indices, count, kind):
    return (indices[:, None] == jnp.arange(count, dtype=jnp.int32)[None, :]).astype(kind)


def pick_middle(table, indices):
    selector = pick_matrix(indices, table.shape[1], jnp.bfloat16)
    return jnp.einsum("trb,mr->tmb", table, selector, preferred_element_type=jnp.float32).astype(
        jnp.bfloat16
    )


def pick_front(table, indices):
    selector = pick_matrix(indices, table.shape[0], jnp.bfloat16)
    return jnp.einsum("ctb,mc->mtb", table, selector, preferred_element_type=jnp.float32).astype(
        jnp.bfloat16
    )


def on_device(
    activations,
    output_grad,
    up_blocks,
    up_scale,
    down_blocks,
    down_scale,
    up_row_block,
    up_col_block,
    down_row_block,
    down_col_block,
    up_count,
    down_count,
):
    token_rows = activations.shape[0]
    block_size = up_blocks.shape[2]
    capacity = up_blocks.shape[1]
    owners = lax.axis_size("fsdp")
    slot_total = owners * capacity
    row_blocks = activations.shape[1] // block_size
    col_blocks = FF // lax.axis_size("tensor") // block_size
    acts_three = activations.reshape(token_rows, row_blocks, block_size)
    grads_three = output_grad.reshape(token_rows, row_blocks, block_size)
    slot_index = jnp.arange(slot_total)
    up_live = (slot_index % capacity < jnp.repeat(up_count[0], capacity)).astype(jnp.float32)
    down_live = (slot_index % capacity < jnp.repeat(down_count[0], capacity)).astype(jnp.float32)
    up_rows = up_row_block[0]
    up_cols = up_col_block[0]
    down_rows = down_row_block[0]
    down_cols = down_col_block[0]
    grad_norm = float(token_rows * owners) ** (-0.5)
    up_tiles = lax.all_gather(up_blocks, "fsdp", axis=1, tiled=True)
    up_mults = lax.all_gather(up_scale, "fsdp", axis=1, tiled=True)
    down_tiles = lax.all_gather(down_blocks, "fsdp", axis=1, tiled=True)
    down_mults = lax.all_gather(down_scale, "fsdp", axis=1, tiled=True)
    row_pick = up_rows
    col_pick = up_cols
    factor = up_mults[0].astype(jnp.float32) * up_live
    source = pick_middle(acts_three, row_pick)
    product = jnp.einsum("tmi,mij->mtj", source, up_tiles[0], preferred_element_type=jnp.float32)
    placing = pick_matrix(col_pick, col_blocks, jnp.float32) * factor[:, None]
    hidden = jnp.einsum("mc,mtj->ctj", placing, product, precision=lax.Precision.HIGHEST)
    row_pick = down_rows
    col_pick = down_cols
    factor = down_mults[0].astype(jnp.float32) * down_live
    target = pick_middle(grads_three, col_pick)
    product = jnp.einsum("tmj,mij->mti", target, down_tiles[0], preferred_element_type=jnp.float32)
    placing = pick_matrix(row_pick, col_blocks, jnp.float32) * factor[:, None]
    backed = jnp.einsum("mc,mti->cti", placing, product, precision=lax.Precision.HIGHEST)
    hidden, backed = (hidden, backed)
    gelu_value, gelu_slope = gelu_parts(hidden)
    activated = gelu_value.astype(jnp.bfloat16)
    hidden_grad = (backed * gelu_slope).astype(jnp.bfloat16)
    up_tiles = lax.all_gather(up_blocks, "fsdp", axis=1, tiled=True)
    up_mults = lax.all_gather(up_scale, "fsdp", axis=1, tiled=True)
    row_pick = up_rows
    col_pick = up_cols
    factor = up_mults[0].astype(jnp.float32) * up_live
    source = pick_front(hidden_grad, col_pick)
    product = jnp.einsum("mtj,mij->tmi", source, up_tiles[0], preferred_element_type=jnp.float32)
    placing = pick_matrix(row_pick, row_blocks, jnp.float32) * factor[:, None]
    partial_sum = jnp.einsum("tmi,mr->tri", product, placing, precision=lax.Precision.HIGHEST)
    row_pick = up_rows
    col_pick = up_cols
    left_side = pick_middle(acts_three, row_pick)
    right_side = pick_front(hidden_grad, col_pick)
    row_pick = down_rows
    col_pick = down_cols
    down_left_side = pick_front(activated, row_pick)
    down_right_side = pick_middle(grads_three, col_pick)
    summed = lax.psum_scatter(
        jnp.stack(
            [
                jnp.einsum(
                    "tmi,mtj->mij", left_side, right_side, preferred_element_type=jnp.float32
                ),
                jnp.einsum(
                    "mti,tmj->mij",
                    down_left_side,
                    down_right_side,
                    preferred_element_type=jnp.float32,
                ),
            ],
            axis=1,
        ).astype(jnp.bfloat16),
        "fsdp",
        scatter_dimension=0,
        tiled=True,
    ).astype(jnp.float32)
    up_summed = summed[:, 0]
    down_summed = summed[:, 1]
    own_start = lax.axis_index("fsdp") * capacity
    up_factor = up_scale[0].astype(jnp.float32) * lax.dynamic_slice_in_dim(
        up_live, own_start, capacity
    )
    down_factor = down_scale[0].astype(jnp.float32) * lax.dynamic_slice_in_dim(
        down_live, own_start, capacity
    )
    up_grad = (up_summed * (up_factor * grad_norm)[:, None, None]).astype(jnp.bfloat16)[None]
    down_grad = (down_summed * (down_factor * grad_norm)[:, None, None]).astype(jnp.bfloat16)[None]
    flat_sum = partial_sum.reshape(token_rows, row_blocks * block_size)
    input_grad = lax.psum_scatter(
        flat_sum.astype(jnp.bfloat16), "tensor", scatter_dimension=1, tiled=True
    )
    return (input_grad, up_grad, down_grad)


def solution(mesh):
    return jax.shard_map(
        on_device,
        mesh=mesh,
        in_specs=(
            P("fsdp", None),
            P("fsdp", None),
            P("tensor", "fsdp", None, None),
            P("tensor", "fsdp"),
            P("tensor", "fsdp", None, None),
            P("tensor", "fsdp"),
            P("tensor", None),
            P("tensor", None),
            P("tensor", None),
            P("tensor", None),
            P("tensor", None),
            P("tensor", None),
        ),
        out_specs=(
            P("fsdp", "tensor"),
            P("tensor", "fsdp", None, None),
            P("tensor", "fsdp", None, None),
        ),
        check_vma=False,
    )
```

profile of v0, /device:TPU:0, one launch (start us, length us, event | category | flops | bytes accessed | tf_op | source)
XLA Modules:
  0.0 551.2 jit_solution(12048156166874295383)
XLA Ops:
  7.2 0.0 all-gather.5.cloned.1.call-start
  7.2 0.7 all-gather.5.cloned.1.call-update
  7.9 0.0 all-gather.3.cloned.1.call-start
  7.9 0.7 all-gather.3.cloned.1.call-update
  8.6 0.0 all-reduce.6.cloned.1.call-start
  8.7 0.7 broadcast_in_dim.4
  9.4 0.1 reshape.93
  9.5 0.0 copy-start.2
  9.5 0.7 broadcast_in_dim.5
  10.3 0.1 reshape.94
  10.4 0.0 copy-start.4
  10.4 0.0 copy-start.6
  10.4 4.8 copy.31
  15.2 6.4 %convert_bitcast_fusion = bf16[256,192,128]{2,1,0:T(8,128)(2,1)} fusion(bf16[256,112,128]{2,1,0:T(8,128)(2,1)S(1)} %bitcast.93, s32[192]{0:T(256)S(1)} %bitcast.102), kind=kOutput, calls=%fused_computation.10 | convolution fusion | flops 1415599104 | bytes 19923712 | tf_op jit(solution)/shard_map/trb,mr->tmb/dot_general | solution.py:28
  21.6 17.7 %copy.20 = bf16[256,192,128]{0,2,1:T(8,128)(2,1)} copy(bf16[256,192,128]{2,1,0:T(8,128)(2,1)} %convert_bitcast_fusion) | data formatting | bytes 25165824 | tf_op jit(solution)/shard_map/convert_element_type | solution.py:28
  39.3 7.8 %copy.30 = bf16[32,8,112,128]{3,2,1,0:T(8,128)(2,1)} copy(bf16[32,8,112,128]{3,1,2,0:T(8,128)(2,1)} %bitcast.99) | data formatting | bytes 14680064
  47.1 0.6 fusion.91
  48.4 0.2 dynamic-update-slice.1
  48.6 0.2 dynamic-update-slice
  48.9 41.1 %all-reduce.3 = (bf16[192]{0:T(256)(128)(2,1)S(1)}, bf16[192]{0:T(256)(128)(2,1)S(1)}) all-reduce(bf16[192]{0:T(256)(128)(2,1)S(1)} %dynamic-update-slice.1, bf16[192]{0:T(256)(128)(2,1)S(1)} %dynamic-update-slice), channel_id=1, replica_groups=mesh['fsdp'=16,'tensor'=8] {'fsdp'}, use_global_device_ids=true, to_apply=%add.1 | all-reduce | flops 384 | bytes 1536
  90.0 9.7 %convert_bitcast_fusion.1 = bf16[256,192,128]{2,1,0:T(8,128)(2,1)} fusion(bf16[256,112,128]{2,1,0:T(8,128)(2,1)} %bitcast.92, s32[192]{0:T(256)S(1)} %bitcast.104), kind=kOutput, calls=%fused_computation.11 | convolution fusion | flops 1415599104 | bytes 19923712 | tf_op jit(solution)/shard_map/trb,mr->tmb/dot_general | solution.py:28
  99.7 15.4 %fusion.27 = f32[192,256,128]{2,1,0:T(8,128)} fusion(bf16[256,192,128]{0,2,1:T(8,128)(2,1)} %copy.20, bf16[1,192,128,128]{3,2,0,1:T(8,128)(2,1)} %all-gather.5.cloned.1.call-done), kind=kOutput, calls=%fused_computation.33 | convolution fusion | flops 1610612736 | bytes 44040192 | tf_op jit(solution)/shard_map/tmi,mij->mtj/dot_general | solution.py:79
  115.1 37.1 %fusion.3 = f32[56,256,128]{2,0,1:T(8,128)S(1)} fusion(f32[192,256,128]{2,1,0:T(8,128)} %fusion.27, f32[192]{0:T(256)S(1)} %convert_select_fusion.1, s32[192]{0:T(256)S(1)} %bitcast.107), kind=kOutput, calls=%fused_computation.3 | convolution fusion | flops 4227879936 | bytes 32507392 | tf_op jit(solution)/shard_map/mc,mtj->ctj/dot_general | solution.py:81
  152.1 0.0 copy-start
  152.1 2.9 copy-done
  155.0 6.5 %fusion.30 = bf16[192,256,128]{2,0,1:T(8,128)(2,1)} fusion(f32[56,256,128]{2,0,1:T(8,128)S(1)} %fusion.3, s32[192]{0:T(256)S(1)} %bitcast.105), kind=kOutput, calls=%fused_computation.38 | convolution fusion | flops 721168896 | bytes 19923712 | tf_op jit(solution)/shard_map/ctb,mc->mtb/dot_general | solution.py:35
  161.5 21.5 %fusion.9 = f32[192,256,128]{2,1,0:T(8,128)} fusion(bf16[256,192,128]{2,1,0:T(8,128)(2,1)} %convert_bitcast_fusion.1, bf16[1,192,128,128]{3,2,0,1:T(8,128)(2,1)} %all-gather.3.cloned.1.call-done), kind=kOutput, calls=%fused_computation.12 | convolution fusion | flops 1610612736 | bytes 44040192 | tf_op jit(solution)/shard_map/tmj,mij->mti/dot_general | solution.py:86
  183.0 51.3 %fusion.5 = f32[56,256,128]{2,0,1:T(8,128)} fusion(f32[192,256,128]{2,1,0:T(8,128)} %fusion.9, f32[192]{0:T(256)S(1)} %convert_select_fusion, s32[192]{0:T(256)S(1)} %bitcast.106), kind=kOutput, calls=%fused_computation.5 | convolution fusion | flops 4227879936 | bytes 32507392 | tf_op jit(solution)/shard_map/mc,mti->cti/dot_general | solution.py:88
  234.3 0.0 copy-done.1
  234.3 12.7 %convolution_convert_fusion = bf16[192,256,128]{2,0,1:T(8,128)(2,1)} fusion(f32[56,256,128]{2,0,1:T(8,128)} %fusion.5, f32[56,256,128]{2,0,1:T(8,128)S(1)} %copy-done.1, s32[192]{0:T(256)S(1)} %bitcast.108), kind=kOutput, calls=%fused_computation.30 | convolution fusion | flops 745810432 | bytes 27263744 | tf_op jit(solution)/shard_map/ctb,mc->mtb/dot_general | solution.py:35
  247.0 21.9 %convert_bitcast_fusion.3 = bf16[192,1,128,128]{3,2,0,1:T(8,128)(2,1)} fusion(bf16[256,192,128]{0,2,1:T(8,128)(2,1)} %copy.20, bf16[192,256,128]{2,0,1:T(8,128)(2,1)} %convolution_convert_fusion), kind=kOutput, calls=%fused_computation.37 | convolution fusion | flops 1613758464 | bytes 31457280 | tf_op jit(solution)/shard_map/tmi,mtj->mij/dot_general | solution.py:113
  268.9 17.9 %copy.27 = bf16[192,256,128]{1,2,0:T(8,128)(2,1)} copy(bf16[192,256,128]{2,0,1:T(8,128)(2,1)} %fusion.30) | data formatting | bytes 25165824 | tf_op jit(solution)/shard_map/ctb,mc->mtb/dot_general | solution.py:35
  286.8 22.2 %convert_bitcast_fusion.2 = bf16[192,1,128,128]{3,2,0,1:T(8,128)(2,1)} fusion(bf16[256,192,128]{2,1,0:T(8,128)(2,1)} %convert_bitcast_fusion.1, bf16[192,256,128]{1,2,0:T(8,128)(2,1)} %copy.27), kind=kOutput, calls=%fused_computation.36 | convolution fusion | flops 1613758464 | bytes 31457280 | tf_op jit(solution)/shard_map/mti,tmj->mij/dot_general | solution.py:116
  309.0 8.3 %pad_maximum_fusion = bf16[192,2,128,128]{3,2,0,1:T(8,128)(2,1)} fusion(bf16[192,1,128,128]{3,2,0,1:T(8,128)(2,1)} %convert_bitcast_fusion.2, bf16[192,1,128,128]{3,2,0,1:T(8,128)(2,1)S(1)} %bitcast.97), kind=kLoop, calls=%fused_computation.7 | loop fusion | flops 6291456 | bytes 25165824 | tf_op jit(solution)/shard_map/stack | solution.py:111
  317.3 0.0 all-reduce.6.cloned.1.call-update
  317.3 0.0 copy-start.7
  317.4 0.0 reduce-scatter.5.cloned.1.call-start
  317.4 21.5 %fusion.12 = f32[192,256,128]{2,1,0:T(8,128)} fusion(bf16[192,256,128]{2,0,1:T(8,128)(2,1)} %convolution_convert_fusion, bf16[1,192,128,128]{3,2,0,1:T(8,128)(2,1)} %all-gather.5.cloned.1.call-done), kind=kOutput, calls=%fused_computation.15 | convolution fusion | flops 1610612736 | bytes 44040192 | tf_op jit(solution)/shard_map/mtj,mij->tmi/dot_general | solution.py:99
  338.9 40.8 %fusion.23 = bf16[112,256,128]{2,0,1:T(8,128)(2,1)} fusion(f32[192,256,128]{2,1,0:T(8,128)} %fusion.12, f32[192]{0:T(256)S(1)} %convert_select_fusion.1, s32[192]{0:T(256)S(1)} %bitcast.103), kind=kOutput, calls=%fused_computation.31 | convolution fusion | flops 8459429888 | bytes 32507392 | tf_op jit(solution)/shard_map/tmi,mr->tri/dot_general | solution.py:101
  379.7 8.0 %copy.56 = bf16[32,8,112,128]{3,1,2,0:T(8,128)(2,1)} copy(bf16[32,8,112,128]{3,2,1,0:T(8,128)(2,1)} %bitcast.95) | data formatting | bytes 14680064
  387.8 0.0 reduce-scatter.5.cloned.1.call-update
  388.4 0.0 copy-done.3
  388.4 0.0 copy-done.5
  388.5 0.1 fusion.73
  388.6 105.2 %all-reduce.6.cloned.1.call-done = bf16[192,2,128,128]{3,2,0,1:T(8,128)(2,1)} async-done(((bf16[192,2,128,128]{3,2,0,1:T(8,128)(2,1)}), bf16[192,2,128,128]{3,2,0,1:T(8,128)(2,1)}) %all-reduce.6.cloned.1.call-update) | async-done | bytes 12582928
  493.7 1.3 dynamic-slice_convert_fusion
  495.0 1.1 fusion.43
  496.1 48.1 %reduce-scatter.5.cloned.1.call-done = bf16[256,1792]{1,0:T(8,128)(2,1)} async-done(((bf16[256,14336]{1,0:T(8,128)(2,1)}), bf16[256,1792]{1,0:T(8,128)(2,1)}) %reduce-scatter.5.cloned.1.call-update) | async-done | bytes 917520 | tf_op jit(solution)/shard_map/reduce_scatter | solution.py:141
  (36 shorter events, 0.1 us)
Async XLA Ops:
  7.2 92.5 %all-gather.5.cloned.1.call-start = ((), (), s32[]{:S(2)}) async-start(), calls=%async_computation.2 | async-start | bytes 6684672 | tf_op jit(solution)/shard_map/all_gather | solution.py:93
  7.9 153.6 %all-gather.3.cloned.1.call-start = ((), (), s32[]{:S(2)}) async-start(), calls=%async_computation.1 | async-start | bytes 6684672 | tf_op jit(solution)/shard_map/all_gather | solution.py:73
  8.6 485.1 %all-reduce.6.cloned.1.call-start = ((), (), s32[]{:S(2)}) async-start(), calls=%async_computation.4 | async-start | bytes 25165824
  9.5 80.4 %copy-start.2 = (s32[192]{0:T(256)}, s32[192]{0:T(256)S(1)}, u32[]{:S(2)}) copy-start(s32[192]{0:T(256)S(1)} %reshape.93) | copy-start | bytes 2308
  10.4 79.6 %copy-start.4 = (s32[192]{0:T(256)}, s32[192]{0:T(256)S(1)}, u32[]{:S(2)}) copy-start(s32[192]{0:T(256)S(1)} %reshape.94) | copy-start | bytes 2308
  10.4 4.8 copy-start.6
  39.3 7.8 %copy-start.8 = (u32[128]{0:T(128)S(1)}, u32[128]{0:T(128)}, u32[]{:S(2)}) copy-start(u32[128]{0:T(128)} %constant.54) | copy-start | bytes 1540
  39.3 9.1 %copy-start.12 = (bf16[1,12]{1,0:T(2,128)(2,1)S(1)}, bf16[1,12]{1,0:T(2,128)(2,1)}, u32[]{:S(2)}) copy-start(bf16[1,12]{1,0:T(2,128)(2,1)} %param.17) | copy-start | bytes 76
  39.3 9.3 %copy-start.14 = (bf16[1,12]{1,0:T(2,128)(2,1)S(1)}, bf16[1,12]{1,0:T(2,128)(2,1)}, u32[]{:S(2)}) copy-start(bf16[1,12]{1,0:T(2,128)(2,1)} %param.15) | copy-start | bytes 76
  39.3 50.7 %copy-start.9 = (s32[1,192]{1,0:T(1,128)S(1)}, s32[1,192]{1,0:T(1,128)}, u32[]{:S(2)}) copy-start(s32[1,192]{1,0:T(1,128)} %param.21) | copy-start | bytes 2308
  99.7 15.4 %copy-start.11 = (s32[1,192]{1,0:T(1,128)S(1)}, s32[1,192]{1,0:T(1,128)}, u32[]{:S(2)}) copy-start(s32[1,192]{1,0:T(1,128)} %param.19) | copy-start | bytes 2308
  115.1 40.0 %copy-start.10 = (s32[1,192]{1,0:T(1,128)S(1)}, s32[1,192]{1,0:T(1,128)}, u32[]{:S(2)}) copy-start(s32[1,192]{1,0:T(1,128)} %param.20) | copy-start | bytes 2308
  152.1 2.9 copy-start
  183.0 51.3 %copy-start.1 = (f32[56,256,128]{2,0,1:T(8,128)S(1)}, f32[56,256,128]{2,0,1:T(8,128)}, u32[]{:S(2)}) copy-start(f32[56,256,128]{2,0,1:T(8,128)} %copy-done) | copy-start | bytes 22020100
  268.9 40.1 %slice-start = ((s8[6291456]{0:T(1024)(128)(4,1)}), s8[2097152]{0:T(1024)(128)(4,1)S(1)}, s32[]{:S(2)}) async-start(s8[6291456]{0:T(1024)(128)(4,1)} %bitcast.96), calls=%async_computation.5 | async-start | bytes 4194304
  286.8 22.2 %slice-start.1 = ((s8[6291456]{0:T(1024)(128)(4,1)}), s8[4194304]{0:T(1024)(128)(4,1)S(1)}, s32[]{:S(2)}) async-start(s8[6291456]{0:T(1024)(128)(4,1)} %bitcast.96), calls=%async_computation.6 | async-start | bytes 8388608
  317.3 21.6 %copy-start.7 = (s32[1,192]{1,0:T(1,128)S(1)}, s32[1,192]{1,0:T(1,128)}, u32[]{:S(2)}) copy-start(s32[1,192]{1,0:T(1,128)} %param.18) | copy-start | bytes 2308
  317.4 226.8 %reduce-scatter.5.cloned.1.call-start = ((), (), s32[]{:S(2)}) async-start(), calls=%async_computation.3 | async-start | bytes 8257536 | tf_op jit(solution)/shard_map/reduce_scatter | solution.py:141
  387.7 0.7 copy-start.3
  387.8 0.7 copy-start.5
  387.8 0.7 copy-start.13
  387.8 0.7 copy-start.15
Sparse Core Ops, SparseCore 0:
  10.1 64.1 all-gather.4
  76.5 60.9 all-gather.2
  317.5 176.2 all-reduce.5
  496.7 47.4 reduce-scatter.4
where the time goes:
time: 559 us; the launch traced here: 551 us
  matrix products  267 us (48%)
  waiting for transfers between devices  155 us (28%)
  local copies, waits for them, and re-layouts  61.9 us (11%)
  blocking collectives  41.1 us (7%)
  between operations  15.7 us (3%)
  other arithmetic  10.8 us (2%)
    unnamed x5, waiting for transfers between devices  107 us
    dot_general x1, matrix products, on_device(): jnp.einsum('mc,mti->cti', placing, product, precision=lax.Precision.HIGHEST)  51.3 us
    reduce_scatter x1, waiting for transfers between devices, on_device(): lax.psum_scatter(flat_sum.astype(jnp.bfloat16), 'tensor', scatter_dimensi...  48.1 us
    unnamed x1, blocking collectives  41.1 us
    dot_general x1, matrix products, on_device(): jnp.einsum('tmi,mr->tri', product, placing, precision=lax.Precision.HIGHEST)  40.8 us
    dot_general x1, matrix products, on_device(): jnp.einsum('mc,mtj->ctj', placing, product, precision=lax.Precision.HIGHEST)  37.1 us
    unnamed x44, local copies, waits for them, and re-layouts  24.7 us
    dot_general x1, matrix products, on_device(): jnp.einsum('mti,tmj->mij', down_left_side, down_right_side, preferred_ele...  22.2 us
  transfers between devices with their start and end apart: 4, of which 2 were waited for; matrix products, arithmetic and copies ran while one was open for 33% of the time, Pallas kernels for 0%

commit v1 on v0

--- a/solution.py
+++ b/solution.py
@@ -1,6 +1,8 @@
 import jax
 import jax.numpy as jnp
 from jax import lax
+from jax.experimental import pallas as pl
+from jax.experimental.pallas import tpu as pltpu
 from jax.sharding import PartitionSpec as P
 
 FF = 57344
@@ -37,7 +39,7 @@
     )
 
 
-def on_device(
+def full_exchange(
     activations,
     output_grad,
     up_blocks,
@@ -144,6 +146,372 @@
     return (input_grad, up_grad, down_grad)
 
 
+SIDE = 4
+CAP = 12
+BLK = 128
+ROOM = 30
+LIST = 128
+VMEM_LIMIT = 60 * 1024 * 1024
+
+
+def shift_x(step):
+    return [(y * SIDE + x, y * SIDE + (x + step) % SIDE) for y in range(SIDE) for x in range(SIDE)]
+
+
+def shift_y(step):
+    return [(y * SIDE + x, (y + step) % SIDE * SIDE + x) for y in range(SIDE) for x in range(SIDE)]
+
+
+def back(place, step):
+    return lax.rem(place + SIDE - step, SIDE)
+
+
+def any_tensor(flag):
+    def moved(pairs):
+        return lax.ppermute(flag, "tensor", pairs)
+
+    flag = jnp.maximum(flag, moved([(t, t ^ 1) for t in range(8)]))
+    flag = jnp.maximum(flag, moved([(t, (t + 2) % 8) for t in range(8)]))
+    return jnp.maximum(flag, moved([(t, (t + 4) % 8) for t in range(8)]))
+
+
+def up_owner(y, x, far, near):
+    return back(y, far) * SIDE + back(x, near)
+
+
+def down_owner(y, x, far, near):
+    return back(y, near) * SIDE + back(x, far)
+
+
+def call(kernel, outs, in_spaces, out_spaces, scratch, name, cost=None):
+    return pl.pallas_call(
+        kernel,
+        out_shape=outs,
+        in_specs=[pl.BlockSpec(memory_space=s) for s in in_spaces],
+        out_specs=[pl.BlockSpec(memory_space=s) for s in out_spaces],
+        scratch_shapes=scratch,
+        compiler_params=pltpu.CompilerParams(vmem_limit_bytes=VMEM_LIMIT),
+        cost_estimate=cost,
+        name=name,
+    )
+
+
+V, S, A = pltpu.VMEM, pltpu.SMEM, pl.ANY
+
+
+def cost(us):
+    return pl.CostEstimate(flops=0, bytes_accessed=int(us * 3e6), transcendentals=0)
+
+
+def blocks(count):
+    return jax.ShapeDtypeStruct((count, BLK, BLK), jnp.bfloat16)
+
+
+def pack_kernel(place, up_count, down_count, *refs):
+    y, x = place[0], place[1]
+    for owner_of, count, ins, out in (
+        (up_owner, up_count, refs[:4], refs[8]),
+        (down_owner, down_count, refs[4:8], refs[9]),
+    ):
+        position = 0
+        for near in range(SIDE):
+            live = count[owner_of(y, x, 0, near)]
+
+            def put(j, at, source=ins[near], out=out):
+                out[at] = source[j]
+                return at + 1
+
+            position = lax.fori_loop(0, live, put, position)
+
+
+def table_kernel(place, up_count, up_row, up_col, down_count, down_row, down_col, table):
+    y, x = place[0], place[1]
+    for first, owner_of, count, rows, cols in (
+        (0, up_owner, up_count, up_row, up_col),
+        (3, down_owner, down_count, down_row, down_col),
+    ):
+        def blank(i, unused, first=first):
+            table[first, i] = SIDE * ROOM
+            table[first + 1, i] = 0
+            table[first + 2, i] = 0
+            return unused
+
+        total = 0
+        for far in range(SIDE):
+            position = far * ROOM
+            for near in range(SIDE):
+                owner = owner_of(y, x, far, near)
+                live = count[owner]
+
+                def note(j, unused, first=first, rows=rows, cols=cols, owner=owner, total=total, position=position):
+                    table[first, total + j] = position + j
+                    table[first + 1, total + j] = rows[owner * CAP + j]
+                    table[first + 2, total + j] = cols[owner * CAP + j]
+                    return unused
+
+                lax.fori_loop(0, live, note, 0)
+                total = total + live
+                position = position + live
+        padded = (total + 3) // 4
+        lax.fori_loop(total, padded * 4, blank, 0)
+        table[6, first] = padded
+
+
+def lane(index):
+    return pl.ds(pl.multiple_of(index * BLK, BLK), BLK)
+
+
+def forward_kernel(table, acts, grads, *refs):
+    ups, downs = refs[:4], refs[4:8]
+    activated, hidden_grad = refs[8:10]
+    up_tiles, down_tiles, hidden, backed, sems = refs[10:]
+    copies = []
+    for far in range(SIDE):
+        for which, (source, target) in enumerate(((ups[far], up_tiles), (downs[far], down_tiles))):
+            copy = pltpu.make_async_copy(
+                source, target.at[pl.ds(far * ROOM, ROOM)], sems.at[which, far]
+            )
+            copy.start()
+            copies.append(copy)
+    up_tiles[SIDE * ROOM] = jnp.zeros((BLK, BLK), jnp.bfloat16)
+    down_tiles[SIDE * ROOM] = jnp.zeros((BLK, BLK), jnp.bfloat16)
+    hidden[...] = jnp.zeros_like(hidden)
+    backed[...] = jnp.zeros_like(backed)
+    for copy in copies:
+        copy.wait()
+
+    def up_step(i, unused):
+        products = []
+        for u in range(4):
+            at = i * 4 + u
+            products.append(
+                jnp.dot(acts[:, lane(table[1, at])], up_tiles[table[0, at]], preferred_element_type=jnp.float32)
+            )
+        for u in range(4):
+            hidden[:, lane(table[2, i * 4 + u])] += products[u]
+        return unused
+
+    lax.fori_loop(0, table[6, 0], up_step, 0)
+
+    def down_step(i, unused):
+        products = []
+        for u in range(4):
+            at = i * 4 + u
+            products.append(
+                lax.dot_general(
+                    grads[:, lane(table[5, at])],
+                    down_tiles[table[3, at]],
+                    (((1,), (1,)), ((), ())),
+                    preferred_element_type=jnp.float32,
+                )
+            )
+        for u in range(4):
+            backed[:, lane(table[4, i * 4 + u])] += products[u]
+        return unused
+
+    lax.fori_loop(0, table[6, 3], down_step, 0)
+
+    def bend(i, unused):
+        value, slope = gelu_parts(hidden[:, lane(i)])
+        activated[:, lane(i)] = value.astype(jnp.bfloat16)
+        hidden_grad[:, lane(i)] = (backed[:, lane(i)] * slope).astype(jnp.bfloat16)
+        return unused
+
+    lax.fori_loop(0, hidden.shape[1] // BLK, bend, 0)
+
+
+def terms_kernel(table, acts, grads, activated, hidden_grad, *refs):
+    outs = refs[:8]
+    up_terms, down_terms, sems = refs[8:]
+
+    def step(first, left, right, terms):
+        def body(i, unused):
+            for u in range(4):
+                at = i * 4 + u
+                terms[table[first, at]] = lax.dot_general(
+                    left[:, lane(table[first + 1, at])],
+                    right[:, lane(table[first + 2, at])],
+                    (((0,), (0,)), ((), ())),
+                    preferred_element_type=jnp.float32,
+                ).astype(jnp.bfloat16)
+            return unused
+
+        lax.fori_loop(0, table[6, first], body, 0)
+
+    copies = []
+
+    def send(which, terms):
+        for far in range(SIDE):
+            copy = pltpu.make_async_copy(
+                terms.at[pl.ds(far * ROOM, ROOM)], outs[which * 4 + far], sems.at[which, far]
+            )
+            copy.start()
+            copies.append(copy)
+
+    step(0, acts, hidden_grad, up_terms)
+    send(0, up_terms)
+    step(3, activated, grads, down_terms)
+    send(1, down_terms)
+    for copy in copies:
+        copy.wait()
+
+
+def partial_kernel(table, hidden_grad, *refs):
+    ups, out = refs[:4], refs[4]
+    up_tiles, partial, sems = refs[5:]
+    copies = []
+    for far in range(SIDE):
+        copy = pltpu.make_async_copy(ups[far], up_tiles.at[pl.ds(far * ROOM, ROOM)], sems.at[far])
+        copy.start()
+        copies.append(copy)
+    up_tiles[SIDE * ROOM] = jnp.zeros((BLK, BLK), jnp.bfloat16)
+    partial[...] = jnp.zeros_like(partial)
+    for copy in copies:
+        copy.wait()
+
+    def step(i, unused):
+        products = []
+        for u in range(4):
+            at = i * 4 + u
+            products.append(
+                lax.dot_general(
+                    hidden_grad[:, lane(table[2, at])],
+                    up_tiles[table[0, at]],
+                    (((1,), (1,)), ((), ())),
+                    preferred_element_type=jnp.float32,
+                )
+            )
+        for u in range(4):
+            partial[:, lane(table[1, i * 4 + u])] += products[u]
+        return unused
+
+    lax.fori_loop(0, table[6, 0], step, 0)
+
+    def write(i, unused):
+        out[:, lane(i)] = partial[:, lane(i)].astype(jnp.bfloat16)
+        return unused
+
+    lax.fori_loop(0, partial.shape[1] // BLK, write, 0)
+
+
+def unpack_kernel(place, up_count, down_count, *refs):
+    y, x = place[0], place[1]
+    for owner_of, count, ins, outs in (
+        (up_owner, up_count, refs[:4], refs[8:12]),
+        (down_owner, down_count, refs[4:8], refs[12:16]),
+    ):
+        position = 0
+        for near in range(SIDE):
+            live = count[owner_of(y, x, 0, near)]
+
+            def put(j, at, ins=ins, out=outs[near]):
+                out[j] = sum(ref[at].astype(jnp.float32) for ref in ins).astype(jnp.bfloat16)
+                return at + 1
+
+            position = lax.fori_loop(0, live, put, position)
+
+
+def finish_kernel(place, up_count, down_count, up_factor, down_factor, *refs):
+    owner = place[0] * SIDE + place[1]
+    for count, factor, ins, out in (
+        (up_count, up_factor, refs[:4], refs[8]),
+        (down_count, down_factor, refs[4:8], refs[9]),
+    ):
+        live = count[owner]
+
+        def put(j, unused, ins=ins, out=out, factor=factor):
+            out[j] = (sum(ref[j].astype(jnp.float32) for ref in ins) * factor[j]).astype(jnp.bfloat16)
+            return unused
+
+        def clear(j, unused, out=out):
+            out[j] = jnp.zeros((BLK, BLK), jnp.bfloat16)
+            return unused
+
+        lax.fori_loop(0, live, put, 0)
+        lax.fori_loop(live, CAP, clear, 0)
+
+
+def packed_exchange(near_up, near_down, activations, output_grad, up_blocks, up_scale, down_blocks, down_scale,
+                    up_row_block, up_col_block, down_row_block, down_col_block, up_count, down_count):
+    tokens = activations.shape[0]
+    width = activations.shape[1]
+    hidden_width = FF // lax.axis_size("tensor")
+    grad_norm = float(tokens * lax.axis_size("fsdp")) ** (-0.5)
+    me = lax.axis_index("fsdp")
+    place = jnp.stack([me // SIDE, me % SIDE]).astype(jnp.int32)
+    up_count, down_count = up_count[0], down_count[0]
+    packed_up, packed_down = call(
+        pack_kernel, [blocks(ROOM)] * 2, [S] * 3 + [V] * 8, [V] * 2, [], "pack", cost(2)
+    )(place, up_count, down_count, *near_up, *near_down)
+    far_up = [packed_up] + [lax.ppermute(packed_up, "fsdp", shift_y(m)) for m in range(1, SIDE)]
+    far_down = [packed_down] + [lax.ppermute(packed_down, "fsdp", shift_x(m)) for m in range(1, SIDE)]
+    (table,) = call(
+        table_kernel, [jax.ShapeDtypeStruct((8, LIST), jnp.int32)], [S] * 7, [S], [], "table", cost(2)
+    )(place, up_count, up_row_block[0], up_col_block[0], down_count, down_row_block[0], down_col_block[0])
+    half = jax.ShapeDtypeStruct((tokens, hidden_width), jnp.bfloat16)
+    tiles = pltpu.VMEM((SIDE * ROOM + 1, BLK, BLK), jnp.bfloat16)
+    activated, hidden_grad = call(
+        forward_kernel,
+        [half, half],
+        [S, V, V] + [A] * 8,
+        [V, V],
+        [tiles, tiles]
+        + [pltpu.VMEM((tokens, hidden_width), jnp.float32)] * 2
+        + [pltpu.SemaphoreType.DMA((2, SIDE))],
+        "forward", cost(25),
+    )(table, activations, output_grad, *far_up, *far_down)
+    terms = call(
+        terms_kernel,
+        [blocks(ROOM)] * 8,
+        [S, V, V, V, V],
+        [A] * 8,
+        [tiles, tiles, pltpu.SemaphoreType.DMA((2, SIDE))],
+        "terms", cost(20),
+    )(table, activations, output_grad, activated, hidden_grad)
+    up_terms = [terms[0]] + [lax.ppermute(terms[m], "fsdp", shift_y(SIDE - m)) for m in range(1, SIDE)]
+    down_terms = [terms[4]] + [lax.ppermute(terms[4 + m], "fsdp", shift_x(SIDE - m)) for m in range(1, SIDE)]
+    (partial,) = call(
+        partial_kernel,
+        [jax.ShapeDtypeStruct((tokens, width), jnp.bfloat16)],
+        [S, V] + [A] * 4,
+        [V],
+        [tiles, pltpu.VMEM((tokens, width), jnp.float32), pltpu.SemaphoreType.DMA((SIDE,))],
+        "partial", cost(15),
+    )(table, hidden_grad, *far_up)
+    input_grad = lax.psum_scatter(partial, "tensor", scatter_dimension=1, tiled=True)
+    sums = call(
+        unpack_kernel, [blocks(CAP)] * 8, [S] * 3 + [V] * 8, [V] * 8, [], "unpack", cost(3)
+    )(place, up_count, down_count, *up_terms, *down_terms)
+    near_up = [sums[0]] + [lax.ppermute(sums[k], "fsdp", shift_x(SIDE - k)) for k in range(1, SIDE)]
+    near_down = [sums[4]] + [lax.ppermute(sums[4 + k], "fsdp", shift_y(SIDE - k)) for k in range(1, SIDE)]
+    up_grad, down_grad = call(
+        finish_kernel, [blocks(CAP)] * 2, [S] * 5 + [V] * 8, [V] * 2, [], "finish", cost(3)
+    )(
+        place, up_count, down_count,
+        up_scale[0].astype(jnp.float32) * grad_norm,
+        down_scale[0].astype(jnp.float32) * grad_norm,
+        *near_up, *near_down,
+    )
+    return input_grad, up_grad[None], down_grad[None]
+
+
+def on_device(*args):
+    up_blocks, up_scale, down_blocks, down_scale = args[2:6]
+    up_live = args[10][0].reshape(SIDE, SIDE).sum(1).max()
+    down_live = args[11][0].reshape(SIDE, SIDE).sum(0).max()
+    crowded = any_tensor(jnp.maximum(up_live, down_live).reshape(1))[0] > ROOM
+    scaled_up = up_blocks[0] * up_scale[0][:, None, None]
+    scaled_down = down_blocks[0] * down_scale[0][:, None, None]
+    near_up = [scaled_up] + [lax.ppermute(scaled_up, "fsdp", shift_x(k)) for k in range(1, SIDE)]
+    near_down = [scaled_down] + [lax.ppermute(scaled_down, "fsdp", shift_y(k)) for k in range(1, SIDE)]
+    return lax.cond(
+        crowded,
+        lambda near_up, near_down, *rest: full_exchange(*rest),
+        packed_exchange,
+        near_up, near_down, *args,
+    )
+
+
 def solution(mesh):
     return jax.shard_map(
         on_device,

time: 559 us -> 276 us (0.49); the launches traced: 551 us -> 275 us
  matrix products: 267 us -> 0 us
  Pallas kernels: 0 us -> 76.9 us
  local copies, waits for them, and re-layouts: 61.9 us -> 2.42 us
  starting transfers between devices: 0.16 us -> 51.2 us
  blocking collectives: 41.1 us -> 0 us
  waiting for transfers between devices: 155 us -> 119 us
    dot_general x12 -> x0, matrix products: 267 us -> none  [the longest x1 51.3 us: on_device(): jnp.einsum('mc,mti->cti', placing, product, precision=lax.Precision.HIGHEST)]
    ppermute x0 -> x27, waiting for transfers between devices: none -> 119 us  [the longest x3 40.7 us: packed_exchange(): lax.ppermute(packed_down, 'fsdp', shift_x(m))]
    unnamed x5 -> x0, waiting for transfers between devices: 107 us -> none
    pallas_call x0 -> x7, Pallas kernels: none -> 76.9 us  [the longest x1 27.7 us: packed_exchange(): call(forward_kernel, [half, half], [S, V, V] + [A] * 8, [V, V], [tiles, t...]
    ppermute x0 -> x27, starting transfers between devices: none -> 51.2 us  [the longest x3 14.9 us: packed_exchange(): lax.ppermute(terms[4 + m], 'fsdp', shift_x(SIDE - m))]
    reduce_scatter x1, waiting for transfers between devices: 48.1 us -> 0.01 us  [packed_exchange(): lax.psum_scatter(partial, 'tensor', scatter_dimension=1, tiled=True)]
    unnamed x1 -> x0, blocking collectives: 41.1 us -> none
    unnamed x44 -> x1, local copies, waits for them, and re-layouts: 24.7 us -> 0.51 us
  transfers between devices with their start and end apart: 4 -> 28, of which waited for: 2 -> 13; matrix products, arithmetic and copies ran while one was open for 33% -> 2% of each run, Pallas kernels for 0% -> 12%
where the time goes in v1:
time: 276 us; the launch traced here: 275 us
  waiting for transfers between devices  119 us (43%)
  Pallas kernels  76.9 us (28%)
  starting transfers between devices  51.2 us (19%)
  between operations  17.5 us (6%)
  other arithmetic  7.4 us (3%)
    ppermute x3, waiting for transfers between devices, packed_exchange(): lax.ppermute(packed_down, 'fsdp', shift_x(m))  40.7 us
    pallas_call x1, Pallas kernels, packed_exchange(): call(forward_kernel, [half, half], [S, V, V] + [A] * 8, [V, V], [tiles, t...  27.7 us
    ppermute x3, waiting for transfers between devices, packed_exchange(): lax.ppermute(terms[m], 'fsdp', shift_y(SIDE - m))  21.2 us
    pallas_call x1, Pallas kernels, packed_exchange(): call(terms_kernel, [blocks(ROOM)] * 8, [S, V, V, V, V], [A] * 8, [tiles,...  20.3 us
    ppermute x3, waiting for transfers between devices, on_device(): lax.ppermute(scaled_down, 'fsdp', shift_y(k))  17.3 us
    ppermute x3, starting transfers between devices, packed_exchange(): lax.ppermute(terms[4 + m], 'fsdp', shift_x(SIDE - m))  14.9 us
    pallas_call x1, Pallas kernels, packed_exchange(): call(partial_kernel, [jax.ShapeDtypeStruct((tokens, width), jnp.bfloat16)...  14.8 us
    ppermute x3, waiting for transfers between devices, packed_exchange(): lax.ppermute(packed_up, 'fsdp', shift_y(m))  11.8 us
  transfers between devices with their start and end apart: 28, of which 13 were waited for; matrix products, arithmetic and copies ran while one was open for 2% of the time, Pallas kernels for 12%

profile of v1, /device:TPU:0, one launch (start us, length us, event | category | flops | bytes accessed | tf_op | source)
XLA Modules:
  0.0 275.0 jit_solution(17840163469743446822)
XLA Ops:
  7.2 1.1 bitcast_multiply_fusion.1
  8.3 2.9 %collective-permute-start.23 = (bf16[12,128,128]{2,1,0:T(8,128)(2,1)S(1)}, bf16[12,128,128]{2,1,0:T(8,128)(2,1)S(1)}, u32[]{:S(2)}, u32[]{:S(2)}) collective-permute-start(bf16[12,128,128]{2,1,0:T(8,128)(2,1)S(1)} %bitcast_multiply_fusion.1), channel_id=1, source_target_pairs={{0,24},{8,0},{16,8},{24,16},{32,56},{40,32},{48,40},{56,48},{64,88... | collective-permute-start | bytes 1179656 | tf_op jit(solution)/shard_map/ppermute | solution.py:505
  11.2 0.8 collective-permute-start.22
  12.0 0.9 collective-permute-start.21
  13.4 1.3 reduce.6
  14.7 1.3 reduce.7
  18.9 0.9 collective-permute-start.18
  19.8 1.1 bitcast_multiply_fusion
  20.9 3.1 %collective-permute-start.26 = (bf16[12,128,128]{2,1,0:T(8,128)(2,1)S(1)}, bf16[12,128,128]{2,1,0:T(8,128)(2,1)S(1)}, u32[]{:S(2)}, u32[]{:S(2)}) collective-permute-start(bf16[12,128,128]{2,1,0:T(8,128)(2,1)S(1)} %bitcast_multiply_fusion), channel_id=1, source_target_pairs={{0,96},{8,104},{16,112},{24,120},{32,0},{40,8},{48,16},{56,24},{64... | collective-permute-start | bytes 1179656 | tf_op jit(solution)/shard_map/ppermute | solution.py:506
  24.7 3.3 %collective-permute-start.19 = (s32[1]{0:T(128)}, s32[1]{0:T(128)}, u32[]{:S(2)}, u32[]{:S(2)}) collective-permute-start(s32[1]{0:T(128)} %max.13), channel_id=1, source_target_pairs={{0,2},{1,3},{2,4},{3,5},{4,6},{5,7},{6,0},{7,1},{8,10},{9,11},{10,... | collective-permute-start | bytes 20 | tf_op jit(solution)/shard_map/ppermute | solution.py:171
  28.0 2.3 collective-permute-done.19
  30.9 3.2 %collective-permute-start.20 = (s32[1]{0:T(128)}, s32[1]{0:T(128)}, u32[]{:S(2)}, u32[]{:S(2)}) collective-permute-start(s32[1]{0:T(128)} %max.14), channel_id=1, source_target_pairs={{0,4},{1,5},{2,6},{3,7},{4,0},{5,1},{6,2},{7,3},{8,12},{9,13},{10,... | collective-permute-start | bytes 20 | tf_op jit(solution)/shard_map/ppermute | solution.py:171
  34.2 1.8 collective-permute-done.20
  36.7 1.0 collective-permute-start.24
  38.4 11.2 %collective-permute-done.25 = bf16[12,128,128]{2,1,0:T(8,128)(2,1)S(1)} collective-permute-done((bf16[12,128,128]{2,1,0:T(8,128)(2,1)S(1)}, bf16[12,128,128]{2,1,0:T(8,128)(2,1)S(1)}, u32[]{:S(2)}, u32[]{:S(2)}) %collective-permute-start.25) | collective-permute-done | bytes 393248 | tf_op jit(solution)/shard_map/ppermute | solution.py:506
  49.6 6.1 %collective-permute-done.24 = bf16[12,128,128]{2,1,0:T(8,128)(2,1)S(1)} collective-permute-done((bf16[12,128,128]{2,1,0:T(8,128)(2,1)S(1)}, bf16[12,128,128]{2,1,0:T(8,128)(2,1)S(1)}, u32[]{:S(2)}, u32[]{:S(2)}) %collective-permute-start.24) | collective-permute-done | bytes 393248 | tf_op jit(solution)/shard_map/ppermute | solution.py:506
  55.7 212.5 %conditional.1 = (bf16[256,1792]{1,0:T(8,128)(2,1)}, bf16[1,12,128,128]{3,2,1,0:T(8,128)(2,1)}, bf16[1,12,128,128]{3,2,1,0:T(8,128)(2,1)}) conditional(s32[]{:T(128)} %bitcast.43, (s32[1,16]{1,0:T(1,128)}, s32[1,192]{1,0:T(1,128)}, s32[1,192]{1,0:T(1,128)}, s32[1,16]{1,0:T(1,128)}, s32[1,192]{1,0:T(1,128)}, /*index=5*/s32[1,192]{1,0:T(1,128)}, ...), branch_computations={%region_4.6_spmd, %region_6.9_spmd} | conditional | flops 29286492160 | bytes 721866240 | solution.py:507
  55.7 0.6 pad_add_fusion.place
  56.3 2.3 pack.1
  58.6 2.1 collective-permute-start.5
  60.7 1.5 collective-permute-start.4
  62.2 0.6 collective-permute-start.2
  62.9 0.7 collective-permute-start.1
  63.5 39.9 %collective-permute-done.5.refs_7_ = bf16[30,128,128]{2,1,0:T(8,128)(2,1)S(1)} collective-permute-done((bf16[30,128,128]{2,1,0:T(8,128)(2,1)}, bf16[30,128,128]{2,1,0:T(8,128)(2,1)S(1)}, u32[]{:S(2)}, u32[]{:S(2)}) %collective-permute-start.5) | collective-permute-done | bytes 983072 | tf_op jit(solution)/shard_map/cond/branch_0_fun/ppermute | solution.py:447
  103.4 2.9 %table.1 = s32[8,128]{1,0:T(8,128)} custom-call(s32[2]{0:T(128)} %pad_add_fusion.place, s32[16]{0:T(128)} %bitcast.125, s32[192]{0:T(256)} %bitcast.134, s32[192]{0:T(256)} %bitcast.141, s32[16]{0:T(128)} %bitcast.130, s32[192]{0:T(256)} %bitcast.144, s32[192]{0:T(256)} %bitcast.147), custom_call_target="tpu_custom_call" | custom-call | bytes 6000000 | tf_op jit(solution)/shard_map/cond/branch_0_fun/table/pallas_call | solution.py:448
  106.3 0.8 collective-permute-done.3.refs_5_
  107.1 11.8 %collective-permute-done.refs_1_ = bf16[30,128,128]{2,1,0:T(8,128)(2,1)S(1)} collective-permute-done((bf16[30,128,128]{2,1,0:T(8,128)(2,1)}, bf16[30,128,128]{2,1,0:T(8,128)(2,1)S(1)}, u32[]{:S(2)}, u32[]{:S(2)}) %collective-permute-start) | collective-permute-done | bytes 983072 | tf_op jit(solution)/shard_map/cond/branch_0_fun/ppermute | solution.py:446
  118.9 0.9 copy-done.4
  119.9 27.7 %forward.1 = (bf16[256,7168]{1,0:T(8,128)(2,1)}, bf16[256,7168]{1,0:T(8,128)(2,1)}) custom-call(s32[8,128]{1,0:T(8,128)} %table.1, bf16[256,14336]{1,0:T(8,128)(2,1)} %get-tuple-element.66.acts, bf16[256,14336]{1,0:T(8,128)(2,1)} %get-tuple-element.67.grads, bf16[30,128,128]{2,1,0:T(8,128)(2,1)} %get-tuple-element.76.refs_0_, ...), custom_call_target="tpu_custom_call" | custom-call | bytes 75000000 | tf_op jit(solution)/shard_map/cond/branch_0_fun/forward/pallas_call | solution.py:453
  147.6 14.8 %partial.1 = bf16[256,14336]{1,0:T(8,128)(2,1)} custom-call(s32[8,128]{1,0:T(8,128)} %table.1, bf16[256,7168]{1,0:T(8,128)(2,1)} %get-tuple-element.78.hidden_grad, bf16[30,128,128]{2,1,0:T(8,128)(2,1)} %get-tuple-element.76.refs_0_, bf16[30,128,128]{2,1,0:T(8,128)(2,1)} %copy-done.4, bf16[30,128,128]{2,1,0:T(8,128)(2,1)} %copy-done.3, ...), custom_call_target="tpu_custom_call" | custom-call | bytes 45000000 | tf_op jit(solution)/shard_map/cond/branch_0_fun/partial/pallas_call | solution.py:473
  162.4 20.3 %terms.1 = (bf16[30,128,128]{2,1,0:T(8,128)(2,1)}, bf16[30,128,128]{2,1,0:T(8,128)(2,1)}, bf16[30,128,128]{2,1,0:T(8,128)(2,1)}, bf16[30,128,128]{2,1,0:T(8,128)...) custom-call(s32[8,128]{1,0:T(8,128)} %table.1, ...), custom_call_target="tpu_custom_call" | custom-call | bytes 60000000 | tf_op jit(solution)/shard_map/cond/branch_0_fun/terms/pallas_call | solution.py:463
  182.9 0.8 collective-permute-start.7
  183.7 1.2 collective-permute-start.8
  184.9 3.5 %collective-permute-start.9 = (bf16[30,128,128]{2,1,0:T(8,128)(2,1)}, bf16[30,128,128]{2,1,0:T(8,128)(2,1)S(1)}, u32[]{:S(2)}, u32[]{:S(2)}) collective-permute-start(bf16[30,128,128]{2,1,0:T(8,128)(2,1)} %get-tuple-element.87), channel_id=1, source_target_pairs={{0,24},{8,0},{16,8},{24,16},{32,56},{40,32},{48,40},{56,48},{64,88... | collective-permute-start | bytes 2949128 | tf_op jit(solution)/shard_map/cond/branch_0_fun/ppermute | solution.py:472
  188.7 19.0 %collective-permute-done.6.refs_1_ = bf16[30,128,128]{2,1,0:T(8,128)(2,1)S(1)} collective-permute-done((bf16[30,128,128]{2,1,0:T(8,128)(2,1)}, bf16[30,128,128]{2,1,0:T(8,128)(2,1)S(1)}, u32[]{:S(2)}, u32[]{:S(2)}) %collective-permute-start.6) | collective-permute-done | bytes 983072 | tf_op jit(solution)/shard_map/cond/branch_0_fun/ppermute | solution.py:471
  207.8 11.1 %collective-permute-start.11 = (bf16[30,128,128]{2,1,0:T(8,128)(2,1)}, bf16[30,128,128]{2,1,0:T(8,128)(2,1)}, u32[]{:S(2)}, u32[]{:S(2)}) collective-permute-start(bf16[30,128,128]{2,1,0:T(8,128)(2,1)} %get-tuple-element.89), channel_id=1, source_target_pairs={{0,8},{8,16},{16,24},{24,0},{32,40},{40,48},{48,56},{56,32},{64,72... | collective-permute-start | bytes 2949128 | tf_op jit(solution)/shard_map/cond/branch_0_fun/ppermute | solution.py:472
  218.9 2.1 collective-permute-done.8.refs_3_
  221.0 11.5 %collective-permute-done.11.refs_7_ = bf16[30,128,128]{2,1,0:T(8,128)(2,1)} collective-permute-done((bf16[30,128,128]{2,1,0:T(8,128)(2,1)}, bf16[30,128,128]{2,1,0:T(8,128)(2,1)}, u32[]{:S(2)}, u32[]{:S(2)}) %collective-permute-start.11) | collective-permute-done | bytes 983072 | tf_op jit(solution)/shard_map/cond/branch_0_fun/ppermute | solution.py:472
  232.5 5.9 %unpack.1 = (bf16[12,128,128]{2,1,0:T(8,128)(2,1)}, bf16[12,128,128]{2,1,0:T(8,128)(2,1)}, bf16[12,128,128]{2,1,0:T(8,128)(2,1)}, bf16[12,128,128]{2,1,0:T(8,128...) custom-call(s32[2]{0:T(128)} %pad_add_fusion.place, ...), custom_call_target="tpu_custom_call" | custom-call | bytes 9000000 | tf_op jit(solution)/shard_map/cond/branch_0_fun/unpack/pallas_call | solution.py:482
  238.4 1.9 collective-permute-start.12
  240.3 0.9 collective-permute-start.13
  241.2 8.9 %collective-permute-start.15 = (bf16[12,128,128]{2,1,0:T(8,128)(2,1)}, bf16[12,128,128]{2,1,0:T(8,128)(2,1)S(1)}, u32[]{:S(2)}, u32[]{:S(2)}) collective-permute-start(bf16[12,128,128]{2,1,0:T(8,128)(2,1)} %get-tuple-element.95), channel_id=1, source_target_pairs={{0,96},{8,104},{16,112},{24,120},{32,0},{40,8},{48,16},{56,24},{64... | collective-permute-start | bytes 1179656 | tf_op jit(solution)/shard_map/cond/branch_0_fun/ppermute | solution.py:486
  250.1 0.8 collective-permute-start.17
  251.5 2.5 collective-permute-done.14.refs_3_
  254.0 5.9 %collective-permute-done.15.refs_5_ = bf16[12,128,128]{2,1,0:T(8,128)(2,1)S(1)} collective-permute-done((bf16[12,128,128]{2,1,0:T(8,128)(2,1)}, bf16[12,128,128]{2,1,0:T(8,128)(2,1)S(1)}, u32[]{:S(2)}, u32[]{:S(2)}) %collective-permute-start.15) | collective-permute-done | bytes 393248 | tf_op jit(solution)/shard_map/cond/branch_0_fun/ppermute | solution.py:486
  259.9 3.9 %collective-permute-done.17.refs_7_ = bf16[12,128,128]{2,1,0:T(8,128)(2,1)S(1)} collective-permute-done((bf16[12,128,128]{2,1,0:T(8,128)(2,1)}, bf16[12,128,128]{2,1,0:T(8,128)(2,1)S(1)}, u32[]{:S(2)}, u32[]{:S(2)}) %collective-permute-start.17) | collective-permute-done | bytes 393248 | tf_op jit(solution)/shard_map/cond/branch_0_fun/ppermute | solution.py:486
  263.8 0.7 copy-done.15
  264.6 3.1 %finish.1 = (bf16[12,128,128]{2,1,0:T(8,128)(2,1)}, bf16[12,128,128]{2,1,0:T(8,128)(2,1)}) custom-call(s32[2]{0:T(128)} %pad_add_fusion.place, s32[16]{0:T(128)S(1)} %bitcast.127, s32[16]{0:T(128)S(1)} %bitcast.132, f32[12]{0:T(128)} %get-tuple-element.133.up_factor, f32[12]{0:T(128)} %get-tuple-element.132.down_factor, ...), custom_call_target="tpu_custom_call" | custom-call | bytes 9000000 | tf_op jit(solution)/shard_map/cond/branch_0_fun/finish/pallas_call | solution.py:487
  (66 shorter events, 3.9 us)
Async XLA Ops:
  8.3 28.4 %collective-permute-start.23 = (bf16[12,128,128]{2,1,0:T(8,128)(2,1)S(1)}, bf16[12,128,128]{2,1,0:T(8,128)(2,1)S(1)}, u32[]{:S(2)}, u32[]{:S(2)}) collective-permute-start(bf16[12,128,128]{2,1,0:T(8,128)(2,1)S(1)} %bitcast_multiply_fusion.1), channel_id=1, source_target_pairs={{0,24},{8,0},{16,8},{24,16},{32,56},{40,32},{48,40},{56,48},{64,88... | collective-permute-start | bytes 1179656 | tf_op jit(solution)/shard_map/ppermute | solution.py:505
  11.2 27.2 %collective-permute-start.22 = (bf16[12,128,128]{2,1,0:T(8,128)(2,1)S(1)}, bf16[12,128,128]{2,1,0:T(8,128)(2,1)S(1)}, u32[]{:S(2)}, u32[]{:S(2)}) collective-permute-start(bf16[12,128,128]{2,1,0:T(8,128)(2,1)S(1)} %bitcast_multiply_fusion.1), channel_id=1, source_target_pairs={{0,16},{8,24},{16,0},{24,8},{32,48},{40,56},{48,32},{56,40},{64,80... | collective-permute-start | bytes 1179656 | tf_op jit(solution)/shard_map/ppermute | solution.py:505
  12.0 26.4 %collective-permute-start.21 = (bf16[12,128,128]{2,1,0:T(8,128)(2,1)S(1)}, bf16[12,128,128]{2,1,0:T(8,128)(2,1)S(1)}, u32[]{:S(2)}, u32[]{:S(2)}) collective-permute-start(bf16[12,128,128]{2,1,0:T(8,128)(2,1)S(1)} %bitcast_multiply_fusion.1), channel_id=1, source_target_pairs={{0,8},{8,16},{16,24},{24,0},{32,40},{40,48},{48,56},{56,32},{64,72... | collective-permute-start | bytes 1179656 | tf_op jit(solution)/shard_map/ppermute | solution.py:505
  18.9 5.1 %collective-permute-start.18 = (s32[1]{0:T(128)}, s32[1]{0:T(128)}, u32[]{:S(2)}, u32[]{:S(2)}) collective-permute-start(s32[1]{0:T(128)} %bitcast.42), channel_id=1, source_target_pairs={{0,1},{1,0},{2,3},{3,2},{4,5},{5,4},{6,7},{7,6},{8,9},{9,8},{10,11... | collective-permute-start | bytes 20 | tf_op jit(solution)/shard_map/ppermute | solution.py:171
  20.9 17.5 %collective-permute-start.26 = (bf16[12,128,128]{2,1,0:T(8,128)(2,1)S(1)}, bf16[12,128,128]{2,1,0:T(8,128)(2,1)S(1)}, u32[]{:S(2)}, u32[]{:S(2)}) collective-permute-start(bf16[12,128,128]{2,1,0:T(8,128)(2,1)S(1)} %bitcast_multiply_fusion), channel_id=1, source_target_pairs={{0,96},{8,104},{16,112},{24,120},{32,0},{40,8},{48,16},{56,24},{64... | collective-permute-start | bytes 1179656 | tf_op jit(solution)/shard_map/ppermute | solution.py:506
  24.7 5.6 %collective-permute-start.19 = (s32[1]{0:T(128)}, s32[1]{0:T(128)}, u32[]{:S(2)}, u32[]{:S(2)}) collective-permute-start(s32[1]{0:T(128)} %max.13), channel_id=1, source_target_pairs={{0,2},{1,3},{2,4},{3,5},{4,6},{5,7},{6,0},{7,1},{8,10},{9,11},{10,... | collective-permute-start | bytes 20 | tf_op jit(solution)/shard_map/ppermute | solution.py:171
  30.9 5.1 %collective-permute-start.20 = (s32[1]{0:T(128)}, s32[1]{0:T(128)}, u32[]{:S(2)}, u32[]{:S(2)}) collective-permute-start(s32[1]{0:T(128)} %max.14), channel_id=1, source_target_pairs={{0,4},{1,5},{2,6},{3,7},{4,0},{5,1},{6,2},{7,3},{8,12},{9,13},{10,... | collective-permute-start | bytes 20 | tf_op jit(solution)/shard_map/ppermute | solution.py:171
  36.0 13.6 %collective-permute-start.25 = (bf16[12,128,128]{2,1,0:T(8,128)(2,1)S(1)}, bf16[12,128,128]{2,1,0:T(8,128)(2,1)S(1)}, u32[]{:S(2)}, u32[]{:S(2)}) collective-permute-start(bf16[12,128,128]{2,1,0:T(8,128)(2,1)S(1)} %bitcast_multiply_fusion), channel_id=1, source_target_pairs={{0,64},{8,72},{16,80},{24,88},{32,96},{40,104},{48,112},{56,120},{... | collective-permute-start | bytes 1179656 | tf_op jit(solution)/shard_map/ppermute | solution.py:506
  36.7 19.0 %collective-permute-start.24 = (bf16[12,128,128]{2,1,0:T(8,128)(2,1)S(1)}, bf16[12,128,128]{2,1,0:T(8,128)(2,1)S(1)}, u32[]{:S(2)}, u32[]{:S(2)}) collective-permute-start(bf16[12,128,128]{2,1,0:T(8,128)(2,1)S(1)} %bitcast_multiply_fusion), channel_id=1, source_target_pairs={{0,32},{8,40},{16,48},{24,56},{32,64},{40,72},{48,80},{56,88},{64,... | collective-permute-start | bytes 1179656 | tf_op jit(solution)/shard_map/ppermute | solution.py:506
  55.7 211.9 %reduce-scatter.6.cloned.1.call-start = ((), (), s32[]{:S(2)}) async-start(), calls=%async_computation.2 | async-start | bytes 8257536 | tf_op jit(solution)/shard_map/cond/branch_0_fun/reduce_scatter | solution.py:481
  58.6 44.8 %collective-permute-start.5 = (bf16[30,128,128]{2,1,0:T(8,128)(2,1)}, bf16[30,128,128]{2,1,0:T(8,128)(2,1)S(1)}, u32[]{:S(2)}, u32[]{:S(2)}) collective-permute-start(bf16[30,128,128]{2,1,0:T(8,128)(2,1)} %get-tuple-element.77.refs_4_), channel_id=1, source_target_pairs={{0,24},{8,0},{16,8},{24,16},{32,56},{40,32},{48,40},{56,48},{64,88... | collective-permute-start | bytes 2949128 | tf_op jit(solution)/shard_map/cond/branch_0_fun/ppermute | solution.py:447
  60.7 45.6 %collective-permute-start.4 = (bf16[30,128,128]{2,1,0:T(8,128)(2,1)}, bf16[30,128,128]{2,1,0:T(8,128)(2,1)}, u32[]{:S(2)}, u32[]{:S(2)}) collective-permute-start(bf16[30,128,128]{2,1,0:T(8,128)(2,1)} %get-tuple-element.77.refs_4_), channel_id=1, source_target_pairs={{0,16},{8,24},{16,0},{24,8},{32,48},{40,56},{48,32},{56,40},{64,80... | collective-permute-start | bytes 2949128 | tf_op jit(solution)/shard_map/cond/branch_0_fun/ppermute | solution.py:447
  62.2 44.9 %collective-permute-start.3 = (bf16[30,128,128]{2,1,0:T(8,128)(2,1)}, bf16[30,128,128]{2,1,0:T(8,128)(2,1)}, u32[]{:S(2)}, u32[]{:S(2)}) collective-permute-start(bf16[30,128,128]{2,1,0:T(8,128)(2,1)} %get-tuple-element.77.refs_4_), channel_id=1, source_target_pairs={{0,8},{8,16},{16,24},{24,0},{32,40},{40,48},{48,56},{56,32},{64,72... | collective-permute-start | bytes 2949128 | tf_op jit(solution)/shard_map/cond/branch_0_fun/ppermute | solution.py:447
  62.2 44.9 %collective-permute-start.2 = (bf16[30,128,128]{2,1,0:T(8,128)(2,1)}, bf16[30,128,128]{2,1,0:T(8,128)(2,1)S(1)}, u32[]{:S(2)}, u32[]{:S(2)}) collective-permute-start(bf16[30,128,128]{2,1,0:T(8,128)(2,1)} %get-tuple-element.76.refs_0_), channel_id=1, source_target_pairs={{0,96},{8,104},{16,112},{24,120},{32,0},{40,8},{48,16},{56,24},{64... | collective-permute-start | bytes 2949128 | tf_op jit(solution)/shard_map/cond/branch_0_fun/ppermute | solution.py:446
  62.9 44.2 %collective-permute-start.1 = (bf16[30,128,128]{2,1,0:T(8,128)(2,1)}, bf16[30,128,128]{2,1,0:T(8,128)(2,1)S(1)}, u32[]{:S(2)}, u32[]{:S(2)}) collective-permute-start(bf16[30,128,128]{2,1,0:T(8,128)(2,1)} %get-tuple-element.76.refs_0_), channel_id=1, source_target_pairs={{0,64},{8,72},{16,80},{24,88},{32,96},{40,104},{48,112},{56,120},{... | collective-permute-start | bytes 2949128 | tf_op jit(solution)/shard_map/cond/branch_0_fun/ppermute | solution.py:446
  103.4 15.5 %copy-start.9 = (bf16[30,128,128]{2,1,0:T(8,128)(2,1)}, bf16[30,128,128]{2,1,0:T(8,128)(2,1)S(1)}, u32[]{:S(2)}) copy-start(bf16[30,128,128]{2,1,0:T(8,128)(2,1)S(1)} %collective-permute-done.5.refs_7_) | copy-start | bytes 2949124 | tf_op jit(solution)/shard_map/cond
  103.4 15.5 %collective-permute-start = (bf16[30,128,128]{2,1,0:T(8,128)(2,1)}, bf16[30,128,128]{2,1,0:T(8,128)(2,1)S(1)}, u32[]{:S(2)}, u32[]{:S(2)}) collective-permute-start(bf16[30,128,128]{2,1,0:T(8,128)(2,1)} %get-tuple-element.76.refs_0_), channel_id=1, source_target_pairs={{0,32},{8,40},{16,48},{24,56},{32,64},{40,72},{48,80},{56,88},{64,... | collective-permute-start | bytes 2949128 | tf_op jit(solution)/shard_map/cond/branch_0_fun/ppermute | solution.py:446
  107.1 11.9 %copy-start.2 = (bf16[30,128,128]{2,1,0:T(8,128)(2,1)}, bf16[30,128,128]{2,1,0:T(8,128)(2,1)S(1)}, u32[]{:S(2)}) copy-start(bf16[30,128,128]{2,1,0:T(8,128)(2,1)S(1)} %collective-permute-done.2.refs_3_) | copy-start | bytes 2949124 | tf_op jit(solution)/shard_map/cond
  107.1 11.8 %copy-start.3 = (bf16[30,128,128]{2,1,0:T(8,128)(2,1)}, bf16[30,128,128]{2,1,0:T(8,128)(2,1)S(1)}, u32[]{:S(2)}) copy-start(bf16[30,128,128]{2,1,0:T(8,128)(2,1)S(1)} %collective-permute-done.1.refs_2_) | copy-start | bytes 2949124 | tf_op jit(solution)/shard_map/cond
  118.9 1.0 copy-start.4
  162.4 70.1 %copy-start.16 = (s32[1,16]{1,0:T(1,128)S(1)}, s32[1,16]{1,0:T(1,128)}, u32[]{:S(2)}) copy-start(s32[1,16]{1,0:T(1,128)} %get-tuple-element.60) | copy-start | bytes 196 | tf_op jit(solution)/shard_map/cond
  162.4 70.1 %copy-start.17 = (s32[1,16]{1,0:T(1,128)S(1)}, s32[1,16]{1,0:T(1,128)}, u32[]{:S(2)}) copy-start(s32[1,16]{1,0:T(1,128)} %get-tuple-element.63) | copy-start | bytes 196 | tf_op jit(solution)/shard_map/cond
  182.8 68.2 %copy-start.24 = (bf16[1,12]{1,0:T(2,128)(2,1)S(1)}, bf16[1,12]{1,0:T(2,128)(2,1)}, u32[]{:S(2)}) copy-start(bf16[1,12]{1,0:T(2,128)(2,1)} %get-tuple-element.79) | copy-start | bytes 76 | tf_op jit(solution)/shard_map/cond
  182.8 68.2 %copy-start.27 = (bf16[1,12]{1,0:T(2,128)(2,1)S(1)}, bf16[1,12]{1,0:T(2,128)(2,1)}, u32[]{:S(2)}) copy-start(bf16[1,12]{1,0:T(2,128)(2,1)} %get-tuple-element.80) | copy-start | bytes 76 | tf_op jit(solution)/shard_map/cond
  182.8 25.0 %collective-permute-start.6 = (bf16[30,128,128]{2,1,0:T(8,128)(2,1)}, bf16[30,128,128]{2,1,0:T(8,128)(2,1)S(1)}, u32[]{:S(2)}, u32[]{:S(2)}) collective-permute-start(bf16[30,128,128]{2,1,0:T(8,128)(2,1)} %get-tuple-element.83), channel_id=1, source_target_pairs={{0,96},{8,104},{16,112},{24,120},{32,0},{40,8},{48,16},{56,24},{64... | collective-permute-start | bytes 2949128 | tf_op jit(solution)/shard_map/cond/branch_0_fun/ppermute | solution.py:471
  182.9 36.0 %collective-permute-start.7 = (bf16[30,128,128]{2,1,0:T(8,128)(2,1)}, bf16[30,128,128]{2,1,0:T(8,128)(2,1)S(1)}, u32[]{:S(2)}, u32[]{:S(2)}) collective-permute-start(bf16[30,128,128]{2,1,0:T(8,128)(2,1)} %get-tuple-element.84), channel_id=1, source_target_pairs={{0,64},{8,72},{16,80},{24,88},{32,96},{40,104},{48,112},{56,120},{... | collective-permute-start | bytes 2949128 | tf_op jit(solution)/shard_map/cond/branch_0_fun/ppermute | solution.py:471
  183.7 37.3 %collective-permute-start.8 = (bf16[30,128,128]{2,1,0:T(8,128)(2,1)}, bf16[30,128,128]{2,1,0:T(8,128)(2,1)S(1)}, u32[]{:S(2)}, u32[]{:S(2)}) collective-permute-start(bf16[30,128,128]{2,1,0:T(8,128)(2,1)} %get-tuple-element.85), channel_id=1, source_target_pairs={{0,32},{8,40},{16,48},{24,56},{32,64},{40,72},{48,80},{56,88},{64,... | collective-permute-start | bytes 2949128 | tf_op jit(solution)/shard_map/cond/branch_0_fun/ppermute | solution.py:471
  184.9 36.1 %collective-permute-start.9 = (bf16[30,128,128]{2,1,0:T(8,128)(2,1)}, bf16[30,128,128]{2,1,0:T(8,128)(2,1)S(1)}, u32[]{:S(2)}, u32[]{:S(2)}) collective-permute-start(bf16[30,128,128]{2,1,0:T(8,128)(2,1)} %get-tuple-element.87), channel_id=1, source_target_pairs={{0,24},{8,0},{16,8},{24,16},{32,56},{40,32},{48,40},{56,48},{64,88... | collective-permute-start | bytes 2949128 | tf_op jit(solution)/shard_map/cond/branch_0_fun/ppermute | solution.py:472
  188.4 32.6 %collective-permute-start.10 = (bf16[30,128,128]{2,1,0:T(8,128)(2,1)}, bf16[30,128,128]{2,1,0:T(8,128)(2,1)}, u32[]{:S(2)}, u32[]{:S(2)}) collective-permute-start(bf16[30,128,128]{2,1,0:T(8,128)(2,1)} %get-tuple-element.88), channel_id=1, source_target_pairs={{0,16},{8,24},{16,0},{24,8},{32,48},{40,56},{48,32},{56,40},{64,80... | collective-permute-start | bytes 2949128 | tf_op jit(solution)/shard_map/cond/branch_0_fun/ppermute | solution.py:472
  207.8 24.7 %copy-start.5 = (bf16[30,128,128]{2,1,0:T(8,128)(2,1)}, bf16[30,128,128]{2,1,0:T(8,128)(2,1)S(1)}, u32[]{:S(2)}) copy-start(bf16[30,128,128]{2,1,0:T(8,128)(2,1)S(1)} %collective-permute-done.6.refs_1_) | copy-start | bytes 2949124 | tf_op jit(solution)/shard_map/cond
  207.8 24.7 %collective-permute-start.11 = (bf16[30,128,128]{2,1,0:T(8,128)(2,1)}, bf16[30,128,128]{2,1,0:T(8,128)(2,1)}, u32[]{:S(2)}, u32[]{:S(2)}) collective-permute-start(bf16[30,128,128]{2,1,0:T(8,128)(2,1)} %get-tuple-element.89), channel_id=1, source_target_pairs={{0,8},{8,16},{16,24},{24,0},{32,40},{40,48},{48,56},{56,32},{64,72... | collective-permute-start | bytes 2949128 | tf_op jit(solution)/shard_map/cond/branch_0_fun/ppermute | solution.py:472
  218.8 13.6 %copy-start.6 = (bf16[30,128,128]{2,1,0:T(8,128)(2,1)}, bf16[30,128,128]{2,1,0:T(8,128)(2,1)S(1)}, u32[]{:S(2)}) copy-start(bf16[30,128,128]{2,1,0:T(8,128)(2,1)S(1)} %collective-permute-done.7.refs_2_) | copy-start | bytes 2949124 | tf_op jit(solution)/shard_map/cond
  221.0 11.5 %copy-start.7 = (bf16[30,128,128]{2,1,0:T(8,128)(2,1)}, bf16[30,128,128]{2,1,0:T(8,128)(2,1)S(1)}, u32[]{:S(2)}) copy-start(bf16[30,128,128]{2,1,0:T(8,128)(2,1)S(1)} %collective-permute-done.8.refs_3_) | copy-start | bytes 2949124 | tf_op jit(solution)/shard_map/cond
  221.0 11.5 %copy-start.8 = (bf16[30,128,128]{2,1,0:T(8,128)(2,1)}, bf16[30,128,128]{2,1,0:T(8,128)(2,1)S(1)}, u32[]{:S(2)}) copy-start(bf16[30,128,128]{2,1,0:T(8,128)(2,1)S(1)} %collective-permute-done.9.refs_5_) | copy-start | bytes 2949124 | tf_op jit(solution)/shard_map/cond
  238.4 11.7 %collective-permute-start.12 = (bf16[12,128,128]{2,1,0:T(8,128)(2,1)}, bf16[12,128,128]{2,1,0:T(8,128)(2,1)S(1)}, u32[]{:S(2)}, u32[]{:S(2)}) collective-permute-start(bf16[12,128,128]{2,1,0:T(8,128)(2,1)} %get-tuple-element.91), channel_id=1, source_target_pairs={{0,24},{8,0},{16,8},{24,16},{32,56},{40,32},{48,40},{56,48},{64,88... | collective-permute-start | bytes 1179656 | tf_op jit(solution)/shard_map/cond/branch_0_fun/ppermute | solution.py:485
  240.3 11.2 %collective-permute-start.13 = (bf16[12,128,128]{2,1,0:T(8,128)(2,1)}, bf16[12,128,128]{2,1,0:T(8,128)(2,1)S(1)}, u32[]{:S(2)}, u32[]{:S(2)}) collective-permute-start(bf16[12,128,128]{2,1,0:T(8,128)(2,1)} %get-tuple-element.92), channel_id=1, source_target_pairs={{0,16},{8,24},{16,0},{24,8},{32,48},{40,56},{48,32},{56,40},{64,80... | collective-permute-start | bytes 1179656 | tf_op jit(solution)/shard_map/cond/branch_0_fun/ppermute | solution.py:485
  241.1 12.9 %collective-permute-start.14 = (bf16[12,128,128]{2,1,0:T(8,128)(2,1)}, bf16[12,128,128]{2,1,0:T(8,128)(2,1)S(1)}, u32[]{:S(2)}, u32[]{:S(2)}) collective-permute-start(bf16[12,128,128]{2,1,0:T(8,128)(2,1)} %get-tuple-element.93), channel_id=1, source_target_pairs={{0,8},{8,16},{16,24},{24,0},{32,40},{40,48},{48,56},{56,32},{64,72... | collective-permute-start | bytes 1179656 | tf_op jit(solution)/shard_map/cond/branch_0_fun/ppermute | solution.py:485
  241.2 18.7 %collective-permute-start.15 = (bf16[12,128,128]{2,1,0:T(8,128)(2,1)}, bf16[12,128,128]{2,1,0:T(8,128)(2,1)S(1)}, u32[]{:S(2)}, u32[]{:S(2)}) collective-permute-start(bf16[12,128,128]{2,1,0:T(8,128)(2,1)} %get-tuple-element.95), channel_id=1, source_target_pairs={{0,96},{8,104},{16,112},{24,120},{32,0},{40,8},{48,16},{56,24},{64... | collective-permute-start | bytes 1179656 | tf_op jit(solution)/shard_map/cond/branch_0_fun/ppermute | solution.py:486
  250.1 9.8 %collective-permute-start.16 = (bf16[12,128,128]{2,1,0:T(8,128)(2,1)}, bf16[12,128,128]{2,1,0:T(8,128)(2,1)S(1)}, u32[]{:S(2)}, u32[]{:S(2)}) collective-permute-start(bf16[12,128,128]{2,1,0:T(8,128)(2,1)} %get-tuple-element.96), channel_id=1, source_target_pairs={{0,64},{8,72},{16,80},{24,88},{32,96},{40,104},{48,112},{56,120},{... | collective-permute-start | bytes 1179656 | tf_op jit(solution)/shard_map/cond/branch_0_fun/ppermute | solution.py:486
  250.1 13.7 %copy-start.10 = (bf16[12,128,128]{2,1,0:T(8,128)(2,1)}, bf16[12,128,128]{2,1,0:T(8,128)(2,1)S(1)}, u32[]{:S(2)}) copy-start(bf16[12,128,128]{2,1,0:T(8,128)(2,1)S(1)} %collective-permute-done.12.refs_1_) | copy-start | bytes 1179652 | tf_op jit(solution)/shard_map/cond
  250.1 13.7 %collective-permute-start.17 = (bf16[12,128,128]{2,1,0:T(8,128)(2,1)}, bf16[12,128,128]{2,1,0:T(8,128)(2,1)S(1)}, u32[]{:S(2)}, u32[]{:S(2)}) collective-permute-start(bf16[12,128,128]{2,1,0:T(8,128)(2,1)} %get-tuple-element.97), channel_id=1, source_target_pairs={{0,32},{8,40},{16,48},{24,56},{32,64},{40,72},{48,80},{56,88},{64,... | collective-permute-start | bytes 1179656 | tf_op jit(solution)/shard_map/cond/branch_0_fun/ppermute | solution.py:486
  251.5 12.3 %copy-start.11 = (bf16[12,128,128]{2,1,0:T(8,128)(2,1)}, bf16[12,128,128]{2,1,0:T(8,128)(2,1)S(1)}, u32[]{:S(2)}) copy-start(bf16[12,128,128]{2,1,0:T(8,128)(2,1)S(1)} %collective-permute-done.13.refs_2_) | copy-start | bytes 1179652 | tf_op jit(solution)/shard_map/cond
  254.0 9.8 %copy-start.12 = (bf16[12,128,128]{2,1,0:T(8,128)(2,1)}, bf16[12,128,128]{2,1,0:T(8,128)(2,1)S(1)}, u32[]{:S(2)}) copy-start(bf16[12,128,128]{2,1,0:T(8,128)(2,1)S(1)} %collective-permute-done.14.refs_3_) | copy-start | bytes 1179652 | tf_op jit(solution)/shard_map/cond
  259.9 3.9 %copy-start.13 = (bf16[12,128,128]{2,1,0:T(8,128)(2,1)}, bf16[12,128,128]{2,1,0:T(8,128)(2,1)S(1)}, u32[]{:S(2)}) copy-start(bf16[12,128,128]{2,1,0:T(8,128)(2,1)S(1)} %collective-permute-done.15.refs_5_) | copy-start | bytes 1179652 | tf_op jit(solution)/shard_map/cond
  259.9 3.9 %copy-start.14 = (bf16[12,128,128]{2,1,0:T(8,128)(2,1)}, bf16[12,128,128]{2,1,0:T(8,128)(2,1)S(1)}, u32[]{:S(2)}) copy-start(bf16[12,128,128]{2,1,0:T(8,128)(2,1)S(1)} %collective-permute-done.16.refs_6_) | copy-start | bytes 1179652 | tf_op jit(solution)/shard_map/cond
  263.8 0.8 copy-start.15
Sparse Core Ops, SparseCore 0:
  162.5 47.7 reduce-scatter.5

commit v2 on v0

v2 whole, which is shorter than its diff:
```python
import jax
import jax.numpy as jnp
from jax import lax
from jax.experimental import pallas as pl
from jax.experimental.pallas import tpu as pltpu
from jax.sharding import PartitionSpec as P

FF = 57344


ROOT_TWO_PI = 0.7978845608028654
CUBIC = 0.044715


def gelu_parts(hidden):
    tangent = jnp.tanh(ROOT_TWO_PI * (hidden + CUBIC * hidden * hidden * hidden))
    gelu_value = 0.5 * hidden * (1.0 + tangent)
    gelu_slope = 0.5 * (1.0 + tangent) + 0.5 * hidden * (1.0 - tangent * tangent) * ROOT_TWO_PI * (
        1.0 + 3.0 * CUBIC * hidden * hidden
    )
    return (gelu_value, gelu_slope)


SIDE = 4
CAP = 12
BLK = 128
ROOM = 30
LIST = 192
VMEM_LIMIT = 60 * 1024 * 1024
V, S, A = pltpu.VMEM, pltpu.SMEM, pl.ANY


def shift_x(step):
    return [(y * SIDE + x, y * SIDE + (x + step) % SIDE) for y in range(SIDE) for x in range(SIDE)]


def shift_y(step):
    return [(y * SIDE + x, (y + step) % SIDE * SIDE + x) for y in range(SIDE) for x in range(SIDE)]


def shift_z(step):
    return [(z * 2 + c, (z + step) % SIDE * 2 + c) for z in range(SIDE) for c in range(2)]


def along(axis, shift):
    return lambda array, step: lax.ppermute(array, axis, shift(step))


over_x, over_y, over_z = along("fsdp", shift_x), along("fsdp", shift_y), along("tensor", shift_z)


def back(place, step):
    return lax.rem(place + SIDE - step, SIDE)


def any_tensor(flag):
    def moved(pairs):
        return lax.ppermute(flag, "tensor", pairs)

    flag = jnp.maximum(flag, moved([(t, t ^ 1) for t in range(8)]))
    flag = jnp.maximum(flag, moved([(t, (t + 2) % 8) for t in range(8)]))
    return jnp.maximum(flag, moved([(t, (t + 4) % 8) for t in range(8)]))


def spread(rings, flag=None):
    half = rings[0][0].shape[0] // 2
    first = [(move(own, 1), move(own, 3)) for own, move in rings]
    if flag is not None:
        first, flag = lax.optimization_barrier((first, any_tensor(flag)))
    second = [
        (move(one[:half], 1), move(three[half:], 3))
        for (own, move), (one, three) in zip(rings, first)
    ]
    spreads = [
        (own, one, low, high, three)
        for (own, move), (one, three), (low, high) in zip(rings, first, second)
    ]
    return spreads if flag is None else (spreads, flag)


def add(*arrays):
    return sum(a.astype(jnp.float32) for a in arrays).astype(jnp.bfloat16)


def collect(rings):
    half = rings[0][3].shape[0]
    first = [(move(back, 3), move(fore, 1)) for own, back, fore, one, three, move in rings]
    second = [
        (move(add(one, from_fore[:half]), 3), move(add(three, from_back[:half]), 1))
        for (own, back, fore, one, three, move), (from_fore, from_back) in zip(rings, first)
    ]
    return [(ring[0],) + f + s for ring, f, s in zip(rings, first, second)]


def up_owner(y, x, far, near):
    return back(y, far) * SIDE + back(x, near)


def down_owner(y, x, far, near):
    return back(y, near) * SIDE + back(x, far)


def cost(us):
    return pl.CostEstimate(flops=0, bytes_accessed=int(us * 3e6), transcendentals=0)


def call(kernel, outs, in_spaces, out_spaces, scratch, name, us):
    return pl.pallas_call(
        kernel,
        out_shape=outs,
        in_specs=[pl.BlockSpec(memory_space=s) for s in in_spaces],
        out_specs=[pl.BlockSpec(memory_space=s) for s in out_spaces],
        scratch_shapes=scratch,
        compiler_params=pltpu.CompilerParams(vmem_limit_bytes=VMEM_LIMIT),
        cost_estimate=cost(us),
        name=name,
    )


def blocks(count):
    return jax.ShapeDtypeStruct((count, BLK, BLK), jnp.bfloat16)


def pieces(size):
    half = size // 2
    return ((0, 0, size), (1, 0, size), (2, 0, half), (2, half, half), (3, 0, size))


def pack_kernel(room, place, up_count, down_count, *refs):
    y, x = place[0], place[1]
    for owner_of, count, ins, out in (
        (up_owner, up_count, refs[:5], refs[10]),
        (down_owner, down_count, refs[5:10], refs[11]),
    ):
        position = 0
        for (near, first, size), source in zip(pieces(CAP), ins):
            live = jnp.clip(count[owner_of(y, x, 0, near)] - first, 0, size)
            live = jnp.minimum(live, room - position)

            def put(j, at, source=source, out=out):
                out[at] = source[j]
                return at + 1

            position = lax.fori_loop(0, live, put, position)


def table_kernel(room, place, up_count, up_row, up_col, down_count, down_row, down_col, table, most):
    y, x = place[0], place[1]
    largest = 0
    for first, owner_of, count, rows, cols in (
        (0, up_owner, up_count, up_row, up_col),
        (3, down_owner, down_count, down_row, down_col),
    ):
        def blank(i, unused, first=first):
            table[first, i] = SIDE * room
            table[first + 1, i] = 0
            table[first + 2, i] = 0
            return unused

        total = 0
        for far in range(SIDE):
            position = far * room
            wanted = 0
            for near in range(SIDE):
                owner = owner_of(y, x, far, near)
                wanted = wanted + count[owner]
                live = jnp.minimum(count[owner], (far + 1) * room - position)

                def note(j, unused, first=first, rows=rows, cols=cols, owner=owner, total=total, position=position):
                    table[first, total + j] = position + j
                    table[first + 1, total + j] = rows[owner * CAP + j]
                    table[first + 2, total + j] = cols[owner * CAP + j]
                    return unused

                lax.fori_loop(0, live, note, 0)
                total = total + live
                position = position + live
            largest = jnp.maximum(largest, wanted)
        padded = (total + 3) // 4
        lax.fori_loop(total, padded * 4, blank, 0)
        table[6, first] = padded
    most[0] = largest


def make_table(room, place, up_count, up_row, up_col, down_count, down_row, down_col):
    def kernel(*refs):
        table_kernel(room, *refs)

    outs = [jax.ShapeDtypeStruct((8, LIST), jnp.int32), jax.ShapeDtypeStruct((1,), jnp.int32)]
    return call(kernel, outs, [S] * 7, [S] * 2, [], "table", 3)(
        place, up_count, up_row, up_col, down_count, down_row, down_col
    )


def lane(index):
    return pl.ds(pl.multiple_of(index * BLK, BLK), BLK)


def block_products(table, first, take, give, left, tiles, out, contract, offset=0):
    def step(i, unused):
        products = []
        for u in range(4):
            at = i * 4 + u
            products.append(
                lax.dot_general(
                    left[:, lane(table[take, at])],
                    tiles[table[first, at]],
                    (((1,), (contract,)), ((), ())),
                    preferred_element_type=jnp.float32,
                )
            )
        for u in range(4):
            out[:, lane(table[give, i * 4 + u] + offset)] += products[u]
        return unused

    lax.fori_loop(0, table[6, first], step, 0)


def fetch_tiles(room, sources, target, sems):
    copies = [
        pltpu.make_async_copy(source, target.at[pl.ds(far * room + first, size)], sems.at[i])
        for i, ((far, first, size), source) in enumerate(zip(pieces(room), sources))
    ]
    for copy in copies:
        copy.start()
    target[SIDE * room] = jnp.zeros((BLK, BLK), jnp.bfloat16)
    return copies


SUM_PARTS = (
    (0, 0, 0, 0), (0, 1, 0, 1), (1, 0, 2, 0), (1, 1, 1, 1), (2, 0, 2, 1), (2, 1, 3, 0), (3, 0, 1, 0), (3, 1, 3, 1),
)


def term_parts(room):
    half = room // 2
    return (
        (0, 0, 0, room),
        (1, 0, 2 * room, half),
        (1, half, room + half, half),
        (2, 0, 2 * room + half, half),
        (2, half, 3 * room, half),
        (3, 0, room, half),
        (4, 0, 3 * room + half, half),
    )


def main_kernel(room, place, table, acts_in, grads_in, *refs):
    ups, downs = refs[:5], refs[5:10]
    keep_outs, send_out, up_outs, down_outs = refs[10:14], refs[14], refs[15:20], refs[20:25]
    acts, grads, up_tiles, down_tiles, sums, activated, hidden_grad, shares, sems = refs[25:]
    load_acts = pltpu.make_async_copy(acts_in, acts, sems.at[2, 0])
    load_grads = pltpu.make_async_copy(grads_in, grads, sems.at[2, 1])
    up_copies = fetch_tiles(room, ups, up_tiles, sems.at[0])
    load_acts.start()
    down_copies = fetch_tiles(room, downs, down_tiles, sems.at[1])
    load_grads.start()
    sums[...] = jnp.zeros_like(sums)
    for copy in up_copies:
        copy.wait()
    load_acts.wait()
    columns = activated.shape[1] // BLK
    block_products(table, 0, 1, 2, acts, up_tiles, sums, 0)
    for copy in down_copies:
        copy.wait()
    load_grads.wait()
    block_products(table, 3, 5, 4, grads, down_tiles, sums, 1, columns)

    def bend(i, unused):
        value, slope = gelu_parts(sums[:, lane(i)])
        activated[:, lane(i)] = value.astype(jnp.bfloat16)
        hidden_grad[:, lane(i)] = (sums[:, lane(i + columns)] * slope).astype(jnp.bfloat16)
        zero = jnp.zeros((sums.shape[0], BLK), jnp.float32)
        sums[:, lane(i)] = zero
        sums[:, lane(i + columns)] = zero
        return unused

    lax.fori_loop(0, columns, bend, 0)
    block_products(table, 0, 2, 1, hidden_grad, up_tiles, sums, 1)
    share = shares.shape[2] // BLK
    rows = shares.shape[1] // 2
    copies = []
    for first, core in ((SIDE, 1 - place[3]), (0, place[3])):
        for buffer, part, far, tokens in SUM_PARTS:
            base = (back(place[2], far) * 2 + core) * share

            def round_one(i, unused, base=base, at=first + buffer, part=part, tokens=tokens):
                shares[at, part * rows:(part + 1) * rows, lane(i)] = sums[
                    tokens * rows:(tokens + 1) * rows, lane(base + i)
                ].astype(jnp.bfloat16)
                return unused

            lax.fori_loop(0, share, round_one, 0)
        if first:
            copies.append(pltpu.make_async_copy(shares.at[pl.ds(SIDE, SIDE)], send_out, sems.at[2, 2]))
            copies[-1].start()
        else:
            for i in range(SIDE):
                copies.append(pltpu.make_async_copy(shares.at[i], keep_outs[i], sems.at[2, 3 + i]))
                copies[-1].start()
    for which, (left, right, terms, outs) in enumerate(
        ((acts, hidden_grad, up_tiles, up_outs), (activated, grads, down_tiles, down_outs))
    ):
        first = which * 3

        def body(i, unused, first=first, left=left, right=right, terms=terms):
            for u in range(4):
                at = i * 4 + u
                terms[table[first, at]] = lax.dot_general(
                    left[:, lane(table[first + 1, at])],
                    right[:, lane(table[first + 2, at])],
                    (((0,), (0,)), ((), ())),
                    preferred_element_type=jnp.float32,
                ).astype(jnp.bfloat16)
            return unused

        lax.fori_loop(0, table[6, first], body, 0)
        for i, (out, to, start, size) in enumerate(term_parts(room)):
            copies.append(
                pltpu.make_async_copy(
                    terms.at[pl.ds(start, size)], outs[out].at[pl.ds(to, size)], sems.at[which, i]
                )
            )
            copies[-1].start()
    for copy in copies:
        copy.wait()


def unpack_kernel(room, place, up_count, down_count, *refs):
    y, x = place[0], place[1]
    half = room // 2
    for owner_of, count, ins, outs in (
        (up_owner, up_count, refs[:5], refs[10:15]),
        (down_owner, down_count, refs[5:10], refs[15:20]),
    ):
        own, from_fore, from_back, rest_fore, rest_back = ins
        position = 0
        for out, to, start, size in sorted(term_parts(CAP), key=lambda part: part[2]):
            near, start = start // CAP, start % CAP
            live = jnp.clip(count[owner_of(y, x, 0, near)] - start, 0, size)
            live = jnp.minimum(live, room - position)
            low = jnp.clip(half - position, 0, live)

            def put_low(j, at, out=outs[out], to=to, own=own, first=rest_fore, second=from_back):
                out[to + j] = add(own[at], first[at], second[half + at])
                return at + 1

            def put_high(j, at, out=outs[out], to=to, own=own, first=from_fore, second=rest_back):
                out[to + j] = add(own[at], first[at], second[at - half])
                return at + 1

            position = lax.fori_loop(0, low, put_low, position)
            position = lax.fori_loop(low, live, put_high, position)


def finish_kernel(place, up_count, down_count, up_factor, down_factor, *refs):
    owner = place[0] * SIDE + place[1]
    half = CAP // 2
    for count, factor, ins, out in (
        (up_count, up_factor, refs[:5], refs[10]),
        (down_count, down_factor, refs[5:10], refs[11]),
    ):
        own, from_fore, from_back, rest_fore, rest_back = ins
        live = count[owner]
        for j in range(CAP):
            if j < half:
                items = (own[j], rest_fore[j], from_back[half + j])
            else:
                items = (own[j], from_fore[j], rest_back[j - half])
            total = sum(item.astype(jnp.float32) for item in items) * factor[j]
            out[j] = jnp.where(j < live, total, 0.0).astype(jnp.bfloat16)


def gather_far(room, place, up_count, down_count, near_up, near_down, flag=None):
    def kernel(*refs):
        pack_kernel(room, *refs)

    packed_up, packed_down = call(
        kernel, [blocks(room)] * 2, [S] * 3 + [V] * 10, [V] * 2, [], "pack", 3
    )(place, up_count, down_count, *near_up, *near_down)
    if flag is not None:
        flag, packed_up, packed_down = lax.optimization_barrier((flag, packed_up, packed_down))
    return spread([(packed_up, over_y), (packed_down, over_x)], flag)


def layer(room, place, table, far_up, far_down, activations, output_grad, up_factor, down_factor, up_count, down_count):
    tokens, width = activations.shape
    hidden_width = FF // lax.axis_size("tensor")
    share = width // (2 * SIDE)
    tiles = pltpu.VMEM((SIDE * room + 1, BLK, BLK), jnp.bfloat16)
    parts = [blocks(room)] * 3 + [blocks(room // 2)] * 2

    def main(*refs):
        main_kernel(room, *refs)

    def unpack(*refs):
        unpack_kernel(room, *refs)

    *keeps, send, up0, up1, up2, up3, up4, down0, down1, down2, down3, down4 = call(
        main,
        [jax.ShapeDtypeStruct((tokens, share), jnp.bfloat16)] * SIDE
        + [jax.ShapeDtypeStruct((SIDE, tokens, share), jnp.bfloat16)]
        + parts * 2,
        [S, S] + [A] * 12,
        [A] * 15,
        [pltpu.VMEM((tokens, width), jnp.bfloat16)] * 2
        + [tiles, tiles, pltpu.VMEM((tokens, 2 * hidden_width), jnp.float32)]
        + [pltpu.VMEM((tokens, hidden_width), jnp.bfloat16)] * 2
        + [pltpu.VMEM((2 * SIDE, tokens, share), jnp.bfloat16), pltpu.SemaphoreType.DMA((3, 8))],
        "main", 40,
    )(place, table, activations, output_grad, *far_up, *far_down)
    other = lax.ppermute(send, "tensor", [(t, t ^ 1) for t in range(2 * SIDE)])
    far_up_terms, far_down_terms = collect(
        [(up0, up1, up2, up3, up4, over_y), (down0, down1, down2, down3, down4, over_x)]
    )
    rows = tokens // 2
    from_fore = over_z(add(keeps[1], other[1]), 3)
    from_back = over_z(add(keeps[2], other[2]), 1)
    rest_fore = over_z(add(keeps[3][:rows], other[3][:rows], from_fore[:rows]), 3)
    rest_back = over_z(add(keeps[3][rows:], other[3][rows:], from_back[:rows]), 1)
    input_grad = jnp.concatenate(
        [
            add(keeps[0][:rows], other[0][:rows], rest_fore, from_back[rows:]),
            add(keeps[0][rows:], other[0][rows:], from_fore[rows:], rest_back),
        ]
    )
    caps = [blocks(CAP)] * 3 + [blocks(CAP // 2)] * 2
    sums = call(
        unpack, caps * 2, [S] * 3 + [V] * 10, [V] * 10, [], "unpack", 4
    )(place, up_count, down_count, *far_up_terms, *far_down_terms)
    near_up, near_down = collect([(*sums[:5], over_x), (*sums[5:], over_y)])
    up_grad, down_grad = call(
        finish_kernel, [blocks(CAP)] * 2, [S] * 5 + [V] * 10, [V] * 2, [], "finish", 3
    )(place, up_count, down_count, up_factor, down_factor, *near_up, *near_down)
    return input_grad, up_grad[None], down_grad[None]


def on_device(
    activations,
    output_grad,
    up_blocks,
    up_scale,
    down_blocks,
    down_scale,
    up_row_block,
    up_col_block,
    down_row_block,
    down_col_block,
    up_count,
    down_count,
):
    me, shard = lax.axis_index("fsdp"), lax.axis_index("tensor")
    place = jnp.stack([me // SIDE, me % SIDE, shard // 2, shard % 2]).astype(jnp.int32)
    up_count, down_count = up_count[0], down_count[0]
    names = (up_count, up_row_block[0], up_col_block[0], down_count, down_row_block[0], down_col_block[0])
    grad_norm = float(activations.shape[0] * lax.axis_size("fsdp")) ** (-0.5)
    rest = (
        activations,
        output_grad,
        up_scale[0].astype(jnp.float32) * grad_norm,
        down_scale[0].astype(jnp.float32) * grad_norm,
        up_count,
        down_count,
    )
    scaled_up = up_blocks[0] * up_scale[0][:, None, None]
    scaled_down = down_blocks[0] * down_scale[0][:, None, None]
    near_up, near_down = spread([(scaled_up, over_x), (scaled_down, over_y)])
    table, most = make_table(ROOM, place, *names)
    (far_up, far_down), most = gather_far(ROOM, place, up_count, down_count, near_up, near_down, most)
    crowded = most[0] > ROOM
    results = layer(ROOM, place, table, far_up, far_down, *rest)

    def full(results, near_up, near_down, *rest):
        room = SIDE * CAP
        far_up, far_down = gather_far(room, place, up_count, down_count, near_up, near_down)
        return layer(room, place, make_table(room, place, *names)[0], far_up, far_down, *rest)

    return lax.cond(
        crowded, full, lambda results, *unused: results, results, near_up, near_down, *rest
    )


def solution(mesh):
    return jax.shard_map(
        on_device,
        mesh=mesh,
        in_specs=(
            P("fsdp", None),
            P("fsdp", None),
            P("tensor", "fsdp", None, None),
            P("tensor", "fsdp"),
            P("tensor", "fsdp", None, None),
            P("tensor", "fsdp"),
            P("tensor", None),
            P("tensor", None),
            P("tensor", None),
            P("tensor", None),
            P("tensor", None),
            P("tensor", None),
        ),
        out_specs=(
            P("fsdp", "tensor"),
            P("tensor", "fsdp", None, None),
            P("tensor", "fsdp", None, None),
        ),
        check_vma=False,
    )
```

time: 559 us -> 219 us (0.39); the launches traced: 551 us -> 218 us
  matrix products: 267 us -> 0 us
  waiting for transfers between devices: 155 us -> 81.7 us
  starting transfers between devices: 0.16 us -> 57.6 us
  Pallas kernels: 0 us -> 56.3 us
  local copies, waits for them, and re-layouts: 61.9 us -> 8.58 us
  blocking collectives: 41.1 us -> 0 us
  between operations: 15.7 us -> 3.71 us
    dot_general x12 -> x0, matrix products: 267 us -> none  [the longest x1 51.3 us: on_device(): jnp.einsum('mc,mti->cti', placing, product, precision=lax.Precision.HIGHEST)]
    unnamed x5 -> x0, waiting for transfers between devices: 107 us -> none
    ppermute x0 -> x40, waiting for transfers between devices: none -> 81.7 us  [the longest x36 75.8 us: along(): return lambda array, step: lax.ppermute(array, axis, shift(step))]
    ppermute x0 -> x40, starting transfers between devices: none -> 57.6 us  [the longest x36 51.1 us: along(): return lambda array, step: lax.ppermute(array, axis, shift(step))]
    pallas_call x0 -> x5, Pallas kernels: none -> 56.3 us  [the longest x1 42.7 us: layer(): call(main, [jax.ShapeDtypeStruct((tokens, share), jnp.bfloat16)] * SIDE +...]
    reduce_scatter x1 -> x0, waiting for transfers between devices: 48.1 us -> none  [on_device(): lax.psum_scatter(flat_sum.astype(jnp.bfloat16), 'tensor', scatter_dimensi...]
    unnamed x1 -> x0, blocking collectives: 41.1 us -> none
    dot_general x1 -> x0, local copies, waits for them, and re-layouts: 17.9 us -> none  [pick_front(): jnp.einsum('ctb,mc->mtb', table, selector, preferred_element_type=jnp.flo...]
  transfers between devices with their start and end apart: 4 -> 40, of which waited for: 2 -> 19; matrix products, arithmetic and copies ran while one was open for 33% -> 4% of each run, Pallas kernels for 0% -> 5%
where the time goes in v2:
time: 219 us; the launch traced here: 218 us
  waiting for transfers between devices  81.7 us (37%)
  starting transfers between devices  57.6 us (26%)
  Pallas kernels  56.3 us (26%)
  other arithmetic  9.94 us (5%)
  local copies, waits for them, and re-layouts  8.58 us (4%)
  between operations  3.71 us (2%)
    ppermute x36, waiting for transfers between devices, along(): return lambda array, step: lax.ppermute(array, axis, shift(step))  75.8 us
    ppermute x36, starting transfers between devices, along(): return lambda array, step: lax.ppermute(array, axis, shift(step))  51.1 us
    pallas_call x1, Pallas kernels, layer(): call(main, [jax.ShapeDtypeStruct((tokens, share), jnp.bfloat16)] * SIDE +...  42.7 us
    convert_element_type x11, other arithmetic, add(): return sum((a.astype(jnp.float32) for a in arrays)).astype(jnp.bfloat16)  7.6 us
    unnamed x112, local copies, waits for them, and re-layouts  6.88 us
    ppermute x3, starting transfers between devices, moved(): return lax.ppermute(flag, 'tensor', pairs)  6.44 us
    ppermute x3, waiting for transfers between devices, moved(): return lax.ppermute(flag, 'tensor', pairs)  5.91 us
    pallas_call x1, Pallas kernels, layer(): call(unpack, caps * 2, [S] * 3 + [V] * 10, [V] * 10, [], 'unpack', 4)  5.58 us
  transfers between devices with their start and end apart: 40, of which 19 were waited for; matrix products, arithmetic and copies ran while one was open for 4% of the time, Pallas kernels for 5%

profile of v2, /device:TPU:0, one launch (start us, length us, event | category | flops | bytes accessed | tf_op | source)
XLA Modules:
  0.0 218.1 jit_solution(4603608470422064995)
XLA Ops:
  0.7 1.1 bitcast_multiply_fusion.refs_8_
  1.8 3.2 %collective-permute-start.35 = (bf16[12,128,128]{2,1,0:T(8,128)(2,1)S(1)}, bf16[12,128,128]{2,1,0:T(8,128)(2,1)S(1)}, u32[]{:S(2)}, u32[]{:S(2)}) collective-permute-start(bf16[12,128,128]{2,1,0:T(8,128)(2,1)S(1)} %bitcast_multiply_fusion.refs_8_), channel_id=1, source_target_pairs={{0,96},{8,104},{16,112},{24,120},{32,0},{40,8},{48,16},{56,24},{64... | collective-permute-start | bytes 1179656 | tf_op jit(solution)/shard_map/ppermute | solution.py:46
  4.9 1.1 bitcast_multiply_fusion.1.refs_3_
  6.1 2.8 %collective-permute-start.31 = (bf16[12,128,128]{2,1,0:T(8,128)(2,1)S(1)}, bf16[12,128,128]{2,1,0:T(8,128)(2,1)S(1)}, u32[]{:S(2)}, u32[]{:S(2)}) collective-permute-start(bf16[12,128,128]{2,1,0:T(8,128)(2,1)S(1)} %bitcast_multiply_fusion.1.refs_3_), channel_id=1, source_target_pairs={{0,24},{8,0},{16,8},{24,16},{32,56},{40,32},{48,40},{56,48},{64,88... | collective-permute-start | bytes 1179656 | tf_op jit(solution)/shard_map/ppermute | solution.py:46
  8.9 4.4 %collective-permute-done.35.refs_12_ = bf16[12,128,128]{2,1,0:T(8,128)(2,1)S(1)} collective-permute-done((bf16[12,128,128]{2,1,0:T(8,128)(2,1)S(1)}, bf16[12,128,128]{2,1,0:T(8,128)(2,1)S(1)}, u32[]{:S(2)}, u32[]{:S(2)}) %collective-permute-start.35) | collective-permute-done | bytes 393248 | tf_op jit(solution)/shard_map/ppermute | solution.py:46
  13.3 3.8 %collective-permute-start.36 = (bf16[6,128,128]{2,1,0:T(8,128)(2,1)S(1)}, bf16[6,128,128]{2,1,0:T(8,128)(2,1)S(1)}, u32[]{:S(2)}, u32[]{:S(2)}) collective-permute-start(bf16[6,128,128]{2,1,0:T(8,128)(2,1)S(1)} %slice.247), channel_id=1, source_target_pairs={{0,96},{8,104},{16,112},{24,120},{32,0},{40,8},{48,16},{56,24},{64... | collective-permute-start | bytes 589832 | tf_op jit(solution)/shard_map/ppermute | solution.py:46
  18.0 3.4 %collective-permute-start.32 = (bf16[6,128,128]{2,1,0:T(8,128)(2,1)}, bf16[6,128,128]{2,1,0:T(8,128)(2,1)S(1)}, u32[]{:S(2)}, u32[]{:S(2)}) collective-permute-start(bf16[6,128,128]{2,1,0:T(8,128)(2,1)} %slice.245), channel_id=1, source_target_pairs={{0,24},{8,0},{16,8},{24,16},{32,56},{40,32},{48,40},{56,48},{64,88... | collective-permute-start | bytes 589832 | tf_op jit(solution)/shard_map/ppermute | solution.py:46
  22.2 2.9 %table.3 = (s32[8,192]{1,0:T(8,128)}, s32[1]{0:T(128)}) custom-call(s32[4]{0:T(128)S(1)} %pad_add_fusion.refs_0_.place, s32[16]{0:T(128)S(1)} %bitcast.81, s32[192]{0:T(256)S(1)} %bitcast.91, s32[192]{0:T(256)} %bitcast.93, s32[16]{0:T(128)S(1)} %bitcast.86, s32[192]{0:T(256)} %bitcast.95, s32[192]{0:T(256)} %bitcast.97), custom_call_target="tpu_custom_call" | custom-call | bytes 9000000 | tf_op jit(solution)/shard_map/table/pallas_call | solution.py:190
  25.2 4.1 %collective-permute-done.30.refs_5_ = bf16[6,128,128]{2,1,0:T(8,128)(2,1)S(1)} collective-permute-done((bf16[6,128,128]{2,1,0:T(8,128)(2,1)}, bf16[6,128,128]{2,1,0:T(8,128)(2,1)S(1)}, u32[]{:S(2)}, u32[]{:S(2)}) %collective-permute-start.30) | collective-permute-done | bytes 196640 | tf_op jit(solution)/shard_map/ppermute | solution.py:46
  29.2 2.2 pack.3
  31.5 3.1 %collective-permute-start.38 = (bf16[30,128,128]{2,1,0:T(8,128)(2,1)}, bf16[30,128,128]{2,1,0:T(8,128)(2,1)S(1)}, u32[]{:S(2)}, u32[]{:S(2)}) collective-permute-start(bf16[30,128,128]{2,1,0:T(8,128)(2,1)} %get-tuple-element.152.refs_4_), channel_id=1, source_target_pairs={{0,96},{8,104},{16,112},{24,120},{32,0},{40,8},{48,16},{56,24},{64... | collective-permute-start | bytes 2949128 | tf_op jit(solution)/shard_map/ppermute | solution.py:46
  34.6 2.0 collective-permute-start.39
  36.6 1.4 collective-permute-done.41
  39.3 3.3 %collective-permute-start.42 = (s32[1]{0:T(128)}, s32[1]{0:T(128)}, u32[]{:S(2)}, u32[]{:S(2)}) collective-permute-start(s32[1]{0:T(128)} %max.9), channel_id=1, source_target_pairs={{0,2},{1,3},{2,4},{3,5},{4,6},{5,7},{6,0},{7,1},{8,10},{9,11},{10,... | collective-permute-start | bytes 20 | tf_op jit(solution)/shard_map/ppermute | solution.py:58
  42.5 2.5 %collective-permute-done.42 = s32[1]{0:T(128)} collective-permute-done((s32[1]{0:T(128)}, s32[1]{0:T(128)}, u32[]{:S(2)}, u32[]{:S(2)}) %collective-permute-start.42) | collective-permute-done | bytes 36 | tf_op jit(solution)/shard_map/ppermute | solution.py:58
  45.6 3.2 %collective-permute-start.43 = (s32[1]{0:T(128)}, s32[1]{0:T(128)}, u32[]{:S(2)}, u32[]{:S(2)}) collective-permute-start(s32[1]{0:T(128)} %max.10), channel_id=1, source_target_pairs={{0,4},{1,5},{2,6},{3,7},{4,0},{5,1},{6,2},{7,3},{8,12},{9,13},{10,... | collective-permute-start | bytes 20 | tf_op jit(solution)/shard_map/ppermute | solution.py:58
  48.8 2.0 collective-permute-done.43
  51.4 1.6 collective-permute-done.38.refs_8_
  53.0 3.3 %collective-permute-done.37.refs_5_ = bf16[30,128,128]{2,1,0:T(8,128)(2,1)S(1)} collective-permute-done((bf16[30,128,128]{2,1,0:T(8,128)(2,1)}, bf16[30,128,128]{2,1,0:T(8,128)(2,1)S(1)}, u32[]{:S(2)}, u32[]{:S(2)}) %collective-permute-start.37) | collective-permute-done | bytes 983072 | tf_op jit(solution)/shard_map/ppermute | solution.py:46
  58.1 1.8 collective-permute-start.46
  59.9 2.3 %collective-permute-start.45 = (bf16[15,128,128]{2,1,0:T(8,128)(2,1)S(1)}, bf16[15,128,128]{2,1,0:T(8,128)(2,1)S(1)}, u32[]{:S(2)}, u32[]{:S(2)}) collective-permute-start(bf16[15,128,128]{2,1,0:T(8,128)(2,1)S(1)} %slice.197), channel_id=1, source_target_pairs={{0,96},{8,104},{16,112},{24,120},{32,0},{40,8},{48,16},{56,24},{64... | collective-permute-start | bytes 1474568 | tf_op jit(solution)/shard_map/ppermute | solution.py:46
  62.3 4.5 %collective-permute-done.47.refs_12_ = bf16[15,128,128]{2,1,0:T(8,128)(2,1)S(1)} collective-permute-done((bf16[15,128,128]{2,1,0:T(8,128)(2,1)S(1)}, bf16[15,128,128]{2,1,0:T(8,128)(2,1)S(1)}, u32[]{:S(2)}, u32[]{:S(2)}) %collective-permute-start.47) | collective-permute-done | bytes 491552 | tf_op jit(solution)/shard_map/ppermute | solution.py:46
  66.7 1.7 collective-permute-done.46.refs_11_
  68.8 3.5 %collective-permute-done.44.refs_6_ = bf16[15,128,128]{2,1,0:T(8,128)(2,1)S(1)} collective-permute-done((bf16[15,128,128]{2,1,0:T(8,128)(2,1)S(1)}, bf16[15,128,128]{2,1,0:T(8,128)(2,1)S(1)}, u32[]{:S(2)}, u32[]{:S(2)}) %collective-permute-start.44) | collective-permute-done | bytes 491552 | tf_op jit(solution)/shard_map/ppermute | solution.py:46
  73.1 42.7 %main.3 = (bf16[256,1792]{1,0:T(8,128)(2,1)}, bf16[256,1792]{1,0:T(8,128)(2,1)}, bf16[256,1792]{1,0:T(8,128)(2,1)}, bf16[256,1792]{1,0:T(8,128)(2,1)}, bf16[4,25...) custom-call(s32[4]{0:T(128)S(1)} %pad_add_fusion.refs_0_.place, ...), custom_call_target="tpu_custom_call" | custom-call | bytes 120000000 | tf_op jit(solution)/shard_map/main/pallas_call | solution.py:399
  116.1 1.9 collective-permute-start.49
  118.0 1.8 collective-permute-start.52
  120.1 20.3 %collective-permute-done.48.refs_4_ = bf16[30,128,128]{2,1,0:T(8,128)(2,1)S(1)} collective-permute-done((bf16[30,128,128]{2,1,0:T(8,128)(2,1)}, bf16[30,128,128]{2,1,0:T(8,128)(2,1)S(1)}, u32[]{:S(2)}, u32[]{:S(2)}) %collective-permute-start.48) | collective-permute-done | bytes 983072 | tf_op jit(solution)/shard_map/ppermute | solution.py:46
  140.3 1.5 add_convert_fusion.11
  141.9 1.5 collective-permute-start.50
  144.3 1.9 collective-permute-start.54
  146.7 8.0 %collective-permute-done.50.refs_6_ = bf16[15,128,128]{2,1,0:T(8,128)(2,1)S(1)} collective-permute-done((bf16[15,128,128]{2,1,0:T(8,128)(2,1)S(1)}, bf16[15,128,128]{2,1,0:T(8,128)(2,1)S(1)}, u32[]{:S(2)}, u32[]{:S(2)}) %collective-permute-start.50) | collective-permute-done | bytes 491552 | tf_op jit(solution)/shard_map/ppermute | solution.py:46
  154.7 2.8 %collective-permute-done.51.refs_7_ = bf16[15,128,128]{2,1,0:T(8,128)(2,1)S(1)} collective-permute-done((bf16[15,128,128]{2,1,0:T(8,128)(2,1)S(1)}, bf16[15,128,128]{2,1,0:T(8,128)(2,1)S(1)}, u32[]{:S(2)}, u32[]{:S(2)}) %collective-permute-start.51) | collective-permute-done | bytes 491552 | tf_op jit(solution)/shard_map/ppermute | solution.py:46
  158.3 1.3 collective-permute-done.55.refs_12_
  160.4 5.6 %unpack.3 = (bf16[12,128,128]{2,1,0:T(8,128)(2,1)}, bf16[12,128,128]{2,1,0:T(8,128)(2,1)}, bf16[12,128,128]{2,1,0:T(8,128)(2,1)}, bf16[6,128,128]{2,1,0:T(8,128)...) custom-call(s32[4]{0:T(128)S(1)} %pad_add_fusion.refs_0_.place, ...), custom_call_target="tpu_custom_call" | custom-call | bytes 12000000 | tf_op jit(solution)/shard_map/unpack/pallas_call | solution.py:428
  166.0 1.4 collective-permute-start.56
  167.4 2.0 fusion.13
  169.4 7.7 %collective-permute-start.65 = (bf16[256,1792]{1,0:T(8,128)(2,1)S(1)}, bf16[256,1792]{1,0:T(8,128)(2,1)S(1)}, u32[]{:S(2)}, u32[]{:S(2)}) collective-permute-start(bf16[256,1792]{1,0:T(8,128)(2,1)S(1)} %get-tuple-element.201), channel_id=1, source_target_pairs={{0,6},{1,7},{2,0},{3,1},{4,2},{5,3},{6,4},{7,5},{8,14},{9,15},{10,... | collective-permute-start | bytes 2752520 | tf_op jit(solution)/shard_map/ppermute | solution.py:46
  178.3 2.7 %collective-permute-start.60 = (bf16[12,128,128]{2,1,0:T(8,128)(2,1)S(1)}, bf16[12,128,128]{2,1,0:T(8,128)(2,1)S(1)}, u32[]{:S(2)}, u32[]{:S(2)}) collective-permute-start(bf16[12,128,128]{2,1,0:T(8,128)(2,1)S(1)} %copy-done.80), channel_id=1, source_target_pairs={{0,96},{8,104},{16,112},{24,120},{32,0},{40,8},{48,16},{56,24},{64... | collective-permute-start | bytes 1179656 | tf_op jit(solution)/shard_map/ppermute | solution.py:46
  181.1 6.3 %collective-permute-done.57.refs_2_ = bf16[12,128,128]{2,1,0:T(8,128)(2,1)S(1)} collective-permute-done((bf16[12,128,128]{2,1,0:T(8,128)(2,1)S(1)}, bf16[12,128,128]{2,1,0:T(8,128)(2,1)S(1)}, u32[]{:S(2)}, u32[]{:S(2)}) %collective-permute-start.57) | collective-permute-done | bytes 393248 | tf_op jit(solution)/shard_map/ppermute | solution.py:46
  187.5 2.1 collective-permute-start.59
  189.7 6.2 %collective-permute-done.65 = bf16[256,1792]{1,0:T(8,128)(2,1)S(1)} collective-permute-done((bf16[256,1792]{1,0:T(8,128)(2,1)S(1)}, bf16[256,1792]{1,0:T(8,128)(2,1)S(1)}, u32[]{:S(2)}, u32[]{:S(2)}) %collective-permute-start.65) | collective-permute-done | bytes 917536 | tf_op jit(solution)/shard_map/ppermute | solution.py:46
  195.9 2.1 collective-permute-start.62
  198.6 1.3 fusion.20
  199.9 2.6 %collective-permute-start.66 = (bf16[128,1792]{1,0:T(8,128)(2,1)}, bf16[128,1792]{1,0:T(8,128)(2,1)}, u32[]{:S(2)}, u32[]{:S(2)}) collective-permute-start(bf16[128,1792]{1,0:T(8,128)(2,1)} %get-tuple-element.199), channel_id=1, source_target_pairs={{0,6},{1,7},{2,0},{3,1},{4,2},{5,3},{6,4},{7,5},{8,14},{9,15},{10,... | collective-permute-start | bytes 1376264 | tf_op jit(solution)/shard_map/ppermute | solution.py:46
  203.5 6.9 %collective-permute-done.63.refs_9_ = bf16[6,128,128]{2,1,0:T(8,128)(2,1)} collective-permute-done((bf16[6,128,128]{2,1,0:T(8,128)(2,1)S(1)}, bf16[6,128,128]{2,1,0:T(8,128)(2,1)}, u32[]{:S(2)}, u32[]{:S(2)}) %collective-permute-start.63) | collective-permute-done | bytes 196640 | tf_op jit(solution)/shard_map/ppermute | solution.py:46
  210.4 3.0 %finish.3 = (bf16[12,128,128]{2,1,0:T(8,128)(2,1)}, bf16[12,128,128]{2,1,0:T(8,128)(2,1)}) custom-call(s32[4]{0:T(128)S(1)} %pad_add_fusion.refs_0_.place, s32[16]{0:T(128)S(1)} %bitcast.84, s32[16]{0:T(128)S(1)} %bitcast.89, f32[12]{0:T(128)S(1)} %get-tuple-element.204.up_factor, f32[12]{0:T(128)S(1)} %get-tuple-element.203.down_factor, ...), custom_call_target="tpu_custom_call" | custom-call | bytes 9000000 | tf_op jit(solution)/shard_map/finish/pallas_call | solution.py:432
  213.4 2.2 fusion.23
  (174 shorter events, 13.5 us)
Async XLA Ops:
  0.6 21.6 %copy-start.71 = (s32[1,16]{1,0:T(1,128)S(1)}, s32[1,16]{1,0:T(1,128)}, u32[]{:S(2)}) copy-start(s32[1,16]{1,0:T(1,128)} %param.24) | copy-start | bytes 196
  0.6 21.6 %copy-start.72 = (s32[1,16]{1,0:T(1,128)S(1)}, s32[1,16]{1,0:T(1,128)}, u32[]{:S(2)}) copy-start(s32[1,16]{1,0:T(1,128)} %param.25) | copy-start | bytes 196
  0.7 21.6 %copy-start.73 = (s32[1,192]{1,0:T(1,128)S(1)}, s32[1,192]{1,0:T(1,128)}, u32[]{:S(2)}) copy-start(s32[1,192]{1,0:T(1,128)} %param.20) | copy-start | bytes 2308
  1.8 11.5 %collective-permute-start.35 = (bf16[12,128,128]{2,1,0:T(8,128)(2,1)S(1)}, bf16[12,128,128]{2,1,0:T(8,128)(2,1)S(1)}, u32[]{:S(2)}, u32[]{:S(2)}) collective-permute-start(bf16[12,128,128]{2,1,0:T(8,128)(2,1)S(1)} %bitcast_multiply_fusion.refs_8_), channel_id=1, source_target_pairs={{0,96},{8,104},{16,112},{24,120},{32,0},{40,8},{48,16},{56,24},{64... | collective-permute-start | bytes 1179656 | tf_op jit(solution)/shard_map/ppermute | solution.py:46
  4.9 12.2 %collective-permute-start.33 = (bf16[12,128,128]{2,1,0:T(8,128)(2,1)S(1)}, bf16[12,128,128]{2,1,0:T(8,128)(2,1)S(1)}, u32[]{:S(2)}, u32[]{:S(2)}) collective-permute-start(bf16[12,128,128]{2,1,0:T(8,128)(2,1)S(1)} %bitcast_multiply_fusion.refs_8_), channel_id=1, source_target_pairs={{0,32},{8,40},{16,48},{24,56},{32,64},{40,72},{48,80},{56,88},{64,... | collective-permute-start | bytes 1179656 | tf_op jit(solution)/shard_map/ppermute | solution.py:46
  6.0 25.4 %copy-start.8 = (bf16[12,128,128]{2,1,0:T(8,128)(2,1)}, bf16[12,128,128]{2,1,0:T(8,128)(2,1)S(1)}, u32[]{:S(2)}) copy-start(bf16[12,128,128]{2,1,0:T(8,128)(2,1)S(1)} %bitcast_multiply_fusion.1.refs_3_) | copy-start | bytes 1179652
  6.1 11.2 %collective-permute-start.31 = (bf16[12,128,128]{2,1,0:T(8,128)(2,1)S(1)}, bf16[12,128,128]{2,1,0:T(8,128)(2,1)S(1)}, u32[]{:S(2)}, u32[]{:S(2)}) collective-permute-start(bf16[12,128,128]{2,1,0:T(8,128)(2,1)S(1)} %bitcast_multiply_fusion.1.refs_3_), channel_id=1, source_target_pairs={{0,24},{8,0},{16,8},{24,16},{32,56},{40,32},{48,40},{56,48},{64,88... | collective-permute-start | bytes 1179656 | tf_op jit(solution)/shard_map/ppermute | solution.py:46
  8.9 12.5 %collective-permute-start.29 = (bf16[12,128,128]{2,1,0:T(8,128)(2,1)S(1)}, bf16[12,128,128]{2,1,0:T(8,128)(2,1)S(1)}, u32[]{:S(2)}, u32[]{:S(2)}) collective-permute-start(bf16[12,128,128]{2,1,0:T(8,128)(2,1)S(1)} %bitcast_multiply_fusion.1.refs_3_), channel_id=1, source_target_pairs={{0,8},{8,16},{16,24},{24,0},{32,40},{40,48},{48,56},{56,32},{64,72... | collective-permute-start | bytes 1179656 | tf_op jit(solution)/shard_map/ppermute | solution.py:46
  13.3 11.8 %collective-permute-start.36 = (bf16[6,128,128]{2,1,0:T(8,128)(2,1)S(1)}, bf16[6,128,128]{2,1,0:T(8,128)(2,1)S(1)}, u32[]{:S(2)}, u32[]{:S(2)}) collective-permute-start(bf16[6,128,128]{2,1,0:T(8,128)(2,1)S(1)} %slice.247), channel_id=1, source_target_pairs={{0,96},{8,104},{16,112},{24,120},{32,0},{40,8},{48,16},{56,24},{64... | collective-permute-start | bytes 589832 | tf_op jit(solution)/shard_map/ppermute | solution.py:46
  17.1 8.0 %collective-permute-start.34 = (bf16[6,128,128]{2,1,0:T(8,128)(2,1)S(1)}, bf16[6,128,128]{2,1,0:T(8,128)(2,1)S(1)}, u32[]{:S(2)}, u32[]{:S(2)}) collective-permute-start(bf16[6,128,128]{2,1,0:T(8,128)(2,1)S(1)} %slice.246), channel_id=1, source_target_pairs={{0,32},{8,40},{16,48},{24,56},{32,64},{40,72},{48,80},{56,88},{64,... | collective-permute-start | bytes 589832 | tf_op jit(solution)/shard_map/ppermute | solution.py:46
  18.0 7.2 %collective-permute-start.32 = (bf16[6,128,128]{2,1,0:T(8,128)(2,1)}, bf16[6,128,128]{2,1,0:T(8,128)(2,1)S(1)}, u32[]{:S(2)}, u32[]{:S(2)}) collective-permute-start(bf16[6,128,128]{2,1,0:T(8,128)(2,1)} %slice.245), channel_id=1, source_target_pairs={{0,24},{8,0},{16,8},{24,16},{32,56},{40,32},{48,40},{56,48},{64,88... | collective-permute-start | bytes 589832 | tf_op jit(solution)/shard_map/ppermute | solution.py:46
  22.2 7.1 %collective-permute-start.30 = (bf16[6,128,128]{2,1,0:T(8,128)(2,1)}, bf16[6,128,128]{2,1,0:T(8,128)(2,1)S(1)}, u32[]{:S(2)}, u32[]{:S(2)}) collective-permute-start(bf16[6,128,128]{2,1,0:T(8,128)(2,1)} %slice.244), channel_id=1, source_target_pairs={{0,8},{8,16},{16,24},{24,0},{32,40},{40,48},{48,56},{56,32},{64,72... | collective-permute-start | bytes 589832 | tf_op jit(solution)/shard_map/ppermute | solution.py:46
  31.5 21.5 %collective-permute-start.38 = (bf16[30,128,128]{2,1,0:T(8,128)(2,1)}, bf16[30,128,128]{2,1,0:T(8,128)(2,1)S(1)}, u32[]{:S(2)}, u32[]{:S(2)}) collective-permute-start(bf16[30,128,128]{2,1,0:T(8,128)(2,1)} %get-tuple-element.152.refs_4_), channel_id=1, source_target_pairs={{0,96},{8,104},{16,112},{24,120},{32,0},{40,8},{48,16},{56,24},{64... | collective-permute-start | bytes 2949128 | tf_op jit(solution)/shard_map/ppermute | solution.py:46
  34.6 21.7 %collective-permute-start.37 = (bf16[30,128,128]{2,1,0:T(8,128)(2,1)}, bf16[30,128,128]{2,1,0:T(8,128)(2,1)S(1)}, u32[]{:S(2)}, u32[]{:S(2)}) collective-permute-start(bf16[30,128,128]{2,1,0:T(8,128)(2,1)} %get-tuple-element.152.refs_4_), channel_id=1, source_target_pairs={{0,32},{8,40},{16,48},{24,56},{32,64},{40,72},{48,80},{56,88},{64,... | collective-permute-start | bytes 2949128 | tf_op jit(solution)/shard_map/ppermute | solution.py:46
  34.6 21.7 %collective-permute-start.40 = (bf16[30,128,128]{2,1,0:T(8,128)(2,1)}, bf16[30,128,128]{2,1,0:T(8,128)(2,1)S(1)}, u32[]{:S(2)}, u32[]{:S(2)}) collective-permute-start(bf16[30,128,128]{2,1,0:T(8,128)(2,1)} %get-tuple-element.153.refs_9_), channel_id=1, source_target_pairs={{0,24},{8,0},{16,8},{24,16},{32,56},{40,32},{48,40},{56,48},{64,88... | collective-permute-start | bytes 2949128 | tf_op jit(solution)/shard_map/ppermute | solution.py:46
  34.6 21.7 %collective-permute-start.39 = (bf16[30,128,128]{2,1,0:T(8,128)(2,1)}, bf16[30,128,128]{2,1,0:T(8,128)(2,1)S(1)}, u32[]{:S(2)}, u32[]{:S(2)}) collective-permute-start(bf16[30,128,128]{2,1,0:T(8,128)(2,1)} %get-tuple-element.153.refs_9_), channel_id=1, source_target_pairs={{0,8},{8,16},{16,24},{24,0},{32,40},{40,48},{48,56},{56,32},{64,72... | collective-permute-start | bytes 2949128 | tf_op jit(solution)/shard_map/ppermute | solution.py:46
  36.6 1.4 collective-permute-start.41
  39.3 5.7 %collective-permute-start.42 = (s32[1]{0:T(128)}, s32[1]{0:T(128)}, u32[]{:S(2)}, u32[]{:S(2)}) collective-permute-start(s32[1]{0:T(128)} %max.9), channel_id=1, source_target_pairs={{0,2},{1,3},{2,4},{3,5},{4,6},{5,7},{6,0},{7,1},{8,10},{9,11},{10,... | collective-permute-start | bytes 20 | tf_op jit(solution)/shard_map/ppermute | solution.py:58
  45.6 5.2 %collective-permute-start.43 = (s32[1]{0:T(128)}, s32[1]{0:T(128)}, u32[]{:S(2)}, u32[]{:S(2)}) collective-permute-start(s32[1]{0:T(128)} %max.10), channel_id=1, source_target_pairs={{0,4},{1,5},{2,6},{3,7},{4,0},{5,1},{6,2},{7,3},{8,12},{9,13},{10,... | collective-permute-start | bytes 20 | tf_op jit(solution)/shard_map/ppermute | solution.py:58
  57.9 8.8 %collective-permute-start.47 = (bf16[15,128,128]{2,1,0:T(8,128)(2,1)S(1)}, bf16[15,128,128]{2,1,0:T(8,128)(2,1)S(1)}, u32[]{:S(2)}, u32[]{:S(2)}) collective-permute-start(bf16[15,128,128]{2,1,0:T(8,128)(2,1)S(1)} %slice.199), channel_id=1, source_target_pairs={{0,24},{8,0},{16,8},{24,16},{32,56},{40,32},{48,40},{56,48},{64,88... | collective-permute-start | bytes 1474568 | tf_op jit(solution)/shard_map/ppermute | solution.py:46
  58.1 10.3 %collective-permute-start.46 = (bf16[15,128,128]{2,1,0:T(8,128)(2,1)S(1)}, bf16[15,128,128]{2,1,0:T(8,128)(2,1)S(1)}, u32[]{:S(2)}, u32[]{:S(2)}) collective-permute-start(bf16[15,128,128]{2,1,0:T(8,128)(2,1)S(1)} %slice.198), channel_id=1, source_target_pairs={{0,8},{8,16},{16,24},{24,0},{32,40},{40,48},{48,56},{56,32},{64,72... | collective-permute-start | bytes 1474568 | tf_op jit(solution)/shard_map/ppermute | solution.py:46
  59.9 8.8 %collective-permute-start.45 = (bf16[15,128,128]{2,1,0:T(8,128)(2,1)S(1)}, bf16[15,128,128]{2,1,0:T(8,128)(2,1)S(1)}, u32[]{:S(2)}, u32[]{:S(2)}) collective-permute-start(bf16[15,128,128]{2,1,0:T(8,128)(2,1)S(1)} %slice.197), channel_id=1, source_target_pairs={{0,96},{8,104},{16,112},{24,120},{32,0},{40,8},{48,16},{56,24},{64... | collective-permute-start | bytes 1474568 | tf_op jit(solution)/shard_map/ppermute | solution.py:46
  62.2 10.0 %collective-permute-start.44 = (bf16[15,128,128]{2,1,0:T(8,128)(2,1)S(1)}, bf16[15,128,128]{2,1,0:T(8,128)(2,1)S(1)}, u32[]{:S(2)}, u32[]{:S(2)}) collective-permute-start(bf16[15,128,128]{2,1,0:T(8,128)(2,1)S(1)} %slice.196), channel_id=1, source_target_pairs={{0,32},{8,40},{16,48},{24,56},{32,64},{40,72},{48,80},{56,88},{64,... | collective-permute-start | bytes 1474568 | tf_op jit(solution)/shard_map/ppermute | solution.py:46
  115.8 27.6 %copy-start.55 = (bf16[15,128,128]{2,1,0:T(8,128)(2,1)S(1)}, bf16[15,128,128]{2,1,0:T(8,128)(2,1)}, u32[]{:S(2)}) copy-start(bf16[15,128,128]{2,1,0:T(8,128)(2,1)} %get-tuple-element.165) | copy-start | bytes 1474564
  115.8 28.3 %copy-start.53 = (bf16[15,128,128]{2,1,0:T(8,128)(2,1)S(1)}, bf16[15,128,128]{2,1,0:T(8,128)(2,1)}, u32[]{:S(2)}) copy-start(bf16[15,128,128]{2,1,0:T(8,128)(2,1)} %get-tuple-element.169) | copy-start | bytes 1474564
  115.9 51.5 %collective-permute-start.64 = (bf16[4,256,1792]{2,1,0:T(8,128)(2,1)}, bf16[4,256,1792]{2,1,0:T(8,128)(2,1)S(1)}, u32[]{:S(2)}, u32[]{:S(2)}) collective-permute-start(bf16[4,256,1792]{2,1,0:T(8,128)(2,1)} %get-tuple-element.184), channel_id=1, source_target_pairs={{0,1},{1,0},{2,3},{3,2},{4,5},{5,4},{6,7},{7,6},{8,9},{9,8},{10,11... | collective-permute-start | bytes 11010056 | tf_op jit(solution)/shard_map/ppermute | solution.py:412
  115.9 24.4 %collective-permute-start.48 = (bf16[30,128,128]{2,1,0:T(8,128)(2,1)}, bf16[30,128,128]{2,1,0:T(8,128)(2,1)S(1)}, u32[]{:S(2)}, u32[]{:S(2)}) collective-permute-start(bf16[30,128,128]{2,1,0:T(8,128)(2,1)} %get-tuple-element.162), channel_id=1, source_target_pairs={{0,96},{8,104},{16,112},{24,120},{32,0},{40,8},{48,16},{56,24},{64... | collective-permute-start | bytes 2949128 | tf_op jit(solution)/shard_map/ppermute | solution.py:46
  116.1 27.3 %collective-permute-start.49 = (bf16[30,128,128]{2,1,0:T(8,128)(2,1)}, bf16[30,128,128]{2,1,0:T(8,128)(2,1)S(1)}, u32[]{:S(2)}, u32[]{:S(2)}) collective-permute-start(bf16[30,128,128]{2,1,0:T(8,128)(2,1)} %get-tuple-element.163), channel_id=1, source_target_pairs={{0,32},{8,40},{16,48},{24,56},{32,64},{40,72},{48,80},{56,88},{64,... | collective-permute-start | bytes 2949128 | tf_op jit(solution)/shard_map/ppermute | solution.py:46
  118.0 26.1 %collective-permute-start.52 = (bf16[30,128,128]{2,1,0:T(8,128)(2,1)}, bf16[30,128,128]{2,1,0:T(8,128)(2,1)S(1)}, u32[]{:S(2)}, u32[]{:S(2)}) collective-permute-start(bf16[30,128,128]{2,1,0:T(8,128)(2,1)} %get-tuple-element.167), channel_id=1, source_target_pairs={{0,24},{8,0},{16,8},{24,16},{32,56},{40,32},{48,40},{56,48},{64,88... | collective-permute-start | bytes 2949128 | tf_op jit(solution)/shard_map/ppermute | solution.py:46
  119.8 26.4 %collective-permute-start.53 = (bf16[30,128,128]{2,1,0:T(8,128)(2,1)}, bf16[30,128,128]{2,1,0:T(8,128)(2,1)S(1)}, u32[]{:S(2)}, u32[]{:S(2)}) collective-permute-start(bf16[30,128,128]{2,1,0:T(8,128)(2,1)} %get-tuple-element.168), channel_id=1, source_target_pairs={{0,8},{8,16},{16,24},{24,0},{32,40},{40,48},{48,56},{56,32},{64,72... | collective-permute-start | bytes 2949128 | tf_op jit(solution)/shard_map/ppermute | solution.py:46
  141.9 12.8 %collective-permute-start.50 = (bf16[15,128,128]{2,1,0:T(8,128)(2,1)S(1)}, bf16[15,128,128]{2,1,0:T(8,128)(2,1)S(1)}, u32[]{:S(2)}, u32[]{:S(2)}) collective-permute-start(bf16[15,128,128]{2,1,0:T(8,128)(2,1)S(1)} %add_convert_fusion.11), channel_id=1, source_target_pairs={{0,96},{8,104},{16,112},{24,120},{32,0},{40,8},{48,16},{56,24},{64... | collective-permute-start | bytes 1474568 | tf_op jit(solution)/shard_map/ppermute | solution.py:46
  143.6 13.9 %collective-permute-start.51 = (bf16[15,128,128]{2,1,0:T(8,128)(2,1)S(1)}, bf16[15,128,128]{2,1,0:T(8,128)(2,1)S(1)}, u32[]{:S(2)}, u32[]{:S(2)}) collective-permute-start(bf16[15,128,128]{2,1,0:T(8,128)(2,1)S(1)} %add_convert_fusion.10), channel_id=1, source_target_pairs={{0,32},{8,40},{16,48},{24,56},{32,64},{40,72},{48,80},{56,88},{64,... | collective-permute-start | bytes 1474568 | tf_op jit(solution)/shard_map/ppermute | solution.py:46
  144.3 13.2 %collective-permute-start.54 = (bf16[15,128,128]{2,1,0:T(8,128)(2,1)S(1)}, bf16[15,128,128]{2,1,0:T(8,128)(2,1)S(1)}, u32[]{:S(2)}, u32[]{:S(2)}) collective-permute-start(bf16[15,128,128]{2,1,0:T(8,128)(2,1)S(1)} %add_convert_fusion.9), channel_id=1, source_target_pairs={{0,24},{8,0},{16,8},{24,16},{32,56},{40,32},{48,40},{56,48},{64,88... | collective-permute-start | bytes 1474568 | tf_op jit(solution)/shard_map/ppermute | solution.py:46
  146.4 13.2 %collective-permute-start.55 = (bf16[15,128,128]{2,1,0:T(8,128)(2,1)S(1)}, bf16[15,128,128]{2,1,0:T(8,128)(2,1)S(1)}, u32[]{:S(2)}, u32[]{:S(2)}) collective-permute-start(bf16[15,128,128]{2,1,0:T(8,128)(2,1)S(1)} %add_convert_fusion.8), channel_id=1, source_target_pairs={{0,8},{8,16},{16,24},{24,0},{32,40},{40,48},{48,56},{56,32},{64,72... | collective-permute-start | bytes 1474568 | tf_op jit(solution)/shard_map/ppermute | solution.py:46
  166.0 15.0 %collective-permute-start.56 = (bf16[12,128,128]{2,1,0:T(8,128)(2,1)}, bf16[12,128,128]{2,1,0:T(8,128)(2,1)S(1)}, u32[]{:S(2)}, u32[]{:S(2)}) collective-permute-start(bf16[12,128,128]{2,1,0:T(8,128)(2,1)} %get-tuple-element.172), channel_id=1, source_target_pairs={{0,24},{8,0},{16,8},{24,16},{32,56},{40,32},{48,40},{56,48},{64,88... | collective-permute-start | bytes 1179656 | tf_op jit(solution)/shard_map/ppermute | solution.py:46
  167.4 22.2 %copy-start.68 = (bf16[6,128,128]{2,1,0:T(8,128)(2,1)S(1)}, bf16[6,128,128]{2,1,0:T(8,128)(2,1)}, u32[]{:S(2)}) copy-start(bf16[6,128,128]{2,1,0:T(8,128)(2,1)} %get-tuple-element.179) | copy-start | bytes 589828
  169.4 29.1 %copy-start.27 = (bf16[256,1792]{1,0:T(8,128)(2,1)S(1)}, bf16[256,1792]{1,0:T(8,128)(2,1)}, u32[]{:S(2)}) copy-start(bf16[256,1792]{1,0:T(8,128)(2,1)} %get-tuple-element.185) | copy-start | bytes 2752516
  169.4 26.5 %collective-permute-start.65 = (bf16[256,1792]{1,0:T(8,128)(2,1)S(1)}, bf16[256,1792]{1,0:T(8,128)(2,1)S(1)}, u32[]{:S(2)}, u32[]{:S(2)}) collective-permute-start(bf16[256,1792]{1,0:T(8,128)(2,1)S(1)} %get-tuple-element.201), channel_id=1, source_target_pairs={{0,6},{1,7},{2,0},{3,1},{4,2},{5,3},{6,4},{7,5},{8,14},{9,15},{10,... | collective-permute-start | bytes 2752520 | tf_op jit(solution)/shard_map/ppermute | solution.py:46
  177.1 21.4 %collective-permute-start.67 = (bf16[256,1792]{1,0:T(8,128)(2,1)S(1)}, bf16[256,1792]{1,0:T(8,128)(2,1)S(1)}, u32[]{:S(2)}, u32[]{:S(2)}) collective-permute-start(bf16[256,1792]{1,0:T(8,128)(2,1)S(1)} %get-tuple-element.202), channel_id=1, source_target_pairs={{0,2},{1,3},{2,4},{3,5},{4,6},{5,7},{6,0},{7,1},{8,10},{9,11},{10,... | collective-permute-start | bytes 2752520 | tf_op jit(solution)/shard_map/ppermute | solution.py:46
  177.6 9.9 %collective-permute-start.57 = (bf16[12,128,128]{2,1,0:T(8,128)(2,1)S(1)}, bf16[12,128,128]{2,1,0:T(8,128)(2,1)S(1)}, u32[]{:S(2)}, u32[]{:S(2)}) collective-permute-start(bf16[12,128,128]{2,1,0:T(8,128)(2,1)S(1)} %copy-done.81), channel_id=1, source_target_pairs={{0,8},{8,16},{16,24},{24,0},{32,40},{40,48},{48,56},{56,32},{64,72... | collective-permute-start | bytes 1179656 | tf_op jit(solution)/shard_map/ppermute | solution.py:46
  178.3 9.2 %collective-permute-start.60 = (bf16[12,128,128]{2,1,0:T(8,128)(2,1)S(1)}, bf16[12,128,128]{2,1,0:T(8,128)(2,1)S(1)}, u32[]{:S(2)}, u32[]{:S(2)}) collective-permute-start(bf16[12,128,128]{2,1,0:T(8,128)(2,1)S(1)} %copy-done.80), channel_id=1, source_target_pairs={{0,96},{8,104},{16,112},{24,120},{32,0},{40,8},{48,16},{56,24},{64... | collective-permute-start | bytes 1179656 | tf_op jit(solution)/shard_map/ppermute | solution.py:46
  181.0 21.5 %collective-permute-start.61 = (bf16[12,128,128]{2,1,0:T(8,128)(2,1)S(1)}, bf16[12,128,128]{2,1,0:T(8,128)(2,1)S(1)}, u32[]{:S(2)}, u32[]{:S(2)}) collective-permute-start(bf16[12,128,128]{2,1,0:T(8,128)(2,1)S(1)} %copy-done.79), channel_id=1, source_target_pairs={{0,32},{8,40},{16,48},{24,56},{32,64},{40,72},{48,80},{56,88},{64,... | collective-permute-start | bytes 1179656 | tf_op jit(solution)/shard_map/ppermute | solution.py:46
  187.4 15.9 %collective-permute-start.58 = (bf16[6,128,128]{2,1,0:T(8,128)(2,1)S(1)}, bf16[6,128,128]{2,1,0:T(8,128)(2,1)}, u32[]{:S(2)}, u32[]{:S(2)}) collective-permute-start(bf16[6,128,128]{2,1,0:T(8,128)(2,1)S(1)} %add_convert_fusion.15), channel_id=1, source_target_pairs={{0,24},{8,0},{16,8},{24,16},{32,56},{40,32},{48,40},{56,48},{64,88... | collective-permute-start | bytes 589832 | tf_op jit(solution)/shard_map/ppermute | solution.py:46
  187.5 15.9 %collective-permute-start.59 = (bf16[6,128,128]{2,1,0:T(8,128)(2,1)S(1)}, bf16[6,128,128]{2,1,0:T(8,128)(2,1)}, u32[]{:S(2)}, u32[]{:S(2)}) collective-permute-start(bf16[6,128,128]{2,1,0:T(8,128)(2,1)S(1)} %add_convert_fusion.14), channel_id=1, source_target_pairs={{0,8},{8,16},{16,24},{24,0},{32,40},{40,48},{48,56},{56,32},{64,72... | collective-permute-start | bytes 589832 | tf_op jit(solution)/shard_map/ppermute | solution.py:46
  195.9 7.6 %collective-permute-start.62 = (bf16[6,128,128]{2,1,0:T(8,128)(2,1)S(1)}, bf16[6,128,128]{2,1,0:T(8,128)(2,1)}, u32[]{:S(2)}, u32[]{:S(2)}) collective-permute-start(bf16[6,128,128]{2,1,0:T(8,128)(2,1)S(1)} %add_convert_fusion.13), channel_id=1, source_target_pairs={{0,96},{8,104},{16,112},{24,120},{32,0},{40,8},{48,16},{56,24},{64... | collective-permute-start | bytes 589832 | tf_op jit(solution)/shard_map/ppermute | solution.py:46
  199.9 13.5 %collective-permute-start.66 = (bf16[128,1792]{1,0:T(8,128)(2,1)}, bf16[128,1792]{1,0:T(8,128)(2,1)}, u32[]{:S(2)}, u32[]{:S(2)}) collective-permute-start(bf16[128,1792]{1,0:T(8,128)(2,1)} %get-tuple-element.199), channel_id=1, source_target_pairs={{0,6},{1,7},{2,0},{3,1},{4,2},{5,3},{6,4},{7,5},{8,14},{9,15},{10,... | collective-permute-start | bytes 1376264 | tf_op jit(solution)/shard_map/ppermute | solution.py:46
  202.5 10.9 %collective-permute-start.68 = (bf16[128,1792]{1,0:T(8,128)(2,1)}, bf16[128,1792]{1,0:T(8,128)(2,1)}, u32[]{:S(2)}, u32[]{:S(2)}) collective-permute-start(bf16[128,1792]{1,0:T(8,128)(2,1)} %get-tuple-element.200), channel_id=1, source_target_pairs={{0,2},{1,3},{2,4},{3,5},{4,6},{5,7},{6,0},{7,1},{8,10},{9,11},{10,... | collective-permute-start | bytes 1376264 | tf_op jit(solution)/shard_map/ppermute | solution.py:46
  203.3 7.1 %collective-permute-start.63 = (bf16[6,128,128]{2,1,0:T(8,128)(2,1)S(1)}, bf16[6,128,128]{2,1,0:T(8,128)(2,1)}, u32[]{:S(2)}, u32[]{:S(2)}) collective-permute-start(bf16[6,128,128]{2,1,0:T(8,128)(2,1)S(1)} %add_convert_fusion.12), channel_id=1, source_target_pairs={{0,32},{8,40},{16,48},{24,56},{32,64},{40,72},{48,80},{56,88},{64,... | collective-permute-start | bytes 589832 | tf_op jit(solution)/shard_map/ppermute | solution.py:46
  (48 other events, 270.3 us)

commit v3 on v2

--- a/solution.py
+++ b/solution.py
@@ -13,12 +13,10 @@
 
 
 def gelu_parts(hidden):
-    tangent = jnp.tanh(ROOT_TWO_PI * (hidden + CUBIC * hidden * hidden * hidden))
-    gelu_value = 0.5 * hidden * (1.0 + tangent)
-    gelu_slope = 0.5 * (1.0 + tangent) + 0.5 * hidden * (1.0 - tangent * tangent) * ROOT_TWO_PI * (
-        1.0 + 3.0 * CUBIC * hidden * hidden
-    )
-    return (gelu_value, gelu_slope)
+    square = hidden * hidden
+    part = 0.5 + 0.5 * jnp.tanh(hidden * (ROOT_TWO_PI + (ROOT_TWO_PI * CUBIC) * square))
+    twice = hidden * (2.0 * ROOT_TWO_PI + (6.0 * ROOT_TWO_PI * CUBIC) * square)
+    return hidden * part, part + part * (1.0 - part) * twice
 
 
 SIDE = 4
@@ -26,7 +24,6 @@
 BLK = 128
 ROOM = 30
 LIST = 192
-VMEM_LIMIT = 60 * 1024 * 1024
 V, S, A = pltpu.VMEM, pltpu.SMEM, pl.ANY
 
 
@@ -62,11 +59,13 @@
     return jnp.maximum(flag, moved([(t, (t + 4) % 8) for t in range(8)]))
 
 
-def spread(rings, flag=None):
+def spread(rings, flag=None, held=None):
     half = rings[0][0].shape[0] // 2
     first = [(move(own, 1), move(own, 3)) for own, move in rings]
     if flag is not None:
         first, flag = lax.optimization_barrier((first, any_tensor(flag)))
+    if held is not None:
+        first, held = lax.optimization_barrier((first, held))
     second = [
         (move(one[:half], 1), move(three[half:], 3))
         for (own, move), (one, three) in zip(rings, first)
@@ -75,7 +74,7 @@
         (own, one, low, high, three)
         for (own, move), (one, three), (low, high) in zip(rings, first, second)
     ]
-    return spreads if flag is None else (spreads, flag)
+    return spreads if flag is None and held is None else (spreads, flag if held is None else held)
 
 
 def add(*arrays):
@@ -104,14 +103,14 @@
     return pl.CostEstimate(flops=0, bytes_accessed=int(us * 3e6), transcendentals=0)
 
 
-def call(kernel, outs, in_spaces, out_spaces, scratch, name, us):
+def call(kernel, outs, in_spaces, out_spaces, scratch, name, us, limit=38):
     return pl.pallas_call(
         kernel,
         out_shape=outs,
         in_specs=[pl.BlockSpec(memory_space=s) for s in in_spaces],
         out_specs=[pl.BlockSpec(memory_space=s) for s in out_spaces],
         scratch_shapes=scratch,
-        compiler_params=pltpu.CompilerParams(vmem_limit_bytes=VMEM_LIMIT),
+        compiler_params=pltpu.CompilerParams(vmem_limit_bytes=limit * 1024 * 1024),
         cost_estimate=cost(us),
         name=name,
     )
@@ -182,13 +181,13 @@
     most[0] = largest
 
 
-def make_table(room, place, up_count, up_row, up_col, down_count, down_row, down_col):
+def make_table(room, place, up_count, up_row, up_col, down_count, down_row, down_col, held=()):
     def kernel(*refs):
-        table_kernel(room, *refs)
+        table_kernel(room, *refs[:7], *refs[7 + len(held):])
 
     outs = [jax.ShapeDtypeStruct((8, LIST), jnp.int32), jax.ShapeDtypeStruct((1,), jnp.int32)]
-    return call(kernel, outs, [S] * 7, [S] * 2, [], "table", 3)(
-        place, up_count, up_row, up_col, down_count, down_row, down_col
+    return call(kernel, outs, [S] * 7 + [V] * len(held), [S] * 2, [], "table", 3)(
+        place, up_count, up_row, up_col, down_count, down_row, down_col, *held
     )
 
 
@@ -196,24 +195,34 @@
     return pl.ds(pl.multiple_of(index * BLK, BLK), BLK)
 
 
+def in_groups(groups, run):
+    def twelve(i, unused):
+        run(i * 12, 12)
+        return unused
+
+    def four(i, unused):
+        run(i * 4, 4)
+        return unused
+
+    lax.fori_loop(0, groups // 3, twelve, 0)
+    lax.fori_loop(groups // 3 * 3, groups, four, 0)
+
+
 def block_products(table, first, take, give, left, tiles, out, contract, offset=0):
-    def step(i, unused):
-        products = []
-        for u in range(4):
-            at = i * 4 + u
-            products.append(
-                lax.dot_general(
-                    left[:, lane(table[take, at])],
-                    tiles[table[first, at]],
-                    (((1,), (contract,)), ((), ())),
-                    preferred_element_type=jnp.float32,
-                )
+    def run(start, count):
+        products = [
+            lax.dot_general(
+                left[:, lane(table[take, start + u])],
+                tiles[table[first, start + u]],
+                (((1,), (contract,)), ((), ())),
+                preferred_element_type=jnp.float32,
             )
-        for u in range(4):
-            out[:, lane(table[give, i * 4 + u] + offset)] += products[u]
-        return unused
-
-    lax.fori_loop(0, table[6, first], step, 0)
+            for u in range(count)
+        ]
+        for u in range(count):
+            out[:, lane(table[give, start + u] + offset)] += products[u]
+
+    in_groups(table[6, first], run)
 
 
 def fetch_tiles(room, sources, target, sems):
@@ -225,11 +234,6 @@
         copy.start()
     target[SIDE * room] = jnp.zeros((BLK, BLK), jnp.bfloat16)
     return copies
-
-
-SUM_PARTS = (
-    (0, 0, 0, 0), (0, 1, 0, 1), (1, 0, 2, 0), (1, 1, 1, 1), (2, 0, 2, 1), (2, 1, 3, 0), (3, 0, 1, 0), (3, 1, 3, 1),
-)
 
 
 def term_parts(room):
@@ -245,31 +249,27 @@
     )
 
 
-def main_kernel(room, place, table, acts_in, grads_in, *refs):
+def main_kernel(room, place, table, acts, grads, *refs):
     ups, downs = refs[:5], refs[5:10]
-    keep_outs, send_out, up_outs, down_outs = refs[10:14], refs[14], refs[15:20], refs[20:25]
-    acts, grads, up_tiles, down_tiles, sums, activated, hidden_grad, shares, sems = refs[25:]
-    load_acts = pltpu.make_async_copy(acts_in, acts, sems.at[2, 0])
-    load_grads = pltpu.make_async_copy(grads_in, grads, sems.at[2, 1])
+    partial_out, up_outs, down_outs = refs[10], refs[11:16], refs[16:21]
+    up_tiles, down_tiles, sums, activated, hidden_grad, shares, sems = refs[21:]
     up_copies = fetch_tiles(room, ups, up_tiles, sems.at[0])
-    load_acts.start()
     down_copies = fetch_tiles(room, downs, down_tiles, sems.at[1])
-    load_grads.start()
     sums[...] = jnp.zeros_like(sums)
     for copy in up_copies:
         copy.wait()
-    load_acts.wait()
     columns = activated.shape[1] // BLK
     block_products(table, 0, 1, 2, acts, up_tiles, sums, 0)
     for copy in down_copies:
         copy.wait()
-    load_grads.wait()
     block_products(table, 3, 5, 4, grads, down_tiles, sums, 1, columns)
 
     def bend(i, unused):
-        value, slope = gelu_parts(sums[:, lane(i)])
-        activated[:, lane(i)] = value.astype(jnp.bfloat16)
-        hidden_grad[:, lane(i)] = (sums[:, lane(i + columns)] * slope).astype(jnp.bfloat16)
+        for row in range(0, sums.shape[0], 64):
+            rows = slice(row, row + 64)
+            value, slope = gelu_parts(sums[rows, lane(i)])
+            activated[rows, lane(i)] = value.astype(jnp.bfloat16)
+            hidden_grad[rows, lane(i)] = (sums[rows, lane(i + columns)] * slope).astype(jnp.bfloat16)
         zero = jnp.zeros((sums.shape[0], BLK), jnp.float32)
         sums[:, lane(i)] = zero
         sums[:, lane(i + columns)] = zero
@@ -277,44 +277,30 @@
 
     lax.fori_loop(0, columns, bend, 0)
     block_products(table, 0, 2, 1, hidden_grad, up_tiles, sums, 1)
-    share = shares.shape[2] // BLK
-    rows = shares.shape[1] // 2
-    copies = []
-    for first, core in ((SIDE, 1 - place[3]), (0, place[3])):
-        for buffer, part, far, tokens in SUM_PARTS:
-            base = (back(place[2], far) * 2 + core) * share
-
-            def round_one(i, unused, base=base, at=first + buffer, part=part, tokens=tokens):
-                shares[at, part * rows:(part + 1) * rows, lane(i)] = sums[
-                    tokens * rows:(tokens + 1) * rows, lane(base + i)
-                ].astype(jnp.bfloat16)
-                return unused
-
-            lax.fori_loop(0, share, round_one, 0)
-        if first:
-            copies.append(pltpu.make_async_copy(shares.at[pl.ds(SIDE, SIDE)], send_out, sems.at[2, 2]))
-            copies[-1].start()
-        else:
-            for i in range(SIDE):
-                copies.append(pltpu.make_async_copy(shares.at[i], keep_outs[i], sems.at[2, 3 + i]))
-                copies[-1].start()
+    def round_two(i, unused):
+        at = pl.ds(pl.multiple_of(i * 2 * BLK, BLK), 2 * BLK)
+        shares[:, at] = sums[:, at].astype(jnp.bfloat16)
+        return unused
+
+    lax.fori_loop(0, columns, round_two, 0)
+    copies = [pltpu.make_async_copy(shares, partial_out, sems.at[2, 2])]
+    copies[0].start()
     for which, (left, right, terms, outs) in enumerate(
         ((acts, hidden_grad, up_tiles, up_outs), (activated, grads, down_tiles, down_outs))
     ):
         first = which * 3
 
-        def body(i, unused, first=first, left=left, right=right, terms=terms):
-            for u in range(4):
-                at = i * 4 + u
+        def run(start, count, first=first, left=left, right=right, terms=terms):
+            for at in range(count):
+                at = start + at
                 terms[table[first, at]] = lax.dot_general(
                     left[:, lane(table[first + 1, at])],
                     right[:, lane(table[first + 2, at])],
                     (((0,), (0,)), ((), ())),
                     preferred_element_type=jnp.float32,
                 ).astype(jnp.bfloat16)
-            return unused
-
-        lax.fori_loop(0, table[6, first], body, 0)
+
+        in_groups(table[6, first], run)
         for i, (out, to, start, size) in enumerate(term_parts(room)):
             copies.append(
                 pltpu.make_async_copy(
@@ -386,7 +372,6 @@
 def layer(room, place, table, far_up, far_down, activations, output_grad, up_factor, down_factor, up_count, down_count):
     tokens, width = activations.shape
     hidden_width = FF // lax.axis_size("tensor")
-    share = width // (2 * SIDE)
     tiles = pltpu.VMEM((SIDE * room + 1, BLK, BLK), jnp.bfloat16)
     parts = [blocks(room)] * 3 + [blocks(room // 2)] * 2
 
@@ -396,33 +381,19 @@
     def unpack(*refs):
         unpack_kernel(room, *refs)
 
-    *keeps, send, up0, up1, up2, up3, up4, down0, down1, down2, down3, down4 = call(
+    partial, up0, up1, up2, up3, up4, down0, down1, down2, down3, down4 = call(
         main,
-        [jax.ShapeDtypeStruct((tokens, share), jnp.bfloat16)] * SIDE
-        + [jax.ShapeDtypeStruct((SIDE, tokens, share), jnp.bfloat16)]
-        + parts * 2,
-        [S, S] + [A] * 12,
-        [A] * 15,
-        [pltpu.VMEM((tokens, width), jnp.bfloat16)] * 2
-        + [tiles, tiles, pltpu.VMEM((tokens, 2 * hidden_width), jnp.float32)]
+        [jax.ShapeDtypeStruct((tokens, width), jnp.bfloat16)] + parts * 2,
+        [S, S, V, V] + [A] * 10,
+        [A] * 11,
+        [tiles, tiles, pltpu.VMEM((tokens, 2 * hidden_width), jnp.float32)]
         + [pltpu.VMEM((tokens, hidden_width), jnp.bfloat16)] * 2
-        + [pltpu.VMEM((2 * SIDE, tokens, share), jnp.bfloat16), pltpu.SemaphoreType.DMA((3, 8))],
-        "main", 40,
+        + [pltpu.VMEM((tokens, width), jnp.bfloat16), pltpu.SemaphoreType.DMA((3, 8))],
+        "main", 40, 38 if room == ROOM else 60,
     )(place, table, activations, output_grad, *far_up, *far_down)
-    other = lax.ppermute(send, "tensor", [(t, t ^ 1) for t in range(2 * SIDE)])
+    input_grad = lax.psum_scatter(partial, "tensor", scatter_dimension=1, tiled=True)
     far_up_terms, far_down_terms = collect(
         [(up0, up1, up2, up3, up4, over_y), (down0, down1, down2, down3, down4, over_x)]
-    )
-    rows = tokens // 2
-    from_fore = over_z(add(keeps[1], other[1]), 3)
-    from_back = over_z(add(keeps[2], other[2]), 1)
-    rest_fore = over_z(add(keeps[3][:rows], other[3][:rows], from_fore[:rows]), 3)
-    rest_back = over_z(add(keeps[3][rows:], other[3][rows:], from_back[:rows]), 1)
-    input_grad = jnp.concatenate(
-        [
-            add(keeps[0][:rows], other[0][:rows], rest_fore, from_back[rows:]),
-            add(keeps[0][rows:], other[0][rows:], from_fore[rows:], rest_back),
-        ]
     )
     caps = [blocks(CAP)] * 3 + [blocks(CAP // 2)] * 2
     sums = call(
@@ -454,9 +425,8 @@
     up_count, down_count = up_count[0], down_count[0]
     names = (up_count, up_row_block[0], up_col_block[0], down_count, down_row_block[0], down_col_block[0])
     grad_norm = float(activations.shape[0] * lax.axis_size("fsdp")) ** (-0.5)
+    wide = (activations, output_grad)
     rest = (
-        activations,
-        output_grad,
         up_scale[0].astype(jnp.float32) * grad_norm,
         down_scale[0].astype(jnp.float32) * grad_norm,
         up_count,
@@ -464,11 +434,15 @@
     )
     scaled_up = up_blocks[0] * up_scale[0][:, None, None]
     scaled_down = down_blocks[0] * down_scale[0][:, None, None]
-    near_up, near_down = spread([(scaled_up, over_x), (scaled_down, over_y)])
-    table, most = make_table(ROOM, place, *names)
+    activations = pltpu.with_memory_space_constraint(activations, pltpu.VMEM)
+    output_grad = pltpu.with_memory_space_constraint(output_grad, pltpu.VMEM)
+    table, most = make_table(ROOM, place, *names, held=(activations, output_grad))
+    (near_up, near_down), (table, most) = spread(
+        [(scaled_up, over_x), (scaled_down, over_y)], held=(table, most)
+    )
     (far_up, far_down), most = gather_far(ROOM, place, up_count, down_count, near_up, near_down, most)
     crowded = most[0] > ROOM
-    results = layer(ROOM, place, table, far_up, far_down, *rest)
+    results = layer(ROOM, place, table, far_up, far_down, activations, output_grad, *rest)
 
     def full(results, near_up, near_down, *rest):
         room = SIDE * CAP
@@ -476,7 +450,7 @@
         return layer(room, place, make_table(room, place, *names)[0], far_up, far_down, *rest)
 
     return lax.cond(
-        crowded, full, lambda results, *unused: results, results, near_up, near_down, *rest
+        crowded, full, lambda results, *unused: results, results, near_up, near_down, wide[0], wide[1], *rest
     )
 
 

time: 219 us -> 185 us (0.84)
  Pallas kernels: 56.3 us -> 37.9 us
  between operations: 3.71 us -> 17.1 us
  starting transfers between devices: 57.6 us -> 45.1 us
  waiting for transfers between devices: 81.7 us -> 70.6 us
  other arithmetic: 9.94 us -> 3.06 us
    ppermute x36 -> x32, starting transfers between devices: 51.1 us -> 38.3 us  [along(): return lambda array, step: lax.ppermute(array, axis, shift(step))]
    pallas_call x2, Pallas kernels: 45.6 us -> 33.9 us  [the longest x1 31.1 us: layer(): call(main, [jax.ShapeDtypeStruct((tokens, width), jnp.bfloat16)] + parts...]
    ppermute x36 -> x32, waiting for transfers between devices: 75.8 us -> 65.4 us  [along(): return lambda array, step: lax.ppermute(array, axis, shift(step))]
    convert_element_type x11 -> x8, other arithmetic: 7.6 us -> 0.79 us  [add(): return sum((a.astype(jnp.float32) for a in arrays)).astype(jnp.bfloat16)]
    pallas_call x1, Pallas kernels: 5.58 us -> 1.37 us  [layer(): call(unpack, caps * 2, [S] * 3 + [V] * 10, [V] * 10, [], 'unpack', 4)]
    unnamed x112 -> x76, local copies, waits for them, and re-layouts: 6.88 us -> 7.79 us
  transfers between devices with their start and end apart: 40 -> 36, of which waited for: 19 -> 22; matrix products, arithmetic and copies ran while one was open for 4% -> 1% of each run, Pallas kernels for 5% -> 3%
where the time goes in v3:
time: 185 us; the launch traced here: 182 us
  waiting for transfers between devices  70.6 us (38%)
  starting transfers between devices  45.1 us (24%)
  Pallas kernels  37.9 us (20%)
  between operations  17.1 us (9%)
  local copies, waits for them, and re-layouts  7.99 us (4%)
  other arithmetic  3.06 us (2%)
    ppermute x32, waiting for transfers between devices, along(): return lambda array, step: lax.ppermute(array, axis, shift(step))  65.4 us
    ppermute x32, starting transfers between devices, along(): return lambda array, step: lax.ppermute(array, axis, shift(step))  38.3 us
    pallas_call x1, Pallas kernels, layer(): call(main, [jax.ShapeDtypeStruct((tokens, width), jnp.bfloat16)] + parts...  31.1 us
    unnamed x76, local copies, waits for them, and re-layouts  7.79 us
    ppermute x3, starting transfers between devices, moved(): return lax.ppermute(flag, 'tensor', pairs)  6.85 us
    ppermute x3, waiting for transfers between devices, moved(): return lax.ppermute(flag, 'tensor', pairs)  5.13 us
  transfers between devices with their start and end apart: 36, of which 22 were waited for; matrix products, arithmetic and copies ran while one was open for 1% of the time, Pallas kernels for 3%

profile of v3, /device:TPU:0, one launch (start us, length us, event | category | flops | bytes accessed | tf_op | source)
XLA Modules:
  0.0 182.1 jit_solution(14676474064309630876)
XLA Ops:
  7.3 1.1 bitcast_multiply_fusion.refs_8_
  8.4 3.2 %collective-permute-start.27 = (bf16[12,128,128]{2,1,0:T(8,128)(2,1)S(1)}, bf16[12,128,128]{2,1,0:T(8,128)(2,1)S(1)}, u32[]{:S(2)}, u32[]{:S(2)}) collective-permute-start(bf16[12,128,128]{2,1,0:T(8,128)(2,1)S(1)} %bitcast_multiply_fusion.refs_8_), channel_id=1, source_target_pairs={{0,96},{8,104},{16,112},{24,120},{32,0},{40,8},{48,16},{56,24},{64... | collective-permute-start | bytes 1179656 | tf_op jit(solution)/shard_map/ppermute | solution.py:43
  11.5 1.1 bitcast_multiply_fusion.1.refs_3_
  12.6 2.8 %collective-permute-start.25 = (bf16[12,128,128]{2,1,0:T(8,128)(2,1)S(1)}, bf16[12,128,128]{2,1,0:T(8,128)(2,1)S(1)}, u32[]{:S(2)}, u32[]{:S(2)}) collective-permute-start(bf16[12,128,128]{2,1,0:T(8,128)(2,1)S(1)} %bitcast_multiply_fusion.1.refs_3_), channel_id=1, source_target_pairs={{0,24},{8,0},{16,8},{24,16},{32,56},{40,32},{48,40},{56,48},{64,88... | collective-permute-start | bytes 1179656 | tf_op jit(solution)/shard_map/ppermute | solution.py:43
  15.6 3.1 %copy-done = bf16[256,14336]{1,0:T(8,128)(2,1)S(1)} copy-done((bf16[256,14336]{1,0:T(8,128)(2,1)S(1)}, bf16[256,14336]{1,0:T(8,128)(2,1)}, u32[]{:S(2)}) %copy-start) | copy-done | bytes 7340056
  18.7 3.1 %copy-done.1 = bf16[256,14336]{1,0:T(8,128)(2,1)S(1)} copy-done((bf16[256,14336]{1,0:T(8,128)(2,1)S(1)}, bf16[256,14336]{1,0:T(8,128)(2,1)}, u32[]{:S(2)}) %copy-start.1) | copy-done | bytes 7340056
  21.8 2.8 %table.3 = (s32[8,192]{1,0:T(8,128)S(1)}, s32[1]{0:T(128)}) custom-call(s32[4]{0:T(128)S(1)} %pad_add_fusion.refs_0_.place, s32[16]{0:T(128)S(1)} %bitcast.21, s32[192]{0:T(256)S(1)} %bitcast.31, s32[192]{0:T(256)S(1)} %bitcast.33, s32[16]{0:T(128)S(1)} %bitcast.26, s32[192]{0:T(256)S(1)} %bitcast.35, s32[192]{0:T(256)S(1)} %bitcast.37, ...), custom_call_target="tpu_custom_call" | custom-call | bytes 9000000 | tf_op jit(solution)/shard_map/table/pallas_call | solution.py:189
  24.6 2.4 %collective-permute-done.24.refs_4_ = bf16[12,128,128]{2,1,0:T(8,128)(2,1)S(1)} collective-permute-done((bf16[12,128,128]{2,1,0:T(8,128)(2,1)S(1)}, bf16[12,128,128]{2,1,0:T(8,128)(2,1)S(1)}, u32[]{:S(2)}, u32[]{:S(2)}) %collective-permute-start.24) | collective-permute-done | bytes 393248 | tf_op jit(solution)/shard_map/ppermute | solution.py:43
  27.1 3.0 %collective-permute-start.31 = (bf16[6,128,128]{2,1,0:T(8,128)(2,1)S(1)}, bf16[6,128,128]{2,1,0:T(8,128)(2,1)S(1)}, u32[]{:S(2)}, u32[]{:S(2)}) collective-permute-start(bf16[6,128,128]{2,1,0:T(8,128)(2,1)S(1)} %slice.87), channel_id=1, source_target_pairs={{0,96},{8,104},{16,112},{24,120},{32,0},{40,8},{48,16},{56,24},{64... | collective-permute-start | bytes 589832 | tf_op jit(solution)/shard_map/ppermute | solution.py:43
  30.1 1.2 collective-permute-start.29
  32.1 1.2 collective-permute-done.31.refs_11_
  33.3 3.7 %collective-permute-done.30.refs_10_ = bf16[6,128,128]{2,1,0:T(8,128)(2,1)S(1)} collective-permute-done((bf16[6,128,128]{2,1,0:T(8,128)(2,1)S(1)}, bf16[6,128,128]{2,1,0:T(8,128)(2,1)S(1)}, u32[]{:S(2)}, u32[]{:S(2)}) %collective-permute-start.30) | collective-permute-done | bytes 196640 | tf_op jit(solution)/shard_map/ppermute | solution.py:43
  37.0 1.2 collective-permute-done.28.refs_5_
  39.1 3.3 %collective-permute-start.33 = (bf16[30,128,128]{2,1,0:T(8,128)(2,1)S(1)}, bf16[30,128,128]{2,1,0:T(8,128)(2,1)S(1)}, u32[]{:S(2)}, u32[]{:S(2)}) collective-permute-start(bf16[30,128,128]{2,1,0:T(8,128)(2,1)S(1)} %get-tuple-element.156.refs_4_), channel_id=1, source_target_pairs={{0,96},{8,104},{16,112},{24,120},{32,0},{40,8},{48,16},{56,24},{64... | collective-permute-start | bytes 2949128 | tf_op jit(solution)/shard_map/ppermute | solution.py:43
  42.4 2.0 %collective-permute-start.34 = (bf16[30,128,128]{2,1,0:T(8,128)(2,1)S(1)}, bf16[30,128,128]{2,1,0:T(8,128)(2,1)S(1)}, u32[]{:S(2)}, u32[]{:S(2)}) collective-permute-start(bf16[30,128,128]{2,1,0:T(8,128)(2,1)S(1)} %get-tuple-element.157.refs_9_), channel_id=1, source_target_pairs={{0,8},{8,16},{16,24},{24,0},{32,40},{40,48},{48,56},{56,32},{64,72... | collective-permute-start | bytes 2949128 | tf_op jit(solution)/shard_map/ppermute | solution.py:43
  44.4 1.2 collective-permute-done.36
  46.9 3.6 %collective-permute-start.37 = (s32[1]{0:T(128)}, s32[1]{0:T(128)}, u32[]{:S(2)}, u32[]{:S(2)}) collective-permute-start(s32[1]{0:T(128)} %max.9), channel_id=1, source_target_pairs={{0,2},{1,3},{2,4},{3,5},{4,6},{5,7},{6,0},{7,1},{8,10},{9,11},{10,... | collective-permute-start | bytes 20 | tf_op jit(solution)/shard_map/ppermute | solution.py:55
  50.5 2.1 %collective-permute-done.37 = s32[1]{0:T(128)} collective-permute-done((s32[1]{0:T(128)}, s32[1]{0:T(128)}, u32[]{:S(2)}, u32[]{:S(2)}) %collective-permute-start.37) | collective-permute-done | bytes 36 | tf_op jit(solution)/shard_map/ppermute | solution.py:55
  53.2 3.3 %collective-permute-start.38 = (s32[1]{0:T(128)}, s32[1]{0:T(128)}, u32[]{:S(2)}, u32[]{:S(2)}) collective-permute-start(s32[1]{0:T(128)} %max.10), channel_id=1, source_target_pairs={{0,4},{1,5},{2,6},{3,7},{4,0},{5,1},{6,2},{7,3},{8,12},{9,13},{10,... | collective-permute-start | bytes 20 | tf_op jit(solution)/shard_map/ppermute | solution.py:55
  56.5 1.8 collective-permute-done.38
  58.9 1.5 collective-permute-done.33.refs_8_
  60.4 3.4 %collective-permute-done.32.refs_5_ = bf16[30,128,128]{2,1,0:T(8,128)(2,1)S(1)} collective-permute-done((bf16[30,128,128]{2,1,0:T(8,128)(2,1)S(1)}, bf16[30,128,128]{2,1,0:T(8,128)(2,1)S(1)}, u32[]{:S(2)}, u32[]{:S(2)}) %collective-permute-start.32) | collective-permute-done | bytes 983072 | tf_op jit(solution)/shard_map/ppermute | solution.py:43
  65.0 1.7 collective-permute-start.41
  66.7 2.3 %collective-permute-start.40 = (bf16[15,128,128]{2,1,0:T(8,128)(2,1)S(1)}, bf16[15,128,128]{2,1,0:T(8,128)(2,1)S(1)}, u32[]{:S(2)}, u32[]{:S(2)}) collective-permute-start(bf16[15,128,128]{2,1,0:T(8,128)(2,1)S(1)} %slice.89), channel_id=1, source_target_pairs={{0,96},{8,104},{16,112},{24,120},{32,0},{40,8},{48,16},{56,24},{64... | collective-permute-start | bytes 1474568 | tf_op jit(solution)/shard_map/ppermute | solution.py:43
  69.1 4.5 %collective-permute-done.42.refs_12_ = bf16[15,128,128]{2,1,0:T(8,128)(2,1)S(1)} collective-permute-done((bf16[15,128,128]{2,1,0:T(8,128)(2,1)S(1)}, bf16[15,128,128]{2,1,0:T(8,128)(2,1)S(1)}, u32[]{:S(2)}, u32[]{:S(2)}) %collective-permute-start.42) | collective-permute-done | bytes 491552 | tf_op jit(solution)/shard_map/ppermute | solution.py:43
  73.5 1.5 collective-permute-done.41.refs_11_
  75.6 3.5 %collective-permute-done.39.refs_6_ = bf16[15,128,128]{2,1,0:T(8,128)(2,1)S(1)} collective-permute-done((bf16[15,128,128]{2,1,0:T(8,128)(2,1)S(1)}, bf16[15,128,128]{2,1,0:T(8,128)(2,1)S(1)}, u32[]{:S(2)}, u32[]{:S(2)}) %collective-permute-start.39) | collective-permute-done | bytes 491552 | tf_op jit(solution)/shard_map/ppermute | solution.py:43
  79.9 31.1 %main.3 = (bf16[256,14336]{1,0:T(8,128)(2,1)}, bf16[30,128,128]{2,1,0:T(8,128)(2,1)}, bf16[30,128,128]{2,1,0:T(8,128)(2,1)}, bf16[30,128,128]{2,1,0:T(8,128)(2,1...) custom-call(s32[4]{0:T(128)S(1)} %pad_add_fusion.refs_0_.place, ...), custom_call_target="tpu_custom_call" | custom-call | bytes 120000000 | tf_op jit(solution)/shard_map/main/pallas_call | solution.py:384
  111.8 1.4 collective-permute-start.44
  113.2 1.5 collective-permute-start.47
  115.2 17.4 %collective-permute-done.43.refs_4_ = bf16[30,128,128]{2,1,0:T(8,128)(2,1)S(1)} collective-permute-done((bf16[30,128,128]{2,1,0:T(8,128)(2,1)}, bf16[30,128,128]{2,1,0:T(8,128)(2,1)S(1)}, u32[]{:S(2)}, u32[]{:S(2)}) %collective-permute-start.43) | collective-permute-done | bytes 983072 | tf_op jit(solution)/shard_map/ppermute | solution.py:43
  132.8 1.2 collective-permute-start.45
  134.1 1.0 collective-permute-start.46
  135.3 2.0 %collective-permute-start.49 = (bf16[15,128,128]{2,1,0:T(8,128)(2,1)S(1)}, bf16[15,128,128]{2,1,0:T(8,128)(2,1)S(1)}, u32[]{:S(2)}, u32[]{:S(2)}) collective-permute-start(bf16[15,128,128]{2,1,0:T(8,128)(2,1)S(1)} %add_convert_fusion.9), channel_id=1, source_target_pairs={{0,24},{8,0},{16,8},{24,16},{32,56},{40,32},{48,40},{56,48},{64,88... | collective-permute-start | bytes 1474568 | tf_op jit(solution)/shard_map/ppermute | solution.py:43
  137.6 4.1 %collective-permute-done.45.refs_6_ = bf16[15,128,128]{2,1,0:T(8,128)(2,1)S(1)} collective-permute-done((bf16[15,128,128]{2,1,0:T(8,128)(2,1)S(1)}, bf16[15,128,128]{2,1,0:T(8,128)(2,1)S(1)}, u32[]{:S(2)}, u32[]{:S(2)}) %collective-permute-start.45) | collective-permute-done | bytes 491552 | tf_op jit(solution)/shard_map/ppermute | solution.py:43
  141.7 2.5 %collective-permute-done.46.refs_7_ = bf16[15,128,128]{2,1,0:T(8,128)(2,1)S(1)} collective-permute-done((bf16[15,128,128]{2,1,0:T(8,128)(2,1)S(1)}, bf16[15,128,128]{2,1,0:T(8,128)(2,1)S(1)}, u32[]{:S(2)}, u32[]{:S(2)}) %collective-permute-start.46) | collective-permute-done | bytes 491552 | tf_op jit(solution)/shard_map/ppermute | solution.py:43
  144.2 3.4 %collective-permute-done.49.refs_11_ = bf16[15,128,128]{2,1,0:T(8,128)(2,1)S(1)} collective-permute-done((bf16[15,128,128]{2,1,0:T(8,128)(2,1)S(1)}, bf16[15,128,128]{2,1,0:T(8,128)(2,1)S(1)}, u32[]{:S(2)}, u32[]{:S(2)}) %collective-permute-start.49) | collective-permute-done | bytes 491552 | tf_op jit(solution)/shard_map/ppermute | solution.py:43
  147.7 4.1 %collective-permute-done.50.refs_12_ = bf16[15,128,128]{2,1,0:T(8,128)(2,1)S(1)} collective-permute-done((bf16[15,128,128]{2,1,0:T(8,128)(2,1)S(1)}, bf16[15,128,128]{2,1,0:T(8,128)(2,1)S(1)}, u32[]{:S(2)}, u32[]{:S(2)}) %collective-permute-start.50) | collective-permute-done | bytes 491552 | tf_op jit(solution)/shard_map/ppermute | solution.py:43
  151.7 1.4 unpack.3
  153.2 2.0 %collective-permute-start.52 = (bf16[12,128,128]{2,1,0:T(8,128)(2,1)S(1)}, bf16[12,128,128]{2,1,0:T(8,128)(2,1)S(1)}, u32[]{:S(2)}, u32[]{:S(2)}) collective-permute-start(bf16[12,128,128]{2,1,0:T(8,128)(2,1)S(1)} %get-tuple-element.177), channel_id=1, source_target_pairs={{0,8},{8,16},{16,24},{24,0},{32,40},{40,48},{48,56},{56,32},{64,72... | collective-permute-start | bytes 1179656 | tf_op jit(solution)/shard_map/ppermute | solution.py:43
  155.2 1.7 collective-permute-start.55
  157.2 3.7 %collective-permute-done.51.refs_1_ = bf16[12,128,128]{2,1,0:T(8,128)(2,1)S(1)} collective-permute-done((bf16[12,128,128]{2,1,0:T(8,128)(2,1)S(1)}, bf16[12,128,128]{2,1,0:T(8,128)(2,1)S(1)}, u32[]{:S(2)}, u32[]{:S(2)}) %collective-permute-start.51) | collective-permute-done | bytes 393248 | tf_op jit(solution)/shard_map/ppermute | solution.py:43
  161.0 1.3 collective-permute-start.53
  162.4 0.9 collective-permute-start.54
  163.3 2.8 %collective-permute-start.57 = (bf16[6,128,128]{2,1,0:T(8,128)(2,1)S(1)}, bf16[6,128,128]{2,1,0:T(8,128)(2,1)S(1)}, u32[]{:S(2)}, u32[]{:S(2)}) collective-permute-start(bf16[6,128,128]{2,1,0:T(8,128)(2,1)S(1)} %add_convert_fusion.13), channel_id=1, source_target_pairs={{0,96},{8,104},{16,112},{24,120},{32,0},{40,8},{48,16},{56,24},{64... | collective-permute-start | bytes 589832 | tf_op jit(solution)/shard_map/ppermute | solution.py:43
  166.8 2.6 %collective-permute-done.54.refs_4_ = bf16[6,128,128]{2,1,0:T(8,128)(2,1)S(1)} collective-permute-done((bf16[6,128,128]{2,1,0:T(8,128)(2,1)S(1)}, bf16[6,128,128]{2,1,0:T(8,128)(2,1)S(1)}, u32[]{:S(2)}, u32[]{:S(2)}) %collective-permute-start.54) | collective-permute-done | bytes 196640 | tf_op jit(solution)/shard_map/ppermute | solution.py:43
  169.3 3.8 %collective-permute-done.58.refs_9_ = bf16[6,128,128]{2,1,0:T(8,128)(2,1)S(1)} collective-permute-done((bf16[6,128,128]{2,1,0:T(8,128)(2,1)S(1)}, bf16[6,128,128]{2,1,0:T(8,128)(2,1)S(1)}, u32[]{:S(2)}, u32[]{:S(2)}) %collective-permute-start.58) | collective-permute-done | bytes 196640 | tf_op jit(solution)/shard_map/ppermute | solution.py:43
  173.1 1.7 finish.3
  (128 shorter events, 8.1 us)
Async XLA Ops:
  7.2 8.4 %copy-start.45 = (s32[1,16]{1,0:T(1,128)S(1)}, s32[1,16]{1,0:T(1,128)}, u32[]{:S(2)}) copy-start(s32[1,16]{1,0:T(1,128)} %param.25) | copy-start | bytes 196
  7.2 8.4 %copy-start.44 = (s32[1,16]{1,0:T(1,128)S(1)}, s32[1,16]{1,0:T(1,128)}, u32[]{:S(2)}) copy-start(s32[1,16]{1,0:T(1,128)} %param.24) | copy-start | bytes 196
  7.2 167.6 %reduce-scatter.5.cloned.1.call-start = ((), (), s32[]{:S(2)}) async-start(), calls=%async_computation.3 | async-start | bytes 8257536 | tf_op jit(solution)/shard_map/reduce_scatter | solution.py:394
  8.4 16.2 %collective-permute-start.27 = (bf16[12,128,128]{2,1,0:T(8,128)(2,1)S(1)}, bf16[12,128,128]{2,1,0:T(8,128)(2,1)S(1)}, u32[]{:S(2)}, u32[]{:S(2)}) collective-permute-start(bf16[12,128,128]{2,1,0:T(8,128)(2,1)S(1)} %bitcast_multiply_fusion.refs_8_), channel_id=1, source_target_pairs={{0,96},{8,104},{16,112},{24,120},{32,0},{40,8},{48,16},{56,24},{64... | collective-permute-start | bytes 1179656 | tf_op jit(solution)/shard_map/ppermute | solution.py:43
  11.5 13.1 %collective-permute-start.26 = (bf16[12,128,128]{2,1,0:T(8,128)(2,1)S(1)}, bf16[12,128,128]{2,1,0:T(8,128)(2,1)S(1)}, u32[]{:S(2)}, u32[]{:S(2)}) collective-permute-start(bf16[12,128,128]{2,1,0:T(8,128)(2,1)S(1)} %bitcast_multiply_fusion.refs_8_), channel_id=1, source_target_pairs={{0,32},{8,40},{16,48},{24,56},{32,64},{40,72},{48,80},{56,88},{64,... | collective-permute-start | bytes 1179656 | tf_op jit(solution)/shard_map/ppermute | solution.py:43
  12.6 12.0 %collective-permute-start.25 = (bf16[12,128,128]{2,1,0:T(8,128)(2,1)S(1)}, bf16[12,128,128]{2,1,0:T(8,128)(2,1)S(1)}, u32[]{:S(2)}, u32[]{:S(2)}) collective-permute-start(bf16[12,128,128]{2,1,0:T(8,128)(2,1)S(1)} %bitcast_multiply_fusion.1.refs_3_), channel_id=1, source_target_pairs={{0,24},{8,0},{16,8},{24,16},{32,56},{40,32},{48,40},{56,48},{64,88... | collective-permute-start | bytes 1179656 | tf_op jit(solution)/shard_map/ppermute | solution.py:43
  15.5 11.5 %collective-permute-start.24 = (bf16[12,128,128]{2,1,0:T(8,128)(2,1)S(1)}, bf16[12,128,128]{2,1,0:T(8,128)(2,1)S(1)}, u32[]{:S(2)}, u32[]{:S(2)}) collective-permute-start(bf16[12,128,128]{2,1,0:T(8,128)(2,1)S(1)} %bitcast_multiply_fusion.1.refs_3_), channel_id=1, source_target_pairs={{0,8},{8,16},{16,24},{24,0},{32,40},{40,48},{48,56},{56,32},{64,72... | collective-permute-start | bytes 1179656 | tf_op jit(solution)/shard_map/ppermute | solution.py:43
  24.6 14.4 %copy-start.16 = (bf16[12,128,128]{2,1,0:T(8,128)(2,1)}, bf16[12,128,128]{2,1,0:T(8,128)(2,1)S(1)}, u32[]{:S(2)}) copy-start(bf16[12,128,128]{2,1,0:T(8,128)(2,1)S(1)} %collective-permute-done.25.refs_7_) | copy-start | bytes 1179652
  27.0 12.1 %copy-start.18 = (bf16[12,128,128]{2,1,0:T(8,128)(2,1)}, bf16[12,128,128]{2,1,0:T(8,128)(2,1)S(1)}, u32[]{:S(2)}) copy-start(bf16[12,128,128]{2,1,0:T(8,128)(2,1)S(1)} %collective-permute-done.24.refs_4_) | copy-start | bytes 1179652
  27.0 52.9 %copy-start.2 = (bf16[256,14336]{1,0:T(8,128)(2,1)S(1)}, bf16[256,14336]{1,0:T(8,128)(2,1)}, u32[]{:S(2)}) copy-start(bf16[256,14336]{1,0:T(8,128)(2,1)} %refs_3_.1) | copy-start | bytes 22020100
  27.1 6.2 %collective-permute-start.31 = (bf16[6,128,128]{2,1,0:T(8,128)(2,1)S(1)}, bf16[6,128,128]{2,1,0:T(8,128)(2,1)S(1)}, u32[]{:S(2)}, u32[]{:S(2)}) collective-permute-start(bf16[6,128,128]{2,1,0:T(8,128)(2,1)S(1)} %slice.87), channel_id=1, source_target_pairs={{0,96},{8,104},{16,112},{24,120},{32,0},{40,8},{48,16},{56,24},{64... | collective-permute-start | bytes 589832 | tf_op jit(solution)/shard_map/ppermute | solution.py:43
  30.1 6.9 %collective-permute-start.30 = (bf16[6,128,128]{2,1,0:T(8,128)(2,1)S(1)}, bf16[6,128,128]{2,1,0:T(8,128)(2,1)S(1)}, u32[]{:S(2)}, u32[]{:S(2)}) collective-permute-start(bf16[6,128,128]{2,1,0:T(8,128)(2,1)S(1)} %slice.86), channel_id=1, source_target_pairs={{0,32},{8,40},{16,48},{24,56},{32,64},{40,72},{48,80},{56,88},{64,... | collective-permute-start | bytes 589832 | tf_op jit(solution)/shard_map/ppermute | solution.py:43
  30.1 6.9 %collective-permute-start.29 = (bf16[6,128,128]{2,1,0:T(8,128)(2,1)S(1)}, bf16[6,128,128]{2,1,0:T(8,128)(2,1)S(1)}, u32[]{:S(2)}, u32[]{:S(2)}) collective-permute-start(bf16[6,128,128]{2,1,0:T(8,128)(2,1)S(1)} %slice.85), channel_id=1, source_target_pairs={{0,24},{8,0},{16,8},{24,16},{32,56},{40,32},{48,40},{56,48},{64,88... | collective-permute-start | bytes 589832 | tf_op jit(solution)/shard_map/ppermute | solution.py:43
  31.3 6.9 %collective-permute-start.28 = (bf16[6,128,128]{2,1,0:T(8,128)(2,1)S(1)}, bf16[6,128,128]{2,1,0:T(8,128)(2,1)S(1)}, u32[]{:S(2)}, u32[]{:S(2)}) collective-permute-start(bf16[6,128,128]{2,1,0:T(8,128)(2,1)S(1)} %slice.84), channel_id=1, source_target_pairs={{0,8},{8,16},{16,24},{24,0},{32,40},{40,48},{48,56},{56,32},{64,72... | collective-permute-start | bytes 589832 | tf_op jit(solution)/shard_map/ppermute | solution.py:43
  39.1 24.9 %copy-start.7 = (bf16[30,128,128]{2,1,0:T(8,128)(2,1)}, bf16[30,128,128]{2,1,0:T(8,128)(2,1)S(1)}, u32[]{:S(2)}) copy-start(bf16[30,128,128]{2,1,0:T(8,128)(2,1)S(1)} %get-tuple-element.156.refs_4_) | copy-start | bytes 2949124
  39.1 24.9 %copy-start.8 = (bf16[30,128,128]{2,1,0:T(8,128)(2,1)}, bf16[30,128,128]{2,1,0:T(8,128)(2,1)S(1)}, u32[]{:S(2)}) copy-start(bf16[30,128,128]{2,1,0:T(8,128)(2,1)S(1)} %get-tuple-element.157.refs_9_) | copy-start | bytes 2949124
  39.1 21.2 %collective-permute-start.33 = (bf16[30,128,128]{2,1,0:T(8,128)(2,1)S(1)}, bf16[30,128,128]{2,1,0:T(8,128)(2,1)S(1)}, u32[]{:S(2)}, u32[]{:S(2)}) collective-permute-start(bf16[30,128,128]{2,1,0:T(8,128)(2,1)S(1)} %get-tuple-element.156.refs_4_), channel_id=1, source_target_pairs={{0,96},{8,104},{16,112},{24,120},{32,0},{40,8},{48,16},{56,24},{64... | collective-permute-start | bytes 2949128 | tf_op jit(solution)/shard_map/ppermute | solution.py:43
  42.4 21.4 %collective-permute-start.32 = (bf16[30,128,128]{2,1,0:T(8,128)(2,1)S(1)}, bf16[30,128,128]{2,1,0:T(8,128)(2,1)S(1)}, u32[]{:S(2)}, u32[]{:S(2)}) collective-permute-start(bf16[30,128,128]{2,1,0:T(8,128)(2,1)S(1)} %get-tuple-element.156.refs_4_), channel_id=1, source_target_pairs={{0,32},{8,40},{16,48},{24,56},{32,64},{40,72},{48,80},{56,88},{64,... | collective-permute-start | bytes 2949128 | tf_op jit(solution)/shard_map/ppermute | solution.py:43
  42.4 21.4 %collective-permute-start.35 = (bf16[30,128,128]{2,1,0:T(8,128)(2,1)S(1)}, bf16[30,128,128]{2,1,0:T(8,128)(2,1)S(1)}, u32[]{:S(2)}, u32[]{:S(2)}) collective-permute-start(bf16[30,128,128]{2,1,0:T(8,128)(2,1)S(1)} %get-tuple-element.157.refs_9_), channel_id=1, source_target_pairs={{0,24},{8,0},{16,8},{24,16},{32,56},{40,32},{48,40},{56,48},{64,88... | collective-permute-start | bytes 2949128 | tf_op jit(solution)/shard_map/ppermute | solution.py:43
  42.4 21.4 %collective-permute-start.34 = (bf16[30,128,128]{2,1,0:T(8,128)(2,1)S(1)}, bf16[30,128,128]{2,1,0:T(8,128)(2,1)S(1)}, u32[]{:S(2)}, u32[]{:S(2)}) collective-permute-start(bf16[30,128,128]{2,1,0:T(8,128)(2,1)S(1)} %get-tuple-element.157.refs_9_), channel_id=1, source_target_pairs={{0,8},{8,16},{16,24},{24,0},{32,40},{40,48},{48,56},{56,32},{64,72... | collective-permute-start | bytes 2949128 | tf_op jit(solution)/shard_map/ppermute | solution.py:43
  44.4 1.2 collective-permute-start.36
  46.9 5.7 %collective-permute-start.37 = (s32[1]{0:T(128)}, s32[1]{0:T(128)}, u32[]{:S(2)}, u32[]{:S(2)}) collective-permute-start(s32[1]{0:T(128)} %max.9), channel_id=1, source_target_pairs={{0,2},{1,3},{2,4},{3,5},{4,6},{5,7},{6,0},{7,1},{8,10},{9,11},{10,... | collective-permute-start | bytes 20 | tf_op jit(solution)/shard_map/ppermute | solution.py:55
  53.2 5.1 %collective-permute-start.38 = (s32[1]{0:T(128)}, s32[1]{0:T(128)}, u32[]{:S(2)}, u32[]{:S(2)}) collective-permute-start(s32[1]{0:T(128)} %max.10), channel_id=1, source_target_pairs={{0,4},{1,5},{2,6},{3,7},{4,0},{5,1},{6,2},{7,3},{8,12},{9,13},{10,... | collective-permute-start | bytes 20 | tf_op jit(solution)/shard_map/ppermute | solution.py:55
  63.8 15.3 %copy-start.22 = (bf16[30,128,128]{2,1,0:T(8,128)(2,1)}, bf16[30,128,128]{2,1,0:T(8,128)(2,1)S(1)}, u32[]{:S(2)}) copy-start(bf16[30,128,128]{2,1,0:T(8,128)(2,1)S(1)} %collective-permute-done.35.refs_13_) | copy-start | bytes 2949124
  63.8 15.3 %copy-start.23 = (bf16[30,128,128]{2,1,0:T(8,128)(2,1)}, bf16[30,128,128]{2,1,0:T(8,128)(2,1)S(1)}, u32[]{:S(2)}) copy-start(bf16[30,128,128]{2,1,0:T(8,128)(2,1)S(1)} %collective-permute-done.34.refs_10_) | copy-start | bytes 2949124
  64.7 8.8 %collective-permute-start.42 = (bf16[15,128,128]{2,1,0:T(8,128)(2,1)S(1)}, bf16[15,128,128]{2,1,0:T(8,128)(2,1)S(1)}, u32[]{:S(2)}, u32[]{:S(2)}) collective-permute-start(bf16[15,128,128]{2,1,0:T(8,128)(2,1)S(1)} %slice.91), channel_id=1, source_target_pairs={{0,24},{8,0},{16,8},{24,16},{32,56},{40,32},{48,40},{56,48},{64,88... | collective-permute-start | bytes 1474568 | tf_op jit(solution)/shard_map/ppermute | solution.py:43
  65.0 10.0 %collective-permute-start.41 = (bf16[15,128,128]{2,1,0:T(8,128)(2,1)S(1)}, bf16[15,128,128]{2,1,0:T(8,128)(2,1)S(1)}, u32[]{:S(2)}, u32[]{:S(2)}) collective-permute-start(bf16[15,128,128]{2,1,0:T(8,128)(2,1)S(1)} %slice.90), channel_id=1, source_target_pairs={{0,8},{8,16},{16,24},{24,0},{32,40},{40,48},{48,56},{56,32},{64,72... | collective-permute-start | bytes 1474568 | tf_op jit(solution)/shard_map/ppermute | solution.py:43
  66.7 8.8 %collective-permute-start.40 = (bf16[15,128,128]{2,1,0:T(8,128)(2,1)S(1)}, bf16[15,128,128]{2,1,0:T(8,128)(2,1)S(1)}, u32[]{:S(2)}, u32[]{:S(2)}) collective-permute-start(bf16[15,128,128]{2,1,0:T(8,128)(2,1)S(1)} %slice.89), channel_id=1, source_target_pairs={{0,96},{8,104},{16,112},{24,120},{32,0},{40,8},{48,16},{56,24},{64... | collective-permute-start | bytes 1474568 | tf_op jit(solution)/shard_map/ppermute | solution.py:43
  69.0 10.0 %collective-permute-start.39 = (bf16[15,128,128]{2,1,0:T(8,128)(2,1)S(1)}, bf16[15,128,128]{2,1,0:T(8,128)(2,1)S(1)}, u32[]{:S(2)}, u32[]{:S(2)}) collective-permute-start(bf16[15,128,128]{2,1,0:T(8,128)(2,1)S(1)} %slice.88), channel_id=1, source_target_pairs={{0,32},{8,40},{16,48},{24,56},{32,64},{40,72},{48,80},{56,88},{64,... | collective-permute-start | bytes 1474568 | tf_op jit(solution)/shard_map/ppermute | solution.py:43
  111.1 21.6 %collective-permute-start.43 = (bf16[30,128,128]{2,1,0:T(8,128)(2,1)}, bf16[30,128,128]{2,1,0:T(8,128)(2,1)S(1)}, u32[]{:S(2)}, u32[]{:S(2)}) collective-permute-start(bf16[30,128,128]{2,1,0:T(8,128)(2,1)} %get-tuple-element.166), channel_id=1, source_target_pairs={{0,96},{8,104},{16,112},{24,120},{32,0},{40,8},{48,16},{56,24},{64... | collective-permute-start | bytes 2949128 | tf_op jit(solution)/shard_map/ppermute | solution.py:43
  111.8 22.1 %collective-permute-start.44 = (bf16[30,128,128]{2,1,0:T(8,128)(2,1)}, bf16[30,128,128]{2,1,0:T(8,128)(2,1)S(1)}, u32[]{:S(2)}, u32[]{:S(2)}) collective-permute-start(bf16[30,128,128]{2,1,0:T(8,128)(2,1)} %get-tuple-element.167), channel_id=1, source_target_pairs={{0,32},{8,40},{16,48},{24,56},{32,64},{40,72},{48,80},{56,88},{64,... | collective-permute-start | bytes 2949128 | tf_op jit(solution)/shard_map/ppermute | solution.py:43
  113.2 22.0 %collective-permute-start.47 = (bf16[30,128,128]{2,1,0:T(8,128)(2,1)}, bf16[30,128,128]{2,1,0:T(8,128)(2,1)S(1)}, u32[]{:S(2)}, u32[]{:S(2)}) collective-permute-start(bf16[30,128,128]{2,1,0:T(8,128)(2,1)} %get-tuple-element.171), channel_id=1, source_target_pairs={{0,24},{8,0},{16,8},{24,16},{32,56},{40,32},{48,40},{56,48},{64,88... | collective-permute-start | bytes 2949128 | tf_op jit(solution)/shard_map/ppermute | solution.py:43
  114.6 22.6 %collective-permute-start.48 = (bf16[30,128,128]{2,1,0:T(8,128)(2,1)}, bf16[30,128,128]{2,1,0:T(8,128)(2,1)S(1)}, u32[]{:S(2)}, u32[]{:S(2)}) collective-permute-start(bf16[30,128,128]{2,1,0:T(8,128)(2,1)} %get-tuple-element.172), channel_id=1, source_target_pairs={{0,8},{8,16},{16,24},{24,0},{32,40},{40,48},{48,56},{56,32},{64,72... | collective-permute-start | bytes 2949128 | tf_op jit(solution)/shard_map/ppermute | solution.py:43
  132.8 8.9 %collective-permute-start.45 = (bf16[15,128,128]{2,1,0:T(8,128)(2,1)S(1)}, bf16[15,128,128]{2,1,0:T(8,128)(2,1)S(1)}, u32[]{:S(2)}, u32[]{:S(2)}) collective-permute-start(bf16[15,128,128]{2,1,0:T(8,128)(2,1)S(1)} %add_convert_fusion.11), channel_id=1, source_target_pairs={{0,96},{8,104},{16,112},{24,120},{32,0},{40,8},{48,16},{56,24},{64... | collective-permute-start | bytes 1474568 | tf_op jit(solution)/shard_map/ppermute | solution.py:43
  134.1 17.6 %copy-start.9 = (bf16[30,128,128]{2,1,0:T(8,128)(2,1)S(1)}, bf16[30,128,128]{2,1,0:T(8,128)(2,1)}, u32[]{:S(2)}) copy-start(bf16[30,128,128]{2,1,0:T(8,128)(2,1)} %get-tuple-element.165.refs_3_) | copy-start | bytes 2949124
  134.1 17.6 %copy-start.10 = (bf16[30,128,128]{2,1,0:T(8,128)(2,1)S(1)}, bf16[30,128,128]{2,1,0:T(8,128)(2,1)}, u32[]{:S(2)}) copy-start(bf16[30,128,128]{2,1,0:T(8,128)(2,1)} %get-tuple-element.170.refs_8_) | copy-start | bytes 2949124
  134.1 10.1 %collective-permute-start.46 = (bf16[15,128,128]{2,1,0:T(8,128)(2,1)S(1)}, bf16[15,128,128]{2,1,0:T(8,128)(2,1)S(1)}, u32[]{:S(2)}, u32[]{:S(2)}) collective-permute-start(bf16[15,128,128]{2,1,0:T(8,128)(2,1)S(1)} %add_convert_fusion.10), channel_id=1, source_target_pairs={{0,32},{8,40},{16,48},{24,56},{32,64},{40,72},{48,80},{56,88},{64,... | collective-permute-start | bytes 1474568 | tf_op jit(solution)/shard_map/ppermute | solution.py:43
  135.3 12.4 %collective-permute-start.49 = (bf16[15,128,128]{2,1,0:T(8,128)(2,1)S(1)}, bf16[15,128,128]{2,1,0:T(8,128)(2,1)S(1)}, u32[]{:S(2)}, u32[]{:S(2)}) collective-permute-start(bf16[15,128,128]{2,1,0:T(8,128)(2,1)S(1)} %add_convert_fusion.9), channel_id=1, source_target_pairs={{0,24},{8,0},{16,8},{24,16},{32,56},{40,32},{48,40},{56,48},{64,88... | collective-permute-start | bytes 1474568 | tf_op jit(solution)/shard_map/ppermute | solution.py:43
  137.4 14.3 %collective-permute-start.50 = (bf16[15,128,128]{2,1,0:T(8,128)(2,1)S(1)}, bf16[15,128,128]{2,1,0:T(8,128)(2,1)S(1)}, u32[]{:S(2)}, u32[]{:S(2)}) collective-permute-start(bf16[15,128,128]{2,1,0:T(8,128)(2,1)S(1)} %add_convert_fusion.8), channel_id=1, source_target_pairs={{0,8},{8,16},{16,24},{24,0},{32,40},{40,48},{48,56},{56,32},{64,72... | collective-permute-start | bytes 1474568 | tf_op jit(solution)/shard_map/ppermute | solution.py:43
  153.1 13.1 %copy-start.54 = (bf16[1,12]{1,0:T(2,128)(2,1)S(1)}, bf16[1,12]{1,0:T(2,128)(2,1)}, u32[]{:S(2)}) copy-start(bf16[1,12]{1,0:T(2,128)(2,1)} %param.19) | copy-start | bytes 76
  153.1 7.8 %collective-permute-start.51 = (bf16[12,128,128]{2,1,0:T(8,128)(2,1)S(1)}, bf16[12,128,128]{2,1,0:T(8,128)(2,1)S(1)}, u32[]{:S(2)}, u32[]{:S(2)}) collective-permute-start(bf16[12,128,128]{2,1,0:T(8,128)(2,1)S(1)} %get-tuple-element.176), channel_id=1, source_target_pairs={{0,24},{8,0},{16,8},{24,16},{32,56},{40,32},{48,40},{56,48},{64,88... | collective-permute-start | bytes 1179656 | tf_op jit(solution)/shard_map/ppermute | solution.py:43
  153.2 9.1 %collective-permute-start.52 = (bf16[12,128,128]{2,1,0:T(8,128)(2,1)S(1)}, bf16[12,128,128]{2,1,0:T(8,128)(2,1)S(1)}, u32[]{:S(2)}, u32[]{:S(2)}) collective-permute-start(bf16[12,128,128]{2,1,0:T(8,128)(2,1)S(1)} %get-tuple-element.177), channel_id=1, source_target_pairs={{0,8},{8,16},{16,24},{24,0},{32,40},{40,48},{48,56},{56,32},{64,72... | collective-permute-start | bytes 1179656 | tf_op jit(solution)/shard_map/ppermute | solution.py:43
  155.2 8.0 %collective-permute-start.55 = (bf16[12,128,128]{2,1,0:T(8,128)(2,1)S(1)}, bf16[12,128,128]{2,1,0:T(8,128)(2,1)S(1)}, u32[]{:S(2)}, u32[]{:S(2)}) collective-permute-start(bf16[12,128,128]{2,1,0:T(8,128)(2,1)S(1)} %get-tuple-element.181), channel_id=1, source_target_pairs={{0,96},{8,104},{16,112},{24,120},{32,0},{40,8},{48,16},{56,24},{64... | collective-permute-start | bytes 1179656 | tf_op jit(solution)/shard_map/ppermute | solution.py:43
  157.0 9.1 %collective-permute-start.56 = (bf16[12,128,128]{2,1,0:T(8,128)(2,1)S(1)}, bf16[12,128,128]{2,1,0:T(8,128)(2,1)S(1)}, u32[]{:S(2)}, u32[]{:S(2)}) collective-permute-start(bf16[12,128,128]{2,1,0:T(8,128)(2,1)S(1)} %get-tuple-element.182), channel_id=1, source_target_pairs={{0,32},{8,40},{16,48},{24,56},{32,64},{40,72},{48,80},{56,88},{64,... | collective-permute-start | bytes 1179656 | tf_op jit(solution)/shard_map/ppermute | solution.py:43
  161.0 5.7 %collective-permute-start.53 = (bf16[6,128,128]{2,1,0:T(8,128)(2,1)S(1)}, bf16[6,128,128]{2,1,0:T(8,128)(2,1)S(1)}, u32[]{:S(2)}, u32[]{:S(2)}) collective-permute-start(bf16[6,128,128]{2,1,0:T(8,128)(2,1)S(1)} %add_convert_fusion.15), channel_id=1, source_target_pairs={{0,24},{8,0},{16,8},{24,16},{32,56},{40,32},{48,40},{56,48},{64,88... | collective-permute-start | bytes 589832 | tf_op jit(solution)/shard_map/ppermute | solution.py:43
  162.4 6.9 %collective-permute-start.54 = (bf16[6,128,128]{2,1,0:T(8,128)(2,1)S(1)}, bf16[6,128,128]{2,1,0:T(8,128)(2,1)S(1)}, u32[]{:S(2)}, u32[]{:S(2)}) collective-permute-start(bf16[6,128,128]{2,1,0:T(8,128)(2,1)S(1)} %add_convert_fusion.14), channel_id=1, source_target_pairs={{0,8},{8,16},{16,24},{24,0},{32,40},{40,48},{48,56},{56,32},{64,72... | collective-permute-start | bytes 589832 | tf_op jit(solution)/shard_map/ppermute | solution.py:43
  163.3 6.0 %collective-permute-start.57 = (bf16[6,128,128]{2,1,0:T(8,128)(2,1)S(1)}, bf16[6,128,128]{2,1,0:T(8,128)(2,1)S(1)}, u32[]{:S(2)}, u32[]{:S(2)}) collective-permute-start(bf16[6,128,128]{2,1,0:T(8,128)(2,1)S(1)} %add_convert_fusion.13), channel_id=1, source_target_pairs={{0,96},{8,104},{16,112},{24,120},{32,0},{40,8},{48,16},{56,24},{64... | collective-permute-start | bytes 589832 | tf_op jit(solution)/shard_map/ppermute | solution.py:43
  166.1 6.9 %collective-permute-start.58 = (bf16[6,128,128]{2,1,0:T(8,128)(2,1)S(1)}, bf16[6,128,128]{2,1,0:T(8,128)(2,1)S(1)}, u32[]{:S(2)}, u32[]{:S(2)}) collective-permute-start(bf16[6,128,128]{2,1,0:T(8,128)(2,1)S(1)} %add_convert_fusion.12), channel_id=1, source_target_pairs={{0,32},{8,40},{16,48},{24,56},{32,64},{40,72},{48,80},{56,88},{64,... | collective-permute-start | bytes 589832 | tf_op jit(solution)/shard_map/ppermute | solution.py:43
  (26 other events, 88.8 us)
Sparse Core Ops, SparseCore 0:
  111.2 47.1 reduce-scatter.4

commit v4 on v3

--- a/solution.py
+++ b/solution.py
@@ -143,9 +143,8 @@
             position = lax.fori_loop(0, live, put, position)
 
 
-def table_kernel(room, place, up_count, up_row, up_col, down_count, down_row, down_col, table, most):
+def table_kernel(room, place, up_count, up_row, up_col, down_count, down_row, down_col, table):
     y, x = place[0], place[1]
-    largest = 0
     for first, owner_of, count, rows, cols in (
         (0, up_owner, up_count, up_row, up_col),
         (3, down_owner, down_count, down_row, down_col),
@@ -159,10 +158,8 @@
         total = 0
         for far in range(SIDE):
             position = far * room
-            wanted = 0
             for near in range(SIDE):
                 owner = owner_of(y, x, far, near)
-                wanted = wanted + count[owner]
                 live = jnp.minimum(count[owner], (far + 1) * room - position)
 
                 def note(j, unused, first=first, rows=rows, cols=cols, owner=owner, total=total, position=position):
@@ -174,21 +171,27 @@
                 lax.fori_loop(0, live, note, 0)
                 total = total + live
                 position = position + live
-            largest = jnp.maximum(largest, wanted)
         padded = (total + 3) // 4
         lax.fori_loop(total, padded * 4, blank, 0)
         table[6, first] = padded
-    most[0] = largest
 
 
 def make_table(room, place, up_count, up_row, up_col, down_count, down_row, down_col, held=()):
     def kernel(*refs):
-        table_kernel(room, *refs[:7], *refs[7 + len(held):])
-
-    outs = [jax.ShapeDtypeStruct((8, LIST), jnp.int32), jax.ShapeDtypeStruct((1,), jnp.int32)]
-    return call(kernel, outs, [S] * 7 + [V] * len(held), [S] * 2, [], "table", 3)(
+        table_kernel(room, *refs[:7], refs[-1])
+
+    outs = [jax.ShapeDtypeStruct((8, LIST), jnp.int32)]
+    return call(kernel, outs, [S] * 7 + [V] * len(held), [S], [], "table", 3)(
         place, up_count, up_row, up_col, down_count, down_row, down_col, *held
-    )
+    )[0]
+
+
+def crowd_kernel(up_count, down_count, most):
+    largest = 0
+    for line in range(SIDE):
+        largest = jnp.maximum(largest, sum(up_count[line * SIDE + i] for i in range(SIDE)))
+        largest = jnp.maximum(largest, sum(down_count[i * SIDE + line] for i in range(SIDE)))
+    most[0] = largest
 
 
 def lane(index):
@@ -436,18 +439,19 @@
     scaled_down = down_blocks[0] * down_scale[0][:, None, None]
     activations = pltpu.with_memory_space_constraint(activations, pltpu.VMEM)
     output_grad = pltpu.with_memory_space_constraint(output_grad, pltpu.VMEM)
-    table, most = make_table(ROOM, place, *names, held=(activations, output_grad))
-    (near_up, near_down), (table, most) = spread(
-        [(scaled_up, over_x), (scaled_down, over_y)], held=(table, most)
-    )
+    (most,) = call(
+        crowd_kernel, [jax.ShapeDtypeStruct((1,), jnp.int32)], [S, S], [S], [], "crowd", 1
+    )(up_count, down_count)
+    near_up, near_down = spread([(scaled_up, over_x), (scaled_down, over_y)])
     (far_up, far_down), most = gather_far(ROOM, place, up_count, down_count, near_up, near_down, most)
+    table = make_table(ROOM, place, *names, held=(activations, output_grad))
     crowded = most[0] > ROOM
     results = layer(ROOM, place, table, far_up, far_down, activations, output_grad, *rest)
 
     def full(results, near_up, near_down, *rest):
         room = SIDE * CAP
         far_up, far_down = gather_far(room, place, up_count, down_count, near_up, near_down)
-        return layer(room, place, make_table(room, place, *names)[0], far_up, far_down, *rest)
+        return layer(room, place, make_table(room, place, *names), far_up, far_down, *rest)
 
     return lax.cond(
         crowded, full, lambda results, *unused: results, results, near_up, near_down, wide[0], wide[1], *rest

time: 185 us -> 185 us (level); the launches traced: 182 us -> 184 us
  waiting for transfers between devices: 70.6 us -> 58.8 us
  starting transfers between devices: 45.1 us -> 52.7 us
  Pallas kernels: 37.9 us -> 41.8 us
    ppermute x32, waiting for transfers between devices: 65.4 us -> 52.9 us  [along(): return lambda array, step: lax.ppermute(array, axis, shift(step))]
    ppermute x32, starting transfers between devices: 38.3 us -> 46.2 us  [along(): return lambda array, step: lax.ppermute(array, axis, shift(step))]
    pallas_call x1, Pallas kernels: 31.1 us -> 33.8 us  [layer(): call(main, [jax.ShapeDtypeStruct((tokens, width), jnp.bfloat16)] + parts...]
    pallas_call x1 -> x2, Pallas kernels: 2.81 us -> 4.08 us  [the longest x1 3 us: make_table(): call(kernel, outs, [S] * 7 + [V] * len(held), [S], [], 'table', 3)]
    unnamed x76 -> x74, local copies, waits for them, and re-layouts: 7.79 us -> 8.04 us
  transfers between devices with their start and end apart: 36 -> 36, of which waited for: 22 -> 18; matrix products, arithmetic and copies ran while one was open for 1% -> 2% of each run, Pallas kernels for 3% -> 4%
where the time goes in v4:
time: 185 us; the launch traced here: 184 us
  waiting for transfers between devices  58.8 us (32%)
  starting transfers between devices  52.7 us (28%)
  Pallas kernels  41.8 us (23%)
  between operations  17.1 us (9%)
  local copies, waits for them, and re-layouts  9.73 us (5%)
  other arithmetic  3.07 us (2%)
    ppermute x32, waiting for transfers between devices, along(): return lambda array, step: lax.ppermute(array, axis, shift(step))  52.9 us
    ppermute x32, starting transfers between devices, along(): return lambda array, step: lax.ppermute(array, axis, shift(step))  46.2 us
    pallas_call x1, Pallas kernels, layer(): call(main, [jax.ShapeDtypeStruct((tokens, width), jnp.bfloat16)] + parts...  33.8 us
    unnamed x74, local copies, waits for them, and re-layouts  8.04 us
    ppermute x3, starting transfers between devices, moved(): return lax.ppermute(flag, 'tensor', pairs)  6.56 us
    ppermute x3, waiting for transfers between devices, moved(): return lax.ppermute(flag, 'tensor', pairs)  5.81 us
  transfers between devices with their start and end apart: 36, of which 18 were waited for; matrix products, arithmetic and copies ran while one was open for 2% of the time, Pallas kernels for 4%

profile of v4, /device:TPU:0, one launch (start us, length us, event | category | flops | bytes accessed | tf_op | source)
XLA Modules:
  0.0 184.2 jit_solution(4277799695235663323)
XLA Ops:
  7.2 1.1 bitcast_multiply_fusion.refs_8_
  8.3 3.2 %collective-permute-start.30 = (bf16[12,128,128]{2,1,0:T(8,128)(2,1)S(1)}, bf16[12,128,128]{2,1,0:T(8,128)(2,1)S(1)}, u32[]{:S(2)}, u32[]{:S(2)}) collective-permute-start(bf16[12,128,128]{2,1,0:T(8,128)(2,1)S(1)} %bitcast_multiply_fusion.refs_8_), channel_id=1, source_target_pairs={{0,96},{8,104},{16,112},{24,120},{32,0},{40,8},{48,16},{56,24},{64... | collective-permute-start | bytes 1179656 | tf_op jit(solution)/shard_map/ppermute | solution.py:43
  11.5 1.1 bitcast_multiply_fusion.1.refs_3_
  12.6 2.8 %collective-permute-start.26 = (bf16[12,128,128]{2,1,0:T(8,128)(2,1)S(1)}, bf16[12,128,128]{2,1,0:T(8,128)(2,1)S(1)}, u32[]{:S(2)}, u32[]{:S(2)}) collective-permute-start(bf16[12,128,128]{2,1,0:T(8,128)(2,1)S(1)} %bitcast_multiply_fusion.1.refs_3_), channel_id=1, source_target_pairs={{0,24},{8,0},{16,8},{24,16},{32,56},{40,32},{48,40},{56,48},{64,88... | collective-permute-start | bytes 1179656 | tf_op jit(solution)/shard_map/ppermute | solution.py:43
  15.4 4.4 %collective-permute-done.30.refs_12_ = bf16[12,128,128]{2,1,0:T(8,128)(2,1)S(1)} collective-permute-done((bf16[12,128,128]{2,1,0:T(8,128)(2,1)S(1)}, bf16[12,128,128]{2,1,0:T(8,128)(2,1)S(1)}, u32[]{:S(2)}, u32[]{:S(2)}) %collective-permute-start.30) | collective-permute-done | bytes 393248 | tf_op jit(solution)/shard_map/ppermute | solution.py:43
  19.9 3.8 %collective-permute-start.31 = (bf16[6,128,128]{2,1,0:T(8,128)(2,1)S(1)}, bf16[6,128,128]{2,1,0:T(8,128)(2,1)S(1)}, u32[]{:S(2)}, u32[]{:S(2)}) collective-permute-start(bf16[6,128,128]{2,1,0:T(8,128)(2,1)S(1)} %slice.115), channel_id=1, source_target_pairs={{0,96},{8,104},{16,112},{24,120},{32,0},{40,8},{48,16},{56,24},{64... | collective-permute-start | bytes 589832 | tf_op jit(solution)/shard_map/ppermute | solution.py:43
  23.8 0.8 slice.113
  24.5 3.4 %collective-permute-start.27 = (bf16[6,128,128]{2,1,0:T(8,128)(2,1)}, bf16[6,128,128]{2,1,0:T(8,128)(2,1)S(1)}, u32[]{:S(2)}, u32[]{:S(2)}) collective-permute-start(bf16[6,128,128]{2,1,0:T(8,128)(2,1)} %slice.113), channel_id=1, source_target_pairs={{0,24},{8,0},{16,8},{24,16},{32,56},{40,32},{48,40},{56,48},{64,88... | collective-permute-start | bytes 589832 | tf_op jit(solution)/shard_map/ppermute | solution.py:43
  28.0 0.8 slice.112
  28.7 1.1 crowd.1
  30.6 0.8 collective-permute-done.27.refs_6_
  31.5 4.4 %collective-permute-done.25.refs_5_ = bf16[6,128,128]{2,1,0:T(8,128)(2,1)S(1)} collective-permute-done((bf16[6,128,128]{2,1,0:T(8,128)(2,1)}, bf16[6,128,128]{2,1,0:T(8,128)(2,1)S(1)}, u32[]{:S(2)}, u32[]{:S(2)}) %collective-permute-start.25) | collective-permute-done | bytes 196640 | tf_op jit(solution)/shard_map/ppermute | solution.py:43
  35.8 0.9 pack.3
  36.8 3.0 %collective-permute-start.33 = (bf16[30,128,128]{2,1,0:T(8,128)(2,1)S(1)}, bf16[30,128,128]{2,1,0:T(8,128)(2,1)S(1)}, u32[]{:S(2)}, u32[]{:S(2)}) collective-permute-start(bf16[30,128,128]{2,1,0:T(8,128)(2,1)S(1)} %get-tuple-element.140.refs_4_), channel_id=1, source_target_pairs={{0,96},{8,104},{16,112},{24,120},{32,0},{40,8},{48,16},{56,24},{64... | collective-permute-start | bytes 2949128 | tf_op jit(solution)/shard_map/ppermute | solution.py:43
  39.8 2.0 %collective-permute-start.34 = (bf16[30,128,128]{2,1,0:T(8,128)(2,1)S(1)}, bf16[30,128,128]{2,1,0:T(8,128)(2,1)S(1)}, u32[]{:S(2)}, u32[]{:S(2)}) collective-permute-start(bf16[30,128,128]{2,1,0:T(8,128)(2,1)S(1)} %get-tuple-element.141.refs_9_), channel_id=1, source_target_pairs={{0,8},{8,16},{16,24},{24,0},{32,40},{40,48},{48,56},{56,32},{64,72... | collective-permute-start | bytes 2949128 | tf_op jit(solution)/shard_map/ppermute | solution.py:43
  41.8 1.4 collective-permute-done.36
  44.4 3.3 %collective-permute-start.37 = (s32[1]{0:T(128)}, s32[1]{0:T(128)}, u32[]{:S(2)}, u32[]{:S(2)}) collective-permute-start(s32[1]{0:T(128)} %max.9), channel_id=1, source_target_pairs={{0,2},{1,3},{2,4},{3,5},{4,6},{5,7},{6,0},{7,1},{8,10},{9,11},{10,... | collective-permute-start | bytes 20 | tf_op jit(solution)/shard_map/ppermute | solution.py:55
  47.7 2.4 %collective-permute-done.37 = s32[1]{0:T(128)} collective-permute-done((s32[1]{0:T(128)}, s32[1]{0:T(128)}, u32[]{:S(2)}, u32[]{:S(2)}) %collective-permute-start.37) | collective-permute-done | bytes 36 | tf_op jit(solution)/shard_map/ppermute | solution.py:55
  50.7 3.2 %collective-permute-start.38 = (s32[1]{0:T(128)}, s32[1]{0:T(128)}, u32[]{:S(2)}, u32[]{:S(2)}) collective-permute-start(s32[1]{0:T(128)} %max.10), channel_id=1, source_target_pairs={{0,4},{1,5},{2,6},{3,7},{4,0},{5,1},{6,2},{7,3},{8,12},{9,13},{10,... | collective-permute-start | bytes 20 | tf_op jit(solution)/shard_map/ppermute | solution.py:55
  54.0 2.0 %collective-permute-done.38 = s32[1]{0:T(128)} collective-permute-done((s32[1]{0:T(128)}, s32[1]{0:T(128)}, u32[]{:S(2)}, u32[]{:S(2)}) %collective-permute-start.38) | collective-permute-done | bytes 36 | tf_op jit(solution)/shard_map/ppermute | solution.py:55
  56.5 1.4 collective-permute-done.33.refs_8_
  57.9 3.4 %collective-permute-done.32.refs_5_ = bf16[30,128,128]{2,1,0:T(8,128)(2,1)S(1)} collective-permute-done((bf16[30,128,128]{2,1,0:T(8,128)(2,1)S(1)}, bf16[30,128,128]{2,1,0:T(8,128)(2,1)S(1)}, u32[]{:S(2)}, u32[]{:S(2)}) %collective-permute-start.32) | collective-permute-done | bytes 983072 | tf_op jit(solution)/shard_map/ppermute | solution.py:43
  62.3 2.0 %collective-permute-start.41 = (bf16[15,128,128]{2,1,0:T(8,128)(2,1)S(1)}, bf16[15,128,128]{2,1,0:T(8,128)(2,1)S(1)}, u32[]{:S(2)}, u32[]{:S(2)}) collective-permute-start(bf16[15,128,128]{2,1,0:T(8,128)(2,1)S(1)} %slice.90), channel_id=1, source_target_pairs={{0,8},{8,16},{16,24},{24,0},{32,40},{40,48},{48,56},{56,32},{64,72... | collective-permute-start | bytes 1474568 | tf_op jit(solution)/shard_map/ppermute | solution.py:43
  64.3 2.4 %collective-permute-start.40 = (bf16[15,128,128]{2,1,0:T(8,128)(2,1)S(1)}, bf16[15,128,128]{2,1,0:T(8,128)(2,1)S(1)}, u32[]{:S(2)}, u32[]{:S(2)}) collective-permute-start(bf16[15,128,128]{2,1,0:T(8,128)(2,1)S(1)} %slice.89), channel_id=1, source_target_pairs={{0,96},{8,104},{16,112},{24,120},{32,0},{40,8},{48,16},{56,24},{64... | collective-permute-start | bytes 1474568 | tf_op jit(solution)/shard_map/ppermute | solution.py:43
  66.7 3.1 %copy-done = bf16[256,14336]{1,0:T(8,128)(2,1)S(1)} copy-done((bf16[256,14336]{1,0:T(8,128)(2,1)S(1)}, bf16[256,14336]{1,0:T(8,128)(2,1)}, u32[]{:S(2)}) %copy-start) | copy-done | bytes 7340056
  69.8 3.1 %copy-done.1 = bf16[256,14336]{1,0:T(8,128)(2,1)S(1)} copy-done((bf16[256,14336]{1,0:T(8,128)(2,1)S(1)}, bf16[256,14336]{1,0:T(8,128)(2,1)}, u32[]{:S(2)}) %copy-start.1) | copy-done | bytes 7340056
  72.8 3.0 %table.3.refs_1_ = s32[8,192]{1,0:T(8,128)S(1)} custom-call(s32[4]{0:T(128)S(1)} %pad_add_fusion.refs_0_.place, s32[16]{0:T(128)S(1)} %bitcast.23, s32[192]{0:T(256)S(1)} %bitcast.33, s32[192]{0:T(256)S(1)} %bitcast.35, s32[16]{0:T(128)S(1)} %bitcast.29, s32[192]{0:T(256)S(1)} %bitcast.37, s32[192]{0:T(256)S(1)} %bitcast.39, bf16[256,14336]{1,0:T(8,128)(2,1)S(1)} %copy-done, ...), custom_call_target="tpu_custom_call" | custom-call | bytes 9000000 | tf_op jit(solution)/shard_map/table/pallas_call | solution.py:184
  75.9 0.7 collective-permute-done.39.refs_6_
  77.0 0.8 copy-done.42
  77.8 33.8 %main.3 = (bf16[256,14336]{1,0:T(8,128)(2,1)}, bf16[30,128,128]{2,1,0:T(8,128)(2,1)}, bf16[30,128,128]{2,1,0:T(8,128)(2,1)}, bf16[30,128,128]{2,1,0:T(8,128)(2,1...) custom-call(s32[4]{0:T(128)S(1)} %pad_add_fusion.refs_0_.place, ...), custom_call_target="tpu_custom_call" | custom-call | bytes 120000000 | tf_op jit(solution)/shard_map/main/pallas_call | solution.py:387
  111.5 3.2 %collective-permute-start.43 = (bf16[30,128,128]{2,1,0:T(8,128)(2,1)}, bf16[30,128,128]{2,1,0:T(8,128)(2,1)S(1)}, u32[]{:S(2)}, u32[]{:S(2)}) collective-permute-start(bf16[30,128,128]{2,1,0:T(8,128)(2,1)} %get-tuple-element.149), channel_id=1, source_target_pairs={{0,96},{8,104},{16,112},{24,120},{32,0},{40,8},{48,16},{56,24},{64... | collective-permute-start | bytes 2949128 | tf_op jit(solution)/shard_map/ppermute | solution.py:43
  114.8 1.5 collective-permute-start.47
  116.8 16.3 %collective-permute-done.43.refs_4_ = bf16[30,128,128]{2,1,0:T(8,128)(2,1)S(1)} collective-permute-done((bf16[30,128,128]{2,1,0:T(8,128)(2,1)}, bf16[30,128,128]{2,1,0:T(8,128)(2,1)S(1)}, u32[]{:S(2)}, u32[]{:S(2)}) %collective-permute-start.43) | collective-permute-done | bytes 983072 | tf_op jit(solution)/shard_map/ppermute | solution.py:43
  133.3 3.5 %collective-permute-start.45 = (bf16[15,128,128]{2,1,0:T(8,128)(2,1)S(1)}, bf16[15,128,128]{2,1,0:T(8,128)(2,1)S(1)}, u32[]{:S(2)}, u32[]{:S(2)}) collective-permute-start(bf16[15,128,128]{2,1,0:T(8,128)(2,1)S(1)} %add_convert_fusion.11), channel_id=1, source_target_pairs={{0,96},{8,104},{16,112},{24,120},{32,0},{40,8},{48,16},{56,24},{64... | collective-permute-start | bytes 1474568 | tf_op jit(solution)/shard_map/ppermute | solution.py:43
  137.2 1.6 collective-permute-start.49
  139.6 3.6 %collective-permute-done.45.refs_6_ = bf16[15,128,128]{2,1,0:T(8,128)(2,1)S(1)} collective-permute-done((bf16[15,128,128]{2,1,0:T(8,128)(2,1)S(1)}, bf16[15,128,128]{2,1,0:T(8,128)(2,1)S(1)}, u32[]{:S(2)}, u32[]{:S(2)}) %collective-permute-start.45) | collective-permute-done | bytes 491552 | tf_op jit(solution)/shard_map/ppermute | solution.py:43
  143.2 3.9 %collective-permute-done.46.refs_7_ = bf16[15,128,128]{2,1,0:T(8,128)(2,1)S(1)} collective-permute-done((bf16[15,128,128]{2,1,0:T(8,128)(2,1)S(1)}, bf16[15,128,128]{2,1,0:T(8,128)(2,1)S(1)}, u32[]{:S(2)}, u32[]{:S(2)}) %collective-permute-start.46) | collective-permute-done | bytes 491552 | tf_op jit(solution)/shard_map/ppermute | solution.py:43
  147.1 4.1 %collective-permute-done.50.refs_12_ = bf16[15,128,128]{2,1,0:T(8,128)(2,1)S(1)} collective-permute-done((bf16[15,128,128]{2,1,0:T(8,128)(2,1)S(1)}, bf16[15,128,128]{2,1,0:T(8,128)(2,1)S(1)}, u32[]{:S(2)}, u32[]{:S(2)}) %collective-permute-start.50) | collective-permute-done | bytes 491552 | tf_op jit(solution)/shard_map/ppermute | solution.py:43
  151.2 1.4 unpack.3
  152.7 2.0 %collective-permute-start.52 = (bf16[12,128,128]{2,1,0:T(8,128)(2,1)S(1)}, bf16[12,128,128]{2,1,0:T(8,128)(2,1)S(1)}, u32[]{:S(2)}, u32[]{:S(2)}) collective-permute-start(bf16[12,128,128]{2,1,0:T(8,128)(2,1)S(1)} %get-tuple-element.160), channel_id=1, source_target_pairs={{0,8},{8,16},{16,24},{24,0},{32,40},{40,48},{48,56},{56,32},{64,72... | collective-permute-start | bytes 1179656 | tf_op jit(solution)/shard_map/ppermute | solution.py:43
  154.8 3.6 %collective-permute-start.55 = (bf16[12,128,128]{2,1,0:T(8,128)(2,1)S(1)}, bf16[12,128,128]{2,1,0:T(8,128)(2,1)S(1)}, u32[]{:S(2)}, u32[]{:S(2)}) collective-permute-start(bf16[12,128,128]{2,1,0:T(8,128)(2,1)S(1)} %get-tuple-element.164), channel_id=1, source_target_pairs={{0,96},{8,104},{16,112},{24,120},{32,0},{40,8},{48,16},{56,24},{64... | collective-permute-start | bytes 1179656 | tf_op jit(solution)/shard_map/ppermute | solution.py:43
  158.4 2.1 %collective-permute-done.51.refs_1_ = bf16[12,128,128]{2,1,0:T(8,128)(2,1)S(1)} collective-permute-done((bf16[12,128,128]{2,1,0:T(8,128)(2,1)S(1)}, bf16[12,128,128]{2,1,0:T(8,128)(2,1)S(1)}, u32[]{:S(2)}, u32[]{:S(2)}) %collective-permute-start.51) | collective-permute-done | bytes 393248 | tf_op jit(solution)/shard_map/ppermute | solution.py:43
  160.6 3.1 %collective-permute-start.53 = (bf16[6,128,128]{2,1,0:T(8,128)(2,1)S(1)}, bf16[6,128,128]{2,1,0:T(8,128)(2,1)S(1)}, u32[]{:S(2)}, u32[]{:S(2)}) collective-permute-start(bf16[6,128,128]{2,1,0:T(8,128)(2,1)S(1)} %add_convert_fusion.15), channel_id=1, source_target_pairs={{0,24},{8,0},{16,8},{24,16},{32,56},{40,32},{48,40},{56,48},{64,88... | collective-permute-start | bytes 589832 | tf_op jit(solution)/shard_map/ppermute | solution.py:43
  164.0 3.5 %collective-permute-start.57 = (bf16[6,128,128]{2,1,0:T(8,128)(2,1)S(1)}, bf16[6,128,128]{2,1,0:T(8,128)(2,1)S(1)}, u32[]{:S(2)}, u32[]{:S(2)}) collective-permute-start(bf16[6,128,128]{2,1,0:T(8,128)(2,1)S(1)} %add_convert_fusion.13), channel_id=1, source_target_pairs={{0,96},{8,104},{16,112},{24,120},{32,0},{40,8},{48,16},{56,24},{64... | collective-permute-start | bytes 589832 | tf_op jit(solution)/shard_map/ppermute | solution.py:43
  167.7 3.1 %collective-permute-done.54.refs_4_ = bf16[6,128,128]{2,1,0:T(8,128)(2,1)S(1)} collective-permute-done((bf16[6,128,128]{2,1,0:T(8,128)(2,1)S(1)}, bf16[6,128,128]{2,1,0:T(8,128)(2,1)S(1)}, u32[]{:S(2)}, u32[]{:S(2)}) %collective-permute-start.54) | collective-permute-done | bytes 196640 | tf_op jit(solution)/shard_map/ppermute | solution.py:43
  170.8 3.7 %collective-permute-done.58.refs_9_ = bf16[6,128,128]{2,1,0:T(8,128)(2,1)S(1)} collective-permute-done((bf16[6,128,128]{2,1,0:T(8,128)(2,1)S(1)}, bf16[6,128,128]{2,1,0:T(8,128)(2,1)S(1)}, u32[]{:S(2)}, u32[]{:S(2)}) %collective-permute-start.58) | collective-permute-done | bytes 196640 | tf_op jit(solution)/shard_map/ppermute | solution.py:43
  174.5 1.7 finish.3
  176.4 1.0 conditional.1
  (126 shorter events, 4.5 us)
Async XLA Ops:
  7.2 169.1 %reduce-scatter.5.cloned.1.call-start = ((), (), s32[]{:S(2)}) async-start(), calls=%async_computation.3 | async-start | bytes 8257536 | tf_op jit(solution)/shard_map/reduce_scatter | solution.py:397
  7.2 21.5 %copy-start.43 = (s32[1,16]{1,0:T(1,128)S(1)}, s32[1,16]{1,0:T(1,128)}, u32[]{:S(2)}) copy-start(s32[1,16]{1,0:T(1,128)} %param.24) | copy-start | bytes 196
  7.2 21.5 %copy-start.44 = (s32[1,16]{1,0:T(1,128)S(1)}, s32[1,16]{1,0:T(1,128)}, u32[]{:S(2)}) copy-start(s32[1,16]{1,0:T(1,128)} %param.25) | copy-start | bytes 196
  8.3 11.5 %collective-permute-start.30 = (bf16[12,128,128]{2,1,0:T(8,128)(2,1)S(1)}, bf16[12,128,128]{2,1,0:T(8,128)(2,1)S(1)}, u32[]{:S(2)}, u32[]{:S(2)}) collective-permute-start(bf16[12,128,128]{2,1,0:T(8,128)(2,1)S(1)} %bitcast_multiply_fusion.refs_8_), channel_id=1, source_target_pairs={{0,96},{8,104},{16,112},{24,120},{32,0},{40,8},{48,16},{56,24},{64... | collective-permute-start | bytes 1179656 | tf_op jit(solution)/shard_map/ppermute | solution.py:43
  11.5 12.2 %collective-permute-start.28 = (bf16[12,128,128]{2,1,0:T(8,128)(2,1)S(1)}, bf16[12,128,128]{2,1,0:T(8,128)(2,1)S(1)}, u32[]{:S(2)}, u32[]{:S(2)}) collective-permute-start(bf16[12,128,128]{2,1,0:T(8,128)(2,1)S(1)} %bitcast_multiply_fusion.refs_8_), channel_id=1, source_target_pairs={{0,32},{8,40},{16,48},{24,56},{32,64},{40,72},{48,80},{56,88},{64,... | collective-permute-start | bytes 1179656 | tf_op jit(solution)/shard_map/ppermute | solution.py:43
  12.6 11.2 %collective-permute-start.26 = (bf16[12,128,128]{2,1,0:T(8,128)(2,1)S(1)}, bf16[12,128,128]{2,1,0:T(8,128)(2,1)S(1)}, u32[]{:S(2)}, u32[]{:S(2)}) collective-permute-start(bf16[12,128,128]{2,1,0:T(8,128)(2,1)S(1)} %bitcast_multiply_fusion.1.refs_3_), channel_id=1, source_target_pairs={{0,24},{8,0},{16,8},{24,16},{32,56},{40,32},{48,40},{56,48},{64,88... | collective-permute-start | bytes 1179656 | tf_op jit(solution)/shard_map/ppermute | solution.py:43
  15.4 12.5 %collective-permute-start.24 = (bf16[12,128,128]{2,1,0:T(8,128)(2,1)S(1)}, bf16[12,128,128]{2,1,0:T(8,128)(2,1)S(1)}, u32[]{:S(2)}, u32[]{:S(2)}) collective-permute-start(bf16[12,128,128]{2,1,0:T(8,128)(2,1)S(1)} %bitcast_multiply_fusion.1.refs_3_), channel_id=1, source_target_pairs={{0,8},{8,16},{16,24},{24,0},{32,40},{40,48},{48,56},{56,32},{64,72... | collective-permute-start | bytes 1179656 | tf_op jit(solution)/shard_map/ppermute | solution.py:43
  19.9 10.0 %collective-permute-start.31 = (bf16[6,128,128]{2,1,0:T(8,128)(2,1)S(1)}, bf16[6,128,128]{2,1,0:T(8,128)(2,1)S(1)}, u32[]{:S(2)}, u32[]{:S(2)}) collective-permute-start(bf16[6,128,128]{2,1,0:T(8,128)(2,1)S(1)} %slice.115), channel_id=1, source_target_pairs={{0,96},{8,104},{16,112},{24,120},{32,0},{40,8},{48,16},{56,24},{64... | collective-permute-start | bytes 589832 | tf_op jit(solution)/shard_map/ppermute | solution.py:43
  23.7 6.9 %collective-permute-start.29 = (bf16[6,128,128]{2,1,0:T(8,128)(2,1)S(1)}, bf16[6,128,128]{2,1,0:T(8,128)(2,1)S(1)}, u32[]{:S(2)}, u32[]{:S(2)}) collective-permute-start(bf16[6,128,128]{2,1,0:T(8,128)(2,1)S(1)} %slice.114), channel_id=1, source_target_pairs={{0,32},{8,40},{16,48},{24,56},{32,64},{40,72},{48,80},{56,88},{64,... | collective-permute-start | bytes 589832 | tf_op jit(solution)/shard_map/ppermute | solution.py:43
  23.8 12.9 %copy-start.15 = (bf16[12,128,128]{2,1,0:T(8,128)(2,1)}, bf16[12,128,128]{2,1,0:T(8,128)(2,1)S(1)}, u32[]{:S(2)}) copy-start(bf16[12,128,128]{2,1,0:T(8,128)(2,1)S(1)} %collective-permute-done.26.refs_7_) | copy-start | bytes 1179652
  24.5 6.9 %collective-permute-start.27 = (bf16[6,128,128]{2,1,0:T(8,128)(2,1)}, bf16[6,128,128]{2,1,0:T(8,128)(2,1)S(1)}, u32[]{:S(2)}, u32[]{:S(2)}) collective-permute-start(bf16[6,128,128]{2,1,0:T(8,128)(2,1)} %slice.113), channel_id=1, source_target_pairs={{0,24},{8,0},{16,8},{24,16},{32,56},{40,32},{48,40},{56,48},{64,88... | collective-permute-start | bytes 589832 | tf_op jit(solution)/shard_map/ppermute | solution.py:43
  28.0 8.8 %copy-start.17 = (bf16[12,128,128]{2,1,0:T(8,128)(2,1)}, bf16[12,128,128]{2,1,0:T(8,128)(2,1)S(1)}, u32[]{:S(2)}) copy-start(bf16[12,128,128]{2,1,0:T(8,128)(2,1)S(1)} %collective-permute-done.24.refs_4_) | copy-start | bytes 1179652
  28.7 7.1 %collective-permute-start.25 = (bf16[6,128,128]{2,1,0:T(8,128)(2,1)}, bf16[6,128,128]{2,1,0:T(8,128)(2,1)S(1)}, u32[]{:S(2)}, u32[]{:S(2)}) collective-permute-start(bf16[6,128,128]{2,1,0:T(8,128)(2,1)} %slice.112), channel_id=1, source_target_pairs={{0,8},{8,16},{16,24},{24,0},{32,40},{40,48},{48,56},{56,32},{64,72... | collective-permute-start | bytes 589832 | tf_op jit(solution)/shard_map/ppermute | solution.py:43
  36.8 24.8 %copy-start.6 = (bf16[30,128,128]{2,1,0:T(8,128)(2,1)}, bf16[30,128,128]{2,1,0:T(8,128)(2,1)S(1)}, u32[]{:S(2)}) copy-start(bf16[30,128,128]{2,1,0:T(8,128)(2,1)S(1)} %get-tuple-element.140.refs_4_) | copy-start | bytes 2949124
  36.8 24.8 %copy-start.7 = (bf16[30,128,128]{2,1,0:T(8,128)(2,1)}, bf16[30,128,128]{2,1,0:T(8,128)(2,1)S(1)}, u32[]{:S(2)}) copy-start(bf16[30,128,128]{2,1,0:T(8,128)(2,1)S(1)} %get-tuple-element.141.refs_9_) | copy-start | bytes 2949124
  36.8 21.1 %collective-permute-start.33 = (bf16[30,128,128]{2,1,0:T(8,128)(2,1)S(1)}, bf16[30,128,128]{2,1,0:T(8,128)(2,1)S(1)}, u32[]{:S(2)}, u32[]{:S(2)}) collective-permute-start(bf16[30,128,128]{2,1,0:T(8,128)(2,1)S(1)} %get-tuple-element.140.refs_4_), channel_id=1, source_target_pairs={{0,96},{8,104},{16,112},{24,120},{32,0},{40,8},{48,16},{56,24},{64... | collective-permute-start | bytes 2949128 | tf_op jit(solution)/shard_map/ppermute | solution.py:43
  39.8 21.5 %collective-permute-start.32 = (bf16[30,128,128]{2,1,0:T(8,128)(2,1)S(1)}, bf16[30,128,128]{2,1,0:T(8,128)(2,1)S(1)}, u32[]{:S(2)}, u32[]{:S(2)}) collective-permute-start(bf16[30,128,128]{2,1,0:T(8,128)(2,1)S(1)} %get-tuple-element.140.refs_4_), channel_id=1, source_target_pairs={{0,32},{8,40},{16,48},{24,56},{32,64},{40,72},{48,80},{56,88},{64,... | collective-permute-start | bytes 2949128 | tf_op jit(solution)/shard_map/ppermute | solution.py:43
  39.8 21.5 %collective-permute-start.35 = (bf16[30,128,128]{2,1,0:T(8,128)(2,1)S(1)}, bf16[30,128,128]{2,1,0:T(8,128)(2,1)S(1)}, u32[]{:S(2)}, u32[]{:S(2)}) collective-permute-start(bf16[30,128,128]{2,1,0:T(8,128)(2,1)S(1)} %get-tuple-element.141.refs_9_), channel_id=1, source_target_pairs={{0,24},{8,0},{16,8},{24,16},{32,56},{40,32},{48,40},{56,48},{64,88... | collective-permute-start | bytes 2949128 | tf_op jit(solution)/shard_map/ppermute | solution.py:43
  39.8 21.5 %collective-permute-start.34 = (bf16[30,128,128]{2,1,0:T(8,128)(2,1)S(1)}, bf16[30,128,128]{2,1,0:T(8,128)(2,1)S(1)}, u32[]{:S(2)}, u32[]{:S(2)}) collective-permute-start(bf16[30,128,128]{2,1,0:T(8,128)(2,1)S(1)} %get-tuple-element.141.refs_9_), channel_id=1, source_target_pairs={{0,8},{8,16},{16,24},{24,0},{32,40},{40,48},{48,56},{56,32},{64,72... | collective-permute-start | bytes 2949128 | tf_op jit(solution)/shard_map/ppermute | solution.py:43
  41.8 1.4 collective-permute-start.36
  44.4 5.8 %collective-permute-start.37 = (s32[1]{0:T(128)}, s32[1]{0:T(128)}, u32[]{:S(2)}, u32[]{:S(2)}) collective-permute-start(s32[1]{0:T(128)} %max.9), channel_id=1, source_target_pairs={{0,2},{1,3},{2,4},{3,5},{4,6},{5,7},{6,0},{7,1},{8,10},{9,11},{10,... | collective-permute-start | bytes 20 | tf_op jit(solution)/shard_map/ppermute | solution.py:55
  50.7 5.2 %collective-permute-start.38 = (s32[1]{0:T(128)}, s32[1]{0:T(128)}, u32[]{:S(2)}, u32[]{:S(2)}) collective-permute-start(s32[1]{0:T(128)} %max.10), channel_id=1, source_target_pairs={{0,4},{1,5},{2,6},{3,7},{4,0},{5,1},{6,2},{7,3},{8,12},{9,13},{10,... | collective-permute-start | bytes 20 | tf_op jit(solution)/shard_map/ppermute | solution.py:55
  61.3 14.5 %copy-start.21 = (bf16[30,128,128]{2,1,0:T(8,128)(2,1)}, bf16[30,128,128]{2,1,0:T(8,128)(2,1)S(1)}, u32[]{:S(2)}) copy-start(bf16[30,128,128]{2,1,0:T(8,128)(2,1)S(1)} %collective-permute-done.35.refs_13_) | copy-start | bytes 2949124
  61.3 14.5 %copy-start.22 = (bf16[30,128,128]{2,1,0:T(8,128)(2,1)}, bf16[30,128,128]{2,1,0:T(8,128)(2,1)S(1)}, u32[]{:S(2)}) copy-start(bf16[30,128,128]{2,1,0:T(8,128)(2,1)S(1)} %collective-permute-done.34.refs_10_) | copy-start | bytes 2949124
  62.3 13.6 %collective-permute-start.42 = (bf16[15,128,128]{2,1,0:T(8,128)(2,1)S(1)}, bf16[15,128,128]{2,1,0:T(8,128)(2,1)S(1)}, u32[]{:S(2)}, u32[]{:S(2)}) collective-permute-start(bf16[15,128,128]{2,1,0:T(8,128)(2,1)S(1)} %slice.91), channel_id=1, source_target_pairs={{0,24},{8,0},{16,8},{24,16},{32,56},{40,32},{48,40},{56,48},{64,88... | collective-permute-start | bytes 1474568 | tf_op jit(solution)/shard_map/ppermute | solution.py:43
  62.3 13.6 %collective-permute-start.41 = (bf16[15,128,128]{2,1,0:T(8,128)(2,1)S(1)}, bf16[15,128,128]{2,1,0:T(8,128)(2,1)S(1)}, u32[]{:S(2)}, u32[]{:S(2)}) collective-permute-start(bf16[15,128,128]{2,1,0:T(8,128)(2,1)S(1)} %slice.90), channel_id=1, source_target_pairs={{0,8},{8,16},{16,24},{24,0},{32,40},{40,48},{48,56},{56,32},{64,72... | collective-permute-start | bytes 1474568 | tf_op jit(solution)/shard_map/ppermute | solution.py:43
  64.3 11.6 %collective-permute-start.40 = (bf16[15,128,128]{2,1,0:T(8,128)(2,1)S(1)}, bf16[15,128,128]{2,1,0:T(8,128)(2,1)S(1)}, u32[]{:S(2)}, u32[]{:S(2)}) collective-permute-start(bf16[15,128,128]{2,1,0:T(8,128)(2,1)S(1)} %slice.89), channel_id=1, source_target_pairs={{0,96},{8,104},{16,112},{24,120},{32,0},{40,8},{48,16},{56,24},{64... | collective-permute-start | bytes 1474568 | tf_op jit(solution)/shard_map/ppermute | solution.py:43
  66.6 10.0 %collective-permute-start.39 = (bf16[15,128,128]{2,1,0:T(8,128)(2,1)S(1)}, bf16[15,128,128]{2,1,0:T(8,128)(2,1)S(1)}, u32[]{:S(2)}, u32[]{:S(2)}) collective-permute-start(bf16[15,128,128]{2,1,0:T(8,128)(2,1)S(1)} %slice.88), channel_id=1, source_target_pairs={{0,32},{8,40},{16,48},{24,56},{32,64},{40,72},{48,80},{56,88},{64,... | collective-permute-start | bytes 1474568 | tf_op jit(solution)/shard_map/ppermute | solution.py:43
  111.5 21.6 %collective-permute-start.43 = (bf16[30,128,128]{2,1,0:T(8,128)(2,1)}, bf16[30,128,128]{2,1,0:T(8,128)(2,1)S(1)}, u32[]{:S(2)}, u32[]{:S(2)}) collective-permute-start(bf16[30,128,128]{2,1,0:T(8,128)(2,1)} %get-tuple-element.149), channel_id=1, source_target_pairs={{0,96},{8,104},{16,112},{24,120},{32,0},{40,8},{48,16},{56,24},{64... | collective-permute-start | bytes 2949128 | tf_op jit(solution)/shard_map/ppermute | solution.py:43
  114.8 22.0 %collective-permute-start.44 = (bf16[30,128,128]{2,1,0:T(8,128)(2,1)}, bf16[30,128,128]{2,1,0:T(8,128)(2,1)S(1)}, u32[]{:S(2)}, u32[]{:S(2)}) collective-permute-start(bf16[30,128,128]{2,1,0:T(8,128)(2,1)} %get-tuple-element.150), channel_id=1, source_target_pairs={{0,32},{8,40},{16,48},{24,56},{32,64},{40,72},{48,80},{56,88},{64,... | collective-permute-start | bytes 2949128 | tf_op jit(solution)/shard_map/ppermute | solution.py:43
  114.8 22.3 %collective-permute-start.47 = (bf16[30,128,128]{2,1,0:T(8,128)(2,1)}, bf16[30,128,128]{2,1,0:T(8,128)(2,1)S(1)}, u32[]{:S(2)}, u32[]{:S(2)}) collective-permute-start(bf16[30,128,128]{2,1,0:T(8,128)(2,1)} %get-tuple-element.154), channel_id=1, source_target_pairs={{0,24},{8,0},{16,8},{24,16},{32,56},{40,32},{48,40},{56,48},{64,88... | collective-permute-start | bytes 2949128 | tf_op jit(solution)/shard_map/ppermute | solution.py:43
  116.3 22.5 %collective-permute-start.48 = (bf16[30,128,128]{2,1,0:T(8,128)(2,1)}, bf16[30,128,128]{2,1,0:T(8,128)(2,1)S(1)}, u32[]{:S(2)}, u32[]{:S(2)}) collective-permute-start(bf16[30,128,128]{2,1,0:T(8,128)(2,1)} %get-tuple-element.155), channel_id=1, source_target_pairs={{0,8},{8,16},{16,24},{24,0},{32,40},{40,48},{48,56},{56,32},{64,72... | collective-permute-start | bytes 2949128 | tf_op jit(solution)/shard_map/ppermute | solution.py:43
  133.3 9.9 %collective-permute-start.45 = (bf16[15,128,128]{2,1,0:T(8,128)(2,1)S(1)}, bf16[15,128,128]{2,1,0:T(8,128)(2,1)S(1)}, u32[]{:S(2)}, u32[]{:S(2)}) collective-permute-start(bf16[15,128,128]{2,1,0:T(8,128)(2,1)S(1)} %add_convert_fusion.11), channel_id=1, source_target_pairs={{0,96},{8,104},{16,112},{24,120},{32,0},{40,8},{48,16},{56,24},{64... | collective-permute-start | bytes 1474568 | tf_op jit(solution)/shard_map/ppermute | solution.py:43
  137.0 14.3 %copy-start.8 = (bf16[30,128,128]{2,1,0:T(8,128)(2,1)S(1)}, bf16[30,128,128]{2,1,0:T(8,128)(2,1)}, u32[]{:S(2)}) copy-start(bf16[30,128,128]{2,1,0:T(8,128)(2,1)} %get-tuple-element.148.refs_3_) | copy-start | bytes 2949124
  137.0 14.3 %copy-start.9 = (bf16[30,128,128]{2,1,0:T(8,128)(2,1)S(1)}, bf16[30,128,128]{2,1,0:T(8,128)(2,1)}, u32[]{:S(2)}) copy-start(bf16[30,128,128]{2,1,0:T(8,128)(2,1)} %get-tuple-element.153.refs_8_) | copy-start | bytes 2949124
  137.0 10.1 %collective-permute-start.46 = (bf16[15,128,128]{2,1,0:T(8,128)(2,1)S(1)}, bf16[15,128,128]{2,1,0:T(8,128)(2,1)S(1)}, u32[]{:S(2)}, u32[]{:S(2)}) collective-permute-start(bf16[15,128,128]{2,1,0:T(8,128)(2,1)S(1)} %add_convert_fusion.10), channel_id=1, source_target_pairs={{0,32},{8,40},{16,48},{24,56},{32,64},{40,72},{48,80},{56,88},{64,... | collective-permute-start | bytes 1474568 | tf_op jit(solution)/shard_map/ppermute | solution.py:43
  137.2 9.9 %collective-permute-start.49 = (bf16[15,128,128]{2,1,0:T(8,128)(2,1)S(1)}, bf16[15,128,128]{2,1,0:T(8,128)(2,1)S(1)}, u32[]{:S(2)}, u32[]{:S(2)}) collective-permute-start(bf16[15,128,128]{2,1,0:T(8,128)(2,1)S(1)} %add_convert_fusion.9), channel_id=1, source_target_pairs={{0,24},{8,0},{16,8},{24,16},{32,56},{40,32},{48,40},{56,48},{64,88... | collective-permute-start | bytes 1474568 | tf_op jit(solution)/shard_map/ppermute | solution.py:43
  139.0 12.2 %collective-permute-start.50 = (bf16[15,128,128]{2,1,0:T(8,128)(2,1)S(1)}, bf16[15,128,128]{2,1,0:T(8,128)(2,1)S(1)}, u32[]{:S(2)}, u32[]{:S(2)}) collective-permute-start(bf16[15,128,128]{2,1,0:T(8,128)(2,1)S(1)} %add_convert_fusion.8), channel_id=1, source_target_pairs={{0,8},{8,16},{16,24},{24,0},{32,40},{40,48},{48,56},{56,32},{64,72... | collective-permute-start | bytes 1474568 | tf_op jit(solution)/shard_map/ppermute | solution.py:43
  152.6 15.0 %copy-start.52 = (bf16[1,12]{1,0:T(2,128)(2,1)S(1)}, bf16[1,12]{1,0:T(2,128)(2,1)}, u32[]{:S(2)}) copy-start(bf16[1,12]{1,0:T(2,128)(2,1)} %param.19) | copy-start | bytes 76
  152.6 15.0 %copy-start.53 = (bf16[1,12]{1,0:T(2,128)(2,1)S(1)}, bf16[1,12]{1,0:T(2,128)(2,1)}, u32[]{:S(2)}) copy-start(bf16[1,12]{1,0:T(2,128)(2,1)} %param.17) | copy-start | bytes 76
  152.7 7.8 %collective-permute-start.51 = (bf16[12,128,128]{2,1,0:T(8,128)(2,1)S(1)}, bf16[12,128,128]{2,1,0:T(8,128)(2,1)S(1)}, u32[]{:S(2)}, u32[]{:S(2)}) collective-permute-start(bf16[12,128,128]{2,1,0:T(8,128)(2,1)S(1)} %get-tuple-element.159), channel_id=1, source_target_pairs={{0,24},{8,0},{16,8},{24,16},{32,56},{40,32},{48,40},{56,48},{64,88... | collective-permute-start | bytes 1179656 | tf_op jit(solution)/shard_map/ppermute | solution.py:43
  152.7 11.0 %collective-permute-start.52 = (bf16[12,128,128]{2,1,0:T(8,128)(2,1)S(1)}, bf16[12,128,128]{2,1,0:T(8,128)(2,1)S(1)}, u32[]{:S(2)}, u32[]{:S(2)}) collective-permute-start(bf16[12,128,128]{2,1,0:T(8,128)(2,1)S(1)} %get-tuple-element.160), channel_id=1, source_target_pairs={{0,8},{8,16},{16,24},{24,0},{32,40},{40,48},{48,56},{56,32},{64,72... | collective-permute-start | bytes 1179656 | tf_op jit(solution)/shard_map/ppermute | solution.py:43
  154.8 9.2 %collective-permute-start.55 = (bf16[12,128,128]{2,1,0:T(8,128)(2,1)S(1)}, bf16[12,128,128]{2,1,0:T(8,128)(2,1)S(1)}, u32[]{:S(2)}, u32[]{:S(2)}) collective-permute-start(bf16[12,128,128]{2,1,0:T(8,128)(2,1)S(1)} %get-tuple-element.164), channel_id=1, source_target_pairs={{0,96},{8,104},{16,112},{24,120},{32,0},{40,8},{48,16},{56,24},{64... | collective-permute-start | bytes 1179656 | tf_op jit(solution)/shard_map/ppermute | solution.py:43
  158.4 9.1 %collective-permute-start.56 = (bf16[12,128,128]{2,1,0:T(8,128)(2,1)S(1)}, bf16[12,128,128]{2,1,0:T(8,128)(2,1)S(1)}, u32[]{:S(2)}, u32[]{:S(2)}) collective-permute-start(bf16[12,128,128]{2,1,0:T(8,128)(2,1)S(1)} %get-tuple-element.165), channel_id=1, source_target_pairs={{0,32},{8,40},{16,48},{24,56},{32,64},{40,72},{48,80},{56,88},{64,... | collective-permute-start | bytes 1179656 | tf_op jit(solution)/shard_map/ppermute | solution.py:43
  160.6 7.1 %collective-permute-start.53 = (bf16[6,128,128]{2,1,0:T(8,128)(2,1)S(1)}, bf16[6,128,128]{2,1,0:T(8,128)(2,1)S(1)}, u32[]{:S(2)}, u32[]{:S(2)}) collective-permute-start(bf16[6,128,128]{2,1,0:T(8,128)(2,1)S(1)} %add_convert_fusion.15), channel_id=1, source_target_pairs={{0,24},{8,0},{16,8},{24,16},{32,56},{40,32},{48,40},{56,48},{64,88... | collective-permute-start | bytes 589832 | tf_op jit(solution)/shard_map/ppermute | solution.py:43
  163.8 6.9 %collective-permute-start.54 = (bf16[6,128,128]{2,1,0:T(8,128)(2,1)S(1)}, bf16[6,128,128]{2,1,0:T(8,128)(2,1)S(1)}, u32[]{:S(2)}, u32[]{:S(2)}) collective-permute-start(bf16[6,128,128]{2,1,0:T(8,128)(2,1)S(1)} %add_convert_fusion.14), channel_id=1, source_target_pairs={{0,8},{8,16},{16,24},{24,0},{32,40},{40,48},{48,56},{56,32},{64,72... | collective-permute-start | bytes 589832 | tf_op jit(solution)/shard_map/ppermute | solution.py:43
  164.0 6.8 %collective-permute-start.57 = (bf16[6,128,128]{2,1,0:T(8,128)(2,1)S(1)}, bf16[6,128,128]{2,1,0:T(8,128)(2,1)S(1)}, u32[]{:S(2)}, u32[]{:S(2)}) collective-permute-start(bf16[6,128,128]{2,1,0:T(8,128)(2,1)S(1)} %add_convert_fusion.13), channel_id=1, source_target_pairs={{0,96},{8,104},{16,112},{24,120},{32,0},{40,8},{48,16},{56,24},{64... | collective-permute-start | bytes 589832 | tf_op jit(solution)/shard_map/ppermute | solution.py:43
  167.5 6.9 %collective-permute-start.58 = (bf16[6,128,128]{2,1,0:T(8,128)(2,1)S(1)}, bf16[6,128,128]{2,1,0:T(8,128)(2,1)S(1)}, u32[]{:S(2)}, u32[]{:S(2)}) collective-permute-start(bf16[6,128,128]{2,1,0:T(8,128)(2,1)S(1)} %add_convert_fusion.12), channel_id=1, source_target_pairs={{0,32},{8,40},{16,48},{24,56},{32,64},{40,72},{48,80},{56,88},{64,... | collective-permute-start | bytes 589832 | tf_op jit(solution)/shard_map/ppermute | solution.py:43
  (25 other events, 70.8 us)
Sparse Core Ops, SparseCore 0:
  111.7 47.9 reduce-scatter.4

commit v5 on v3

--- a/solution.py
+++ b/solution.py
@@ -195,17 +195,17 @@
     return pl.ds(pl.multiple_of(index * BLK, BLK), BLK)
 
 
-def in_groups(groups, run):
-    def twelve(i, unused):
-        run(i * 12, 12)
-        return unused
-
-    def four(i, unused):
-        run(i * 4, 4)
-        return unused
-
-    lax.fori_loop(0, groups // 3, twelve, 0)
-    lax.fori_loop(groups // 3 * 3, groups, four, 0)
+def in_groups(groups, run, sizes=(3, 1)):
+    done = 0
+    for size in sizes:
+        steps = (groups - done) // size
+
+        def step(i, unused, size=size, done=done):
+            run((done + i * size) * 4, size * 4)
+            return unused
+
+        lax.fori_loop(0, steps, step, 0)
+        done = done + steps * size
 
 
 def block_products(table, first, take, give, left, tiles, out, contract, offset=0):
@@ -300,7 +300,7 @@
                     preferred_element_type=jnp.float32,
                 ).astype(jnp.bfloat16)
 
-        in_groups(table[6, first], run)
+        in_groups(table[6, first], run, (6, 3, 1))
         for i, (out, to, start, size) in enumerate(term_parts(room)):
             copies.append(
                 pltpu.make_async_copy(

time: 185 us -> 199 us (1.076)
  the two profiles are of different devices: /device:TPU:0 before, /device:TPU:64 now
where the time goes in v5:
time: 199 us; the launch traced here: 197 us
  waiting for transfers between devices  69.1 us (35%)
  starting transfers between devices  59.3 us (30%)
  Pallas kernels  40.5 us (20%)
  between operations  17.4 us (9%)
  local copies, waits for them, and re-layouts  7.91 us (4%)
  other arithmetic  3.06 us (2%)
    ppermute x32, waiting for transfers between devices, along(): return lambda array, step: lax.ppermute(array, axis, shift(step))  64.8 us
    ppermute x32, starting transfers between devices, along(): return lambda array, step: lax.ppermute(array, axis, shift(step))  53.6 us
    pallas_call x1, Pallas kernels, layer(): call(main, [jax.ShapeDtypeStruct((tokens, width), jnp.bfloat16)] + parts...  33 us
    unnamed x76, local copies, waits for them, and re-layouts  7.71 us
    ppermute x3, starting transfers between devices, moved(): return lax.ppermute(flag, 'tensor', pairs)  5.66 us
    ppermute x3, waiting for transfers between devices, moved(): return lax.ppermute(flag, 'tensor', pairs)  4.21 us
  transfers between devices with their start and end apart: 36, of which 21 were waited for; matrix products, arithmetic and copies ran while one was open for 1% of the time, Pallas kernels for 3%

profile of v5, /device:TPU:64, one launch (start us, length us, event | category | flops | bytes accessed | tf_op | source)
XLA Modules:
  0.0 197.2 jit_solution(17097204057686378110)
XLA Ops:
  7.3 1.1 bitcast_multiply_fusion.refs_8_
  8.4 3.1 %collective-permute-start.27 = (bf16[12,128,128]{2,1,0:T(8,128)(2,1)S(1)}, bf16[12,128,128]{2,1,0:T(8,128)(2,1)S(1)}, u32[]{:S(2)}, u32[]{:S(2)}) collective-permute-start(bf16[12,128,128]{2,1,0:T(8,128)(2,1)S(1)} %bitcast_multiply_fusion.refs_8_), channel_id=1, source_target_pairs={{0,96},{8,104},{16,112},{24,120},{32,0},{40,8},{48,16},{56,24},{64... | collective-permute-start | bytes 1179656 | tf_op jit(solution)/shard_map/ppermute | solution.py:43
  11.5 1.1 bitcast_multiply_fusion.1.refs_3_
  12.6 2.8 %collective-permute-start.25 = (bf16[12,128,128]{2,1,0:T(8,128)(2,1)S(1)}, bf16[12,128,128]{2,1,0:T(8,128)(2,1)S(1)}, u32[]{:S(2)}, u32[]{:S(2)}) collective-permute-start(bf16[12,128,128]{2,1,0:T(8,128)(2,1)S(1)} %bitcast_multiply_fusion.1.refs_3_), channel_id=1, source_target_pairs={{0,24},{8,0},{16,8},{24,16},{32,56},{40,32},{48,40},{56,48},{64,88... | collective-permute-start | bytes 1179656 | tf_op jit(solution)/shard_map/ppermute | solution.py:43
  15.5 3.1 %copy-done = bf16[256,14336]{1,0:T(8,128)(2,1)S(1)} copy-done((bf16[256,14336]{1,0:T(8,128)(2,1)S(1)}, bf16[256,14336]{1,0:T(8,128)(2,1)}, u32[]{:S(2)}) %copy-start) | copy-done | bytes 7340056
  18.6 3.1 %copy-done.1 = bf16[256,14336]{1,0:T(8,128)(2,1)S(1)} copy-done((bf16[256,14336]{1,0:T(8,128)(2,1)S(1)}, bf16[256,14336]{1,0:T(8,128)(2,1)}, u32[]{:S(2)}) %copy-start.1) | copy-done | bytes 7340056
  21.7 3.0 %table.3 = (s32[8,192]{1,0:T(8,128)S(1)}, s32[1]{0:T(128)}) custom-call(s32[4]{0:T(128)S(1)} %pad_add_fusion.refs_0_.place, s32[16]{0:T(128)S(1)} %bitcast.21, s32[192]{0:T(256)S(1)} %bitcast.31, s32[192]{0:T(256)S(1)} %bitcast.33, s32[16]{0:T(128)S(1)} %bitcast.26, s32[192]{0:T(256)S(1)} %bitcast.35, s32[192]{0:T(256)S(1)} %bitcast.37, ...), custom_call_target="tpu_custom_call" | custom-call | bytes 9000000 | tf_op jit(solution)/shard_map/table/pallas_call | solution.py:189
  24.8 2.1 %collective-permute-done.24.refs_4_ = bf16[12,128,128]{2,1,0:T(8,128)(2,1)S(1)} collective-permute-done((bf16[12,128,128]{2,1,0:T(8,128)(2,1)S(1)}, bf16[12,128,128]{2,1,0:T(8,128)(2,1)S(1)}, u32[]{:S(2)}, u32[]{:S(2)}) %collective-permute-start.24) | collective-permute-done | bytes 393248 | tf_op jit(solution)/shard_map/ppermute | solution.py:43
  27.0 3.0 %collective-permute-start.31 = (bf16[6,128,128]{2,1,0:T(8,128)(2,1)S(1)}, bf16[6,128,128]{2,1,0:T(8,128)(2,1)S(1)}, u32[]{:S(2)}, u32[]{:S(2)}) collective-permute-start(bf16[6,128,128]{2,1,0:T(8,128)(2,1)S(1)} %slice.87), channel_id=1, source_target_pairs={{0,96},{8,104},{16,112},{24,120},{32,0},{40,8},{48,16},{56,24},{64... | collective-permute-start | bytes 589832 | tf_op jit(solution)/shard_map/ppermute | solution.py:43
  30.0 1.4 collective-permute-start.29
  32.0 1.2 collective-permute-done.31.refs_11_
  33.2 3.7 %collective-permute-done.30.refs_10_ = bf16[6,128,128]{2,1,0:T(8,128)(2,1)S(1)} collective-permute-done((bf16[6,128,128]{2,1,0:T(8,128)(2,1)S(1)}, bf16[6,128,128]{2,1,0:T(8,128)(2,1)S(1)}, u32[]{:S(2)}, u32[]{:S(2)}) %collective-permute-start.30) | collective-permute-done | bytes 196640 | tf_op jit(solution)/shard_map/ppermute | solution.py:43
  36.9 1.4 collective-permute-done.28.refs_5_
  38.3 1.0 pack.3
  39.4 3.2 %collective-permute-start.33 = (bf16[30,128,128]{2,1,0:T(8,128)(2,1)S(1)}, bf16[30,128,128]{2,1,0:T(8,128)(2,1)S(1)}, u32[]{:S(2)}, u32[]{:S(2)}) collective-permute-start(bf16[30,128,128]{2,1,0:T(8,128)(2,1)S(1)} %get-tuple-element.156.refs_4_), channel_id=1, source_target_pairs={{0,96},{8,104},{16,112},{24,120},{32,0},{40,8},{48,16},{56,24},{64... | collective-permute-start | bytes 2949128 | tf_op jit(solution)/shard_map/ppermute | solution.py:43
  42.7 2.0 %collective-permute-start.34 = (bf16[30,128,128]{2,1,0:T(8,128)(2,1)S(1)}, bf16[30,128,128]{2,1,0:T(8,128)(2,1)S(1)}, u32[]{:S(2)}, u32[]{:S(2)}) collective-permute-start(bf16[30,128,128]{2,1,0:T(8,128)(2,1)S(1)} %get-tuple-element.157.refs_9_), channel_id=1, source_target_pairs={{0,8},{8,16},{16,24},{24,0},{32,40},{40,48},{48,56},{56,32},{64,72... | collective-permute-start | bytes 2949128 | tf_op jit(solution)/shard_map/ppermute | solution.py:43
  44.7 1.2 collective-permute-done.36
  47.2 2.8 %collective-permute-start.37 = (s32[1]{0:T(128)}, s32[1]{0:T(128)}, u32[]{:S(2)}, u32[]{:S(2)}) collective-permute-start(s32[1]{0:T(128)} %max.9), channel_id=1, source_target_pairs={{0,2},{1,3},{2,4},{3,5},{4,6},{5,7},{6,0},{7,1},{8,10},{9,11},{10,... | collective-permute-start | bytes 20 | tf_op jit(solution)/shard_map/ppermute | solution.py:55
  51.4 2.9 %collective-permute-start.38 = (s32[1]{0:T(128)}, s32[1]{0:T(128)}, u32[]{:S(2)}, u32[]{:S(2)}) collective-permute-start(s32[1]{0:T(128)} %max.10), channel_id=1, source_target_pairs={{0,4},{1,5},{2,6},{3,7},{4,0},{5,1},{6,2},{7,3},{8,12},{9,13},{10,... | collective-permute-start | bytes 20 | tf_op jit(solution)/shard_map/ppermute | solution.py:55
  54.2 2.2 %collective-permute-done.38 = s32[1]{0:T(128)} collective-permute-done((s32[1]{0:T(128)}, s32[1]{0:T(128)}, u32[]{:S(2)}, u32[]{:S(2)}) %collective-permute-start.38) | collective-permute-done | bytes 36 | tf_op jit(solution)/shard_map/ppermute | solution.py:55
  57.1 3.3 %collective-permute-done.33.refs_8_ = bf16[30,128,128]{2,1,0:T(8,128)(2,1)S(1)} collective-permute-done((bf16[30,128,128]{2,1,0:T(8,128)(2,1)S(1)}, bf16[30,128,128]{2,1,0:T(8,128)(2,1)S(1)}, u32[]{:S(2)}, u32[]{:S(2)}) %collective-permute-start.33) | collective-permute-done | bytes 983072 | tf_op jit(solution)/shard_map/ppermute | solution.py:43
  60.3 3.4 %collective-permute-done.32.refs_5_ = bf16[30,128,128]{2,1,0:T(8,128)(2,1)S(1)} collective-permute-done((bf16[30,128,128]{2,1,0:T(8,128)(2,1)S(1)}, bf16[30,128,128]{2,1,0:T(8,128)(2,1)S(1)}, u32[]{:S(2)}, u32[]{:S(2)}) %collective-permute-start.32) | collective-permute-done | bytes 983072 | tf_op jit(solution)/shard_map/ppermute | solution.py:43
  65.0 1.6 collective-permute-start.41
  66.7 2.9 %collective-permute-start.40 = (bf16[15,128,128]{2,1,0:T(8,128)(2,1)S(1)}, bf16[15,128,128]{2,1,0:T(8,128)(2,1)S(1)}, u32[]{:S(2)}, u32[]{:S(2)}) collective-permute-start(bf16[15,128,128]{2,1,0:T(8,128)(2,1)S(1)} %slice.89), channel_id=1, source_target_pairs={{0,96},{8,104},{16,112},{24,120},{32,0},{40,8},{48,16},{56,24},{64... | collective-permute-start | bytes 1474568 | tf_op jit(solution)/shard_map/ppermute | solution.py:43
  69.6 3.9 %collective-permute-done.42.refs_12_ = bf16[15,128,128]{2,1,0:T(8,128)(2,1)S(1)} collective-permute-done((bf16[15,128,128]{2,1,0:T(8,128)(2,1)S(1)}, bf16[15,128,128]{2,1,0:T(8,128)(2,1)S(1)}, u32[]{:S(2)}, u32[]{:S(2)}) %collective-permute-start.42) | collective-permute-done | bytes 491552 | tf_op jit(solution)/shard_map/ppermute | solution.py:43
  73.5 1.6 collective-permute-done.41.refs_11_
  75.1 0.8 collective-permute-done.40.refs_7_
  75.9 3.7 %collective-permute-done.39.refs_6_ = bf16[15,128,128]{2,1,0:T(8,128)(2,1)S(1)} collective-permute-done((bf16[15,128,128]{2,1,0:T(8,128)(2,1)S(1)}, bf16[15,128,128]{2,1,0:T(8,128)(2,1)S(1)}, u32[]{:S(2)}, u32[]{:S(2)}) %collective-permute-start.39) | collective-permute-done | bytes 491552 | tf_op jit(solution)/shard_map/ppermute | solution.py:43
  80.4 33.0 %main.3 = (bf16[256,14336]{1,0:T(8,128)(2,1)}, bf16[30,128,128]{2,1,0:T(8,128)(2,1)}, bf16[30,128,128]{2,1,0:T(8,128)(2,1)}, bf16[30,128,128]{2,1,0:T(8,128)(2,1...) custom-call(s32[4]{0:T(128)S(1)} %pad_add_fusion.refs_0_.place, ...), custom_call_target="tpu_custom_call" | custom-call | bytes 120000000 | tf_op jit(solution)/shard_map/main/pallas_call | solution.py:384
  113.5 0.9 collective-permute-start.43
  114.4 1.2 collective-permute-start.44
  115.6 1.5 collective-permute-start.47
  117.6 15.7 %collective-permute-done.43.refs_4_ = bf16[30,128,128]{2,1,0:T(8,128)(2,1)S(1)} collective-permute-done((bf16[30,128,128]{2,1,0:T(8,128)(2,1)}, bf16[30,128,128]{2,1,0:T(8,128)(2,1)S(1)}, u32[]{:S(2)}, u32[]{:S(2)}) %collective-permute-start.43) | collective-permute-done | bytes 983072 | tf_op jit(solution)/shard_map/ppermute | solution.py:43
  133.4 2.3 %collective-permute-start.45 = (bf16[15,128,128]{2,1,0:T(8,128)(2,1)S(1)}, bf16[15,128,128]{2,1,0:T(8,128)(2,1)S(1)}, u32[]{:S(2)}, u32[]{:S(2)}) collective-permute-start(bf16[15,128,128]{2,1,0:T(8,128)(2,1)S(1)} %add_convert_fusion.11), channel_id=1, source_target_pairs={{0,96},{8,104},{16,112},{24,120},{32,0},{40,8},{48,16},{56,24},{64... | collective-permute-start | bytes 1474568 | tf_op jit(solution)/shard_map/ppermute | solution.py:43
  136.1 2.0 collective-permute-start.49
  138.4 3.9 %collective-permute-done.45.refs_6_ = bf16[15,128,128]{2,1,0:T(8,128)(2,1)S(1)} collective-permute-done((bf16[15,128,128]{2,1,0:T(8,128)(2,1)S(1)}, bf16[15,128,128]{2,1,0:T(8,128)(2,1)S(1)}, u32[]{:S(2)}, u32[]{:S(2)}) %collective-permute-start.45) | collective-permute-done | bytes 491552 | tf_op jit(solution)/shard_map/ppermute | solution.py:43
  142.3 3.7 %collective-permute-done.46.refs_7_ = bf16[15,128,128]{2,1,0:T(8,128)(2,1)S(1)} collective-permute-done((bf16[15,128,128]{2,1,0:T(8,128)(2,1)S(1)}, bf16[15,128,128]{2,1,0:T(8,128)(2,1)S(1)}, u32[]{:S(2)}, u32[]{:S(2)}) %collective-permute-start.46) | collective-permute-done | bytes 491552 | tf_op jit(solution)/shard_map/ppermute | solution.py:43
  146.0 2.7 %collective-permute-done.49.refs_11_ = bf16[15,128,128]{2,1,0:T(8,128)(2,1)S(1)} collective-permute-done((bf16[15,128,128]{2,1,0:T(8,128)(2,1)S(1)}, bf16[15,128,128]{2,1,0:T(8,128)(2,1)S(1)}, u32[]{:S(2)}, u32[]{:S(2)}) %collective-permute-start.49) | collective-permute-done | bytes 491552 | tf_op jit(solution)/shard_map/ppermute | solution.py:43
  148.6 3.5 %collective-permute-done.50.refs_12_ = bf16[15,128,128]{2,1,0:T(8,128)(2,1)S(1)} collective-permute-done((bf16[15,128,128]{2,1,0:T(8,128)(2,1)S(1)}, bf16[15,128,128]{2,1,0:T(8,128)(2,1)S(1)}, u32[]{:S(2)}, u32[]{:S(2)}) %collective-permute-start.50) | collective-permute-done | bytes 491552 | tf_op jit(solution)/shard_map/ppermute | solution.py:43
  152.1 1.7 unpack.3
  154.0 2.0 %collective-permute-start.52 = (bf16[12,128,128]{2,1,0:T(8,128)(2,1)S(1)}, bf16[12,128,128]{2,1,0:T(8,128)(2,1)S(1)}, u32[]{:S(2)}, u32[]{:S(2)}) collective-permute-start(bf16[12,128,128]{2,1,0:T(8,128)(2,1)S(1)} %get-tuple-element.177), channel_id=1, source_target_pairs={{0,8},{8,16},{16,24},{24,0},{32,40},{40,48},{48,56},{56,32},{64,72... | collective-permute-start | bytes 1179656 | tf_op jit(solution)/shard_map/ppermute | solution.py:43
  156.0 2.3 %collective-permute-start.55 = (bf16[12,128,128]{2,1,0:T(8,128)(2,1)S(1)}, bf16[12,128,128]{2,1,0:T(8,128)(2,1)S(1)}, u32[]{:S(2)}, u32[]{:S(2)}) collective-permute-start(bf16[12,128,128]{2,1,0:T(8,128)(2,1)S(1)} %get-tuple-element.181), channel_id=1, source_target_pairs={{0,96},{8,104},{16,112},{24,120},{32,0},{40,8},{48,16},{56,24},{64... | collective-permute-start | bytes 1179656 | tf_op jit(solution)/shard_map/ppermute | solution.py:43
  158.3 3.5 %collective-permute-done.51.refs_1_ = bf16[12,128,128]{2,1,0:T(8,128)(2,1)S(1)} collective-permute-done((bf16[12,128,128]{2,1,0:T(8,128)(2,1)S(1)}, bf16[12,128,128]{2,1,0:T(8,128)(2,1)S(1)}, u32[]{:S(2)}, u32[]{:S(2)}) %collective-permute-start.51) | collective-permute-done | bytes 393248 | tf_op jit(solution)/shard_map/ppermute | solution.py:43
  161.8 1.3 collective-permute-start.53
  164.1 3.3 %collective-permute-start.57 = (bf16[6,128,128]{2,1,0:T(8,128)(2,1)S(1)}, bf16[6,128,128]{2,1,0:T(8,128)(2,1)S(1)}, u32[]{:S(2)}, u32[]{:S(2)}) collective-permute-start(bf16[6,128,128]{2,1,0:T(8,128)(2,1)S(1)} %add_convert_fusion.13), channel_id=1, source_target_pairs={{0,96},{8,104},{16,112},{24,120},{32,0},{40,8},{48,16},{56,24},{64... | collective-permute-start | bytes 589832 | tf_op jit(solution)/shard_map/ppermute | solution.py:43
  167.4 14.0 %collective-permute-start.58 = (bf16[6,128,128]{2,1,0:T(8,128)(2,1)S(1)}, bf16[6,128,128]{2,1,0:T(8,128)(2,1)S(1)}, u32[]{:S(2)}, u32[]{:S(2)}) collective-permute-start(bf16[6,128,128]{2,1,0:T(8,128)(2,1)S(1)} %add_convert_fusion.12), channel_id=1, source_target_pairs={{0,32},{8,40},{16,48},{24,56},{32,64},{40,72},{48,80},{56,88},{64,... | collective-permute-start | bytes 589832 | tf_op jit(solution)/shard_map/ppermute | solution.py:43
  181.5 6.8 %collective-permute-done.58.refs_9_ = bf16[6,128,128]{2,1,0:T(8,128)(2,1)S(1)} collective-permute-done((bf16[6,128,128]{2,1,0:T(8,128)(2,1)S(1)}, bf16[6,128,128]{2,1,0:T(8,128)(2,1)S(1)}, u32[]{:S(2)}, u32[]{:S(2)}) %collective-permute-start.58) | collective-permute-done | bytes 196640 | tf_op jit(solution)/shard_map/ppermute | solution.py:43
  188.4 1.7 finish.3
  (128 shorter events, 6.3 us)
Async XLA Ops:
  7.2 8.3 %copy-start.45 = (s32[1,16]{1,0:T(1,128)S(1)}, s32[1,16]{1,0:T(1,128)}, u32[]{:S(2)}) copy-start(s32[1,16]{1,0:T(1,128)} %param.25) | copy-start | bytes 196
  7.2 8.3 %copy-start.44 = (s32[1,16]{1,0:T(1,128)S(1)}, s32[1,16]{1,0:T(1,128)}, u32[]{:S(2)}) copy-start(s32[1,16]{1,0:T(1,128)} %param.24) | copy-start | bytes 196
  7.2 182.9 %reduce-scatter.5.cloned.1.call-start = ((), (), s32[]{:S(2)}) async-start(), calls=%async_computation.3 | async-start | bytes 8257536 | tf_op jit(solution)/shard_map/reduce_scatter | solution.py:394
  8.4 16.4 %collective-permute-start.27 = (bf16[12,128,128]{2,1,0:T(8,128)(2,1)S(1)}, bf16[12,128,128]{2,1,0:T(8,128)(2,1)S(1)}, u32[]{:S(2)}, u32[]{:S(2)}) collective-permute-start(bf16[12,128,128]{2,1,0:T(8,128)(2,1)S(1)} %bitcast_multiply_fusion.refs_8_), channel_id=1, source_target_pairs={{0,96},{8,104},{16,112},{24,120},{32,0},{40,8},{48,16},{56,24},{64... | collective-permute-start | bytes 1179656 | tf_op jit(solution)/shard_map/ppermute | solution.py:43
  11.5 13.3 %collective-permute-start.26 = (bf16[12,128,128]{2,1,0:T(8,128)(2,1)S(1)}, bf16[12,128,128]{2,1,0:T(8,128)(2,1)S(1)}, u32[]{:S(2)}, u32[]{:S(2)}) collective-permute-start(bf16[12,128,128]{2,1,0:T(8,128)(2,1)S(1)} %bitcast_multiply_fusion.refs_8_), channel_id=1, source_target_pairs={{0,32},{8,40},{16,48},{24,56},{32,64},{40,72},{48,80},{56,88},{64,... | collective-permute-start | bytes 1179656 | tf_op jit(solution)/shard_map/ppermute | solution.py:43
  12.6 12.2 %collective-permute-start.25 = (bf16[12,128,128]{2,1,0:T(8,128)(2,1)S(1)}, bf16[12,128,128]{2,1,0:T(8,128)(2,1)S(1)}, u32[]{:S(2)}, u32[]{:S(2)}) collective-permute-start(bf16[12,128,128]{2,1,0:T(8,128)(2,1)S(1)} %bitcast_multiply_fusion.1.refs_3_), channel_id=1, source_target_pairs={{0,24},{8,0},{16,8},{24,16},{32,56},{40,32},{48,40},{56,48},{64,88... | collective-permute-start | bytes 1179656 | tf_op jit(solution)/shard_map/ppermute | solution.py:43
  15.4 11.5 %collective-permute-start.24 = (bf16[12,128,128]{2,1,0:T(8,128)(2,1)S(1)}, bf16[12,128,128]{2,1,0:T(8,128)(2,1)S(1)}, u32[]{:S(2)}, u32[]{:S(2)}) collective-permute-start(bf16[12,128,128]{2,1,0:T(8,128)(2,1)S(1)} %bitcast_multiply_fusion.1.refs_3_), channel_id=1, source_target_pairs={{0,8},{8,16},{16,24},{24,0},{32,40},{40,48},{48,56},{56,32},{64,72... | collective-permute-start | bytes 1179656 | tf_op jit(solution)/shard_map/ppermute | solution.py:43
  24.8 14.6 %copy-start.16 = (bf16[12,128,128]{2,1,0:T(8,128)(2,1)}, bf16[12,128,128]{2,1,0:T(8,128)(2,1)S(1)}, u32[]{:S(2)}) copy-start(bf16[12,128,128]{2,1,0:T(8,128)(2,1)S(1)} %collective-permute-done.25.refs_7_) | copy-start | bytes 1179652
  26.9 12.5 %copy-start.18 = (bf16[12,128,128]{2,1,0:T(8,128)(2,1)}, bf16[12,128,128]{2,1,0:T(8,128)(2,1)S(1)}, u32[]{:S(2)}) copy-start(bf16[12,128,128]{2,1,0:T(8,128)(2,1)S(1)} %collective-permute-done.24.refs_4_) | copy-start | bytes 1179652
  27.0 53.5 %copy-start.2 = (bf16[256,14336]{1,0:T(8,128)(2,1)S(1)}, bf16[256,14336]{1,0:T(8,128)(2,1)}, u32[]{:S(2)}) copy-start(bf16[256,14336]{1,0:T(8,128)(2,1)} %refs_3_.1) | copy-start | bytes 22020100
  27.0 6.2 %collective-permute-start.31 = (bf16[6,128,128]{2,1,0:T(8,128)(2,1)S(1)}, bf16[6,128,128]{2,1,0:T(8,128)(2,1)S(1)}, u32[]{:S(2)}, u32[]{:S(2)}) collective-permute-start(bf16[6,128,128]{2,1,0:T(8,128)(2,1)S(1)} %slice.87), channel_id=1, source_target_pairs={{0,96},{8,104},{16,112},{24,120},{32,0},{40,8},{48,16},{56,24},{64... | collective-permute-start | bytes 589832 | tf_op jit(solution)/shard_map/ppermute | solution.py:43
  30.0 6.9 %collective-permute-start.30 = (bf16[6,128,128]{2,1,0:T(8,128)(2,1)S(1)}, bf16[6,128,128]{2,1,0:T(8,128)(2,1)S(1)}, u32[]{:S(2)}, u32[]{:S(2)}) collective-permute-start(bf16[6,128,128]{2,1,0:T(8,128)(2,1)S(1)} %slice.86), channel_id=1, source_target_pairs={{0,32},{8,40},{16,48},{24,56},{32,64},{40,72},{48,80},{56,88},{64,... | collective-permute-start | bytes 589832 | tf_op jit(solution)/shard_map/ppermute | solution.py:43
  30.0 6.9 %collective-permute-start.29 = (bf16[6,128,128]{2,1,0:T(8,128)(2,1)S(1)}, bf16[6,128,128]{2,1,0:T(8,128)(2,1)S(1)}, u32[]{:S(2)}, u32[]{:S(2)}) collective-permute-start(bf16[6,128,128]{2,1,0:T(8,128)(2,1)S(1)} %slice.85), channel_id=1, source_target_pairs={{0,24},{8,0},{16,8},{24,16},{32,56},{40,32},{48,40},{56,48},{64,88... | collective-permute-start | bytes 589832 | tf_op jit(solution)/shard_map/ppermute | solution.py:43
  31.5 6.9 %collective-permute-start.28 = (bf16[6,128,128]{2,1,0:T(8,128)(2,1)S(1)}, bf16[6,128,128]{2,1,0:T(8,128)(2,1)S(1)}, u32[]{:S(2)}, u32[]{:S(2)}) collective-permute-start(bf16[6,128,128]{2,1,0:T(8,128)(2,1)S(1)} %slice.84), channel_id=1, source_target_pairs={{0,8},{8,16},{16,24},{24,0},{32,40},{40,48},{48,56},{56,32},{64,72... | collective-permute-start | bytes 589832 | tf_op jit(solution)/shard_map/ppermute | solution.py:43
  39.4 24.6 %copy-start.7 = (bf16[30,128,128]{2,1,0:T(8,128)(2,1)}, bf16[30,128,128]{2,1,0:T(8,128)(2,1)S(1)}, u32[]{:S(2)}) copy-start(bf16[30,128,128]{2,1,0:T(8,128)(2,1)S(1)} %get-tuple-element.156.refs_4_) | copy-start | bytes 2949124
  39.4 24.6 %copy-start.8 = (bf16[30,128,128]{2,1,0:T(8,128)(2,1)}, bf16[30,128,128]{2,1,0:T(8,128)(2,1)S(1)}, u32[]{:S(2)}) copy-start(bf16[30,128,128]{2,1,0:T(8,128)(2,1)S(1)} %get-tuple-element.157.refs_9_) | copy-start | bytes 2949124
  39.4 20.9 %collective-permute-start.33 = (bf16[30,128,128]{2,1,0:T(8,128)(2,1)S(1)}, bf16[30,128,128]{2,1,0:T(8,128)(2,1)S(1)}, u32[]{:S(2)}, u32[]{:S(2)}) collective-permute-start(bf16[30,128,128]{2,1,0:T(8,128)(2,1)S(1)} %get-tuple-element.156.refs_4_), channel_id=1, source_target_pairs={{0,96},{8,104},{16,112},{24,120},{32,0},{40,8},{48,16},{56,24},{64... | collective-permute-start | bytes 2949128 | tf_op jit(solution)/shard_map/ppermute | solution.py:43
  42.7 21.1 %collective-permute-start.32 = (bf16[30,128,128]{2,1,0:T(8,128)(2,1)S(1)}, bf16[30,128,128]{2,1,0:T(8,128)(2,1)S(1)}, u32[]{:S(2)}, u32[]{:S(2)}) collective-permute-start(bf16[30,128,128]{2,1,0:T(8,128)(2,1)S(1)} %get-tuple-element.156.refs_4_), channel_id=1, source_target_pairs={{0,32},{8,40},{16,48},{24,56},{32,64},{40,72},{48,80},{56,88},{64,... | collective-permute-start | bytes 2949128 | tf_op jit(solution)/shard_map/ppermute | solution.py:43
  42.7 21.1 %collective-permute-start.35 = (bf16[30,128,128]{2,1,0:T(8,128)(2,1)S(1)}, bf16[30,128,128]{2,1,0:T(8,128)(2,1)S(1)}, u32[]{:S(2)}, u32[]{:S(2)}) collective-permute-start(bf16[30,128,128]{2,1,0:T(8,128)(2,1)S(1)} %get-tuple-element.157.refs_9_), channel_id=1, source_target_pairs={{0,24},{8,0},{16,8},{24,16},{32,56},{40,32},{48,40},{56,48},{64,88... | collective-permute-start | bytes 2949128 | tf_op jit(solution)/shard_map/ppermute | solution.py:43
  42.7 21.2 %collective-permute-start.34 = (bf16[30,128,128]{2,1,0:T(8,128)(2,1)S(1)}, bf16[30,128,128]{2,1,0:T(8,128)(2,1)S(1)}, u32[]{:S(2)}, u32[]{:S(2)}) collective-permute-start(bf16[30,128,128]{2,1,0:T(8,128)(2,1)S(1)} %get-tuple-element.157.refs_9_), channel_id=1, source_target_pairs={{0,8},{8,16},{16,24},{24,0},{32,40},{40,48},{48,56},{56,32},{64,72... | collective-permute-start | bytes 2949128 | tf_op jit(solution)/shard_map/ppermute | solution.py:43
  44.7 1.2 collective-permute-start.36
  47.2 3.6 %collective-permute-start.37 = (s32[1]{0:T(128)}, s32[1]{0:T(128)}, u32[]{:S(2)}, u32[]{:S(2)}) collective-permute-start(s32[1]{0:T(128)} %max.9), channel_id=1, source_target_pairs={{0,2},{1,3},{2,4},{3,5},{4,6},{5,7},{6,0},{7,1},{8,10},{9,11},{10,... | collective-permute-start | bytes 20 | tf_op jit(solution)/shard_map/ppermute | solution.py:55
  51.4 5.1 %collective-permute-start.38 = (s32[1]{0:T(128)}, s32[1]{0:T(128)}, u32[]{:S(2)}, u32[]{:S(2)}) collective-permute-start(s32[1]{0:T(128)} %max.10), channel_id=1, source_target_pairs={{0,4},{1,5},{2,6},{3,7},{4,0},{5,1},{6,2},{7,3},{8,12},{9,13},{10,... | collective-permute-start | bytes 20 | tf_op jit(solution)/shard_map/ppermute | solution.py:55
  63.7 15.9 %copy-start.22 = (bf16[30,128,128]{2,1,0:T(8,128)(2,1)}, bf16[30,128,128]{2,1,0:T(8,128)(2,1)S(1)}, u32[]{:S(2)}) copy-start(bf16[30,128,128]{2,1,0:T(8,128)(2,1)S(1)} %collective-permute-done.35.refs_13_) | copy-start | bytes 2949124
  63.8 15.8 %copy-start.23 = (bf16[30,128,128]{2,1,0:T(8,128)(2,1)}, bf16[30,128,128]{2,1,0:T(8,128)(2,1)S(1)}, u32[]{:S(2)}) copy-start(bf16[30,128,128]{2,1,0:T(8,128)(2,1)S(1)} %collective-permute-done.34.refs_10_) | copy-start | bytes 2949124
  64.6 8.8 %collective-permute-start.42 = (bf16[15,128,128]{2,1,0:T(8,128)(2,1)S(1)}, bf16[15,128,128]{2,1,0:T(8,128)(2,1)S(1)}, u32[]{:S(2)}, u32[]{:S(2)}) collective-permute-start(bf16[15,128,128]{2,1,0:T(8,128)(2,1)S(1)} %slice.91), channel_id=1, source_target_pairs={{0,24},{8,0},{16,8},{24,16},{32,56},{40,32},{48,40},{56,48},{64,88... | collective-permute-start | bytes 1474568 | tf_op jit(solution)/shard_map/ppermute | solution.py:43
  65.0 10.0 %collective-permute-start.41 = (bf16[15,128,128]{2,1,0:T(8,128)(2,1)S(1)}, bf16[15,128,128]{2,1,0:T(8,128)(2,1)S(1)}, u32[]{:S(2)}, u32[]{:S(2)}) collective-permute-start(bf16[15,128,128]{2,1,0:T(8,128)(2,1)S(1)} %slice.90), channel_id=1, source_target_pairs={{0,8},{8,16},{16,24},{24,0},{32,40},{40,48},{48,56},{56,32},{64,72... | collective-permute-start | bytes 1474568 | tf_op jit(solution)/shard_map/ppermute | solution.py:43
  66.7 9.2 %collective-permute-start.40 = (bf16[15,128,128]{2,1,0:T(8,128)(2,1)S(1)}, bf16[15,128,128]{2,1,0:T(8,128)(2,1)S(1)}, u32[]{:S(2)}, u32[]{:S(2)}) collective-permute-start(bf16[15,128,128]{2,1,0:T(8,128)(2,1)S(1)} %slice.89), channel_id=1, source_target_pairs={{0,96},{8,104},{16,112},{24,120},{32,0},{40,8},{48,16},{56,24},{64... | collective-permute-start | bytes 1474568 | tf_op jit(solution)/shard_map/ppermute | solution.py:43
  69.6 10.0 %collective-permute-start.39 = (bf16[15,128,128]{2,1,0:T(8,128)(2,1)S(1)}, bf16[15,128,128]{2,1,0:T(8,128)(2,1)S(1)}, u32[]{:S(2)}, u32[]{:S(2)}) collective-permute-start(bf16[15,128,128]{2,1,0:T(8,128)(2,1)S(1)} %slice.88), channel_id=1, source_target_pairs={{0,32},{8,40},{16,48},{24,56},{32,64},{40,72},{48,80},{56,88},{64,... | collective-permute-start | bytes 1474568 | tf_op jit(solution)/shard_map/ppermute | solution.py:43
  113.5 19.8 %collective-permute-start.43 = (bf16[30,128,128]{2,1,0:T(8,128)(2,1)}, bf16[30,128,128]{2,1,0:T(8,128)(2,1)S(1)}, u32[]{:S(2)}, u32[]{:S(2)}) collective-permute-start(bf16[30,128,128]{2,1,0:T(8,128)(2,1)} %get-tuple-element.166), channel_id=1, source_target_pairs={{0,96},{8,104},{16,112},{24,120},{32,0},{40,8},{48,16},{56,24},{64... | collective-permute-start | bytes 2949128 | tf_op jit(solution)/shard_map/ppermute | solution.py:43
  114.4 21.3 %collective-permute-start.44 = (bf16[30,128,128]{2,1,0:T(8,128)(2,1)}, bf16[30,128,128]{2,1,0:T(8,128)(2,1)S(1)}, u32[]{:S(2)}, u32[]{:S(2)}) collective-permute-start(bf16[30,128,128]{2,1,0:T(8,128)(2,1)} %get-tuple-element.167), channel_id=1, source_target_pairs={{0,32},{8,40},{16,48},{24,56},{32,64},{40,72},{48,80},{56,88},{64,... | collective-permute-start | bytes 2949128 | tf_op jit(solution)/shard_map/ppermute | solution.py:43
  115.6 20.4 %collective-permute-start.47 = (bf16[30,128,128]{2,1,0:T(8,128)(2,1)}, bf16[30,128,128]{2,1,0:T(8,128)(2,1)S(1)}, u32[]{:S(2)}, u32[]{:S(2)}) collective-permute-start(bf16[30,128,128]{2,1,0:T(8,128)(2,1)} %get-tuple-element.171), channel_id=1, source_target_pairs={{0,24},{8,0},{16,8},{24,16},{32,56},{40,32},{48,40},{56,48},{64,88... | collective-permute-start | bytes 2949128 | tf_op jit(solution)/shard_map/ppermute | solution.py:43
  117.1 21.0 %collective-permute-start.48 = (bf16[30,128,128]{2,1,0:T(8,128)(2,1)}, bf16[30,128,128]{2,1,0:T(8,128)(2,1)S(1)}, u32[]{:S(2)}, u32[]{:S(2)}) collective-permute-start(bf16[30,128,128]{2,1,0:T(8,128)(2,1)} %get-tuple-element.172), channel_id=1, source_target_pairs={{0,8},{8,16},{16,24},{24,0},{32,40},{40,48},{48,56},{56,32},{64,72... | collective-permute-start | bytes 2949128 | tf_op jit(solution)/shard_map/ppermute | solution.py:43
  133.4 8.9 %collective-permute-start.45 = (bf16[15,128,128]{2,1,0:T(8,128)(2,1)S(1)}, bf16[15,128,128]{2,1,0:T(8,128)(2,1)S(1)}, u32[]{:S(2)}, u32[]{:S(2)}) collective-permute-start(bf16[15,128,128]{2,1,0:T(8,128)(2,1)S(1)} %add_convert_fusion.11), channel_id=1, source_target_pairs={{0,96},{8,104},{16,112},{24,120},{32,0},{40,8},{48,16},{56,24},{64... | collective-permute-start | bytes 1474568 | tf_op jit(solution)/shard_map/ppermute | solution.py:43
  135.9 16.3 %copy-start.9 = (bf16[30,128,128]{2,1,0:T(8,128)(2,1)S(1)}, bf16[30,128,128]{2,1,0:T(8,128)(2,1)}, u32[]{:S(2)}) copy-start(bf16[30,128,128]{2,1,0:T(8,128)(2,1)} %get-tuple-element.165.refs_3_) | copy-start | bytes 2949124
  135.9 16.2 %copy-start.10 = (bf16[30,128,128]{2,1,0:T(8,128)(2,1)S(1)}, bf16[30,128,128]{2,1,0:T(8,128)(2,1)}, u32[]{:S(2)}) copy-start(bf16[30,128,128]{2,1,0:T(8,128)(2,1)} %get-tuple-element.170.refs_8_) | copy-start | bytes 2949124
  135.9 10.1 %collective-permute-start.46 = (bf16[15,128,128]{2,1,0:T(8,128)(2,1)S(1)}, bf16[15,128,128]{2,1,0:T(8,128)(2,1)S(1)}, u32[]{:S(2)}, u32[]{:S(2)}) collective-permute-start(bf16[15,128,128]{2,1,0:T(8,128)(2,1)S(1)} %add_convert_fusion.10), channel_id=1, source_target_pairs={{0,32},{8,40},{16,48},{24,56},{32,64},{40,72},{48,80},{56,88},{64,... | collective-permute-start | bytes 1474568 | tf_op jit(solution)/shard_map/ppermute | solution.py:43
  136.1 12.5 %collective-permute-start.49 = (bf16[15,128,128]{2,1,0:T(8,128)(2,1)S(1)}, bf16[15,128,128]{2,1,0:T(8,128)(2,1)S(1)}, u32[]{:S(2)}, u32[]{:S(2)}) collective-permute-start(bf16[15,128,128]{2,1,0:T(8,128)(2,1)S(1)} %add_convert_fusion.9), channel_id=1, source_target_pairs={{0,24},{8,0},{16,8},{24,16},{32,56},{40,32},{48,40},{56,48},{64,88... | collective-permute-start | bytes 1474568 | tf_op jit(solution)/shard_map/ppermute | solution.py:43
  138.2 13.9 %collective-permute-start.50 = (bf16[15,128,128]{2,1,0:T(8,128)(2,1)S(1)}, bf16[15,128,128]{2,1,0:T(8,128)(2,1)S(1)}, u32[]{:S(2)}, u32[]{:S(2)}) collective-permute-start(bf16[15,128,128]{2,1,0:T(8,128)(2,1)S(1)} %add_convert_fusion.8), channel_id=1, source_target_pairs={{0,8},{8,16},{16,24},{24,0},{32,40},{40,48},{48,56},{56,32},{64,72... | collective-permute-start | bytes 1474568 | tf_op jit(solution)/shard_map/ppermute | solution.py:43
  153.9 27.6 %copy-start.54 = (bf16[1,12]{1,0:T(2,128)(2,1)S(1)}, bf16[1,12]{1,0:T(2,128)(2,1)}, u32[]{:S(2)}) copy-start(bf16[1,12]{1,0:T(2,128)(2,1)} %param.19) | copy-start | bytes 76
  153.9 7.8 %collective-permute-start.51 = (bf16[12,128,128]{2,1,0:T(8,128)(2,1)S(1)}, bf16[12,128,128]{2,1,0:T(8,128)(2,1)S(1)}, u32[]{:S(2)}, u32[]{:S(2)}) collective-permute-start(bf16[12,128,128]{2,1,0:T(8,128)(2,1)S(1)} %get-tuple-element.176), channel_id=1, source_target_pairs={{0,24},{8,0},{16,8},{24,16},{32,56},{40,32},{48,40},{56,48},{64,88... | collective-permute-start | bytes 1179656 | tf_op jit(solution)/shard_map/ppermute | solution.py:43
  154.0 9.1 %collective-permute-start.52 = (bf16[12,128,128]{2,1,0:T(8,128)(2,1)S(1)}, bf16[12,128,128]{2,1,0:T(8,128)(2,1)S(1)}, u32[]{:S(2)}, u32[]{:S(2)}) collective-permute-start(bf16[12,128,128]{2,1,0:T(8,128)(2,1)S(1)} %get-tuple-element.177), channel_id=1, source_target_pairs={{0,8},{8,16},{16,24},{24,0},{32,40},{40,48},{48,56},{56,32},{64,72... | collective-permute-start | bytes 1179656 | tf_op jit(solution)/shard_map/ppermute | solution.py:43
  156.0 8.0 %collective-permute-start.55 = (bf16[12,128,128]{2,1,0:T(8,128)(2,1)S(1)}, bf16[12,128,128]{2,1,0:T(8,128)(2,1)S(1)}, u32[]{:S(2)}, u32[]{:S(2)}) collective-permute-start(bf16[12,128,128]{2,1,0:T(8,128)(2,1)S(1)} %get-tuple-element.181), channel_id=1, source_target_pairs={{0,96},{8,104},{16,112},{24,120},{32,0},{40,8},{48,16},{56,24},{64... | collective-permute-start | bytes 1179656 | tf_op jit(solution)/shard_map/ppermute | solution.py:43
  158.3 9.1 %collective-permute-start.56 = (bf16[12,128,128]{2,1,0:T(8,128)(2,1)S(1)}, bf16[12,128,128]{2,1,0:T(8,128)(2,1)S(1)}, u32[]{:S(2)}, u32[]{:S(2)}) collective-permute-start(bf16[12,128,128]{2,1,0:T(8,128)(2,1)S(1)} %get-tuple-element.182), channel_id=1, source_target_pairs={{0,32},{8,40},{16,48},{24,56},{32,64},{40,72},{48,80},{56,88},{64,... | collective-permute-start | bytes 1179656 | tf_op jit(solution)/shard_map/ppermute | solution.py:43
  161.8 19.7 %collective-permute-start.53 = (bf16[6,128,128]{2,1,0:T(8,128)(2,1)S(1)}, bf16[6,128,128]{2,1,0:T(8,128)(2,1)S(1)}, u32[]{:S(2)}, u32[]{:S(2)}) collective-permute-start(bf16[6,128,128]{2,1,0:T(8,128)(2,1)S(1)} %add_convert_fusion.15), channel_id=1, source_target_pairs={{0,24},{8,0},{16,8},{24,16},{32,56},{40,32},{48,40},{56,48},{64,88... | collective-permute-start | bytes 589832 | tf_op jit(solution)/shard_map/ppermute | solution.py:43
  163.2 18.3 %collective-permute-start.54 = (bf16[6,128,128]{2,1,0:T(8,128)(2,1)S(1)}, bf16[6,128,128]{2,1,0:T(8,128)(2,1)S(1)}, u32[]{:S(2)}, u32[]{:S(2)}) collective-permute-start(bf16[6,128,128]{2,1,0:T(8,128)(2,1)S(1)} %add_convert_fusion.14), channel_id=1, source_target_pairs={{0,8},{8,16},{16,24},{24,0},{32,40},{40,48},{48,56},{56,32},{64,72... | collective-permute-start | bytes 589832 | tf_op jit(solution)/shard_map/ppermute | solution.py:43
  164.1 17.4 %collective-permute-start.57 = (bf16[6,128,128]{2,1,0:T(8,128)(2,1)S(1)}, bf16[6,128,128]{2,1,0:T(8,128)(2,1)S(1)}, u32[]{:S(2)}, u32[]{:S(2)}) collective-permute-start(bf16[6,128,128]{2,1,0:T(8,128)(2,1)S(1)} %add_convert_fusion.13), channel_id=1, source_target_pairs={{0,96},{8,104},{16,112},{24,120},{32,0},{40,8},{48,16},{56,24},{64... | collective-permute-start | bytes 589832 | tf_op jit(solution)/shard_map/ppermute | solution.py:43
  167.4 20.9 %collective-permute-start.58 = (bf16[6,128,128]{2,1,0:T(8,128)(2,1)S(1)}, bf16[6,128,128]{2,1,0:T(8,128)(2,1)S(1)}, u32[]{:S(2)}, u32[]{:S(2)}) collective-permute-start(bf16[6,128,128]{2,1,0:T(8,128)(2,1)S(1)} %add_convert_fusion.12), channel_id=1, source_target_pairs={{0,32},{8,40},{16,48},{24,56},{32,64},{40,72},{48,80},{56,88},{64,... | collective-permute-start | bytes 589832 | tf_op jit(solution)/shard_map/ppermute | solution.py:43
  (26 other events, 91.5 us)
Sparse Core Ops, SparseCore 0:
  113.6 42.6 reduce-scatter.4
